TPU v7x, 32 devices: a whole 2x2x4 slice. The times are simulated.
32 devices in a mesh: dp: 16 (over z, y, x), seq: 2 (over core).
Axes of the slice: x: 2, y: 2, z: 4, core: 2. Of those that a mesh axis runs over, the one named last changes fastest.
Arguments:
- inputs: float32 [32, 8192, 768], P('dp', 'seq'), may hold values from -45 to 45
- conv_one: bfloat16 [5, 768, 768], replicated, may hold values from -0.09375 to 0.09375
- conv_two: bfloat16 [3, 768, 384], replicated, may hold values from -0.125 to 0.125
- conv_three: bfloat16 [384, 768], replicated, may hold values from -0.3125 to 0.3125
- gain_one: float32 [768], replicated, may hold values from 0.5 to 1.5
- shift_one: float32 [768], replicated, may hold values from -2 to 2
- gain_two: float32 [768], replicated, may hold values from 0.5 to 1.5
- shift_two: float32 [768], replicated, may hold values from -2 to 2
- gain_three: float32 [384], replicated, may hold values from 0.5 to 1.5
- shift_three: float32 [384], replicated, may hold values from -2 to 2
- cotangent: float32 [32, 4096, 768], P('dp', 'seq'), may hold values from -6 to 6
Outputs:
- outputs: float32 [32, 4096, 768], P('dp', 'seq')
- input_grad: float32 [32, 8192, 768], P('dp', 'seq')
- conv_one_grad: float32 [5, 768, 768], replicated
- conv_two_grad: float32 [3, 768, 384], replicated
- conv_three_grad: float32 [384, 768], replicated
- gain_one_grad: float32 [768], replicated
- shift_one_grad: float32 [768], replicated
- gain_two_grad: float32 [768], replicated
- shift_two_grad: float32 [768], replicated
- gain_three_grad: float32 [384], replicated
- shift_three_grad: float32 [384], replicated
All inputs are finite; a program needn't handle non-finite values.
Results may differ from a plain program's by a relative error of at most 0.0084.
Values may be sent and summed in bfloat16 or wider, within the bound.
A program may use at most 320 MiB of HBM per device.

v0:
```python
import jax
import jax.numpy as jnp
from jax import lax
from jax.sharding import PartitionSpec as P

epsilon = 1e-05


def with_halo(cells, sides, width):
    for axis, dim in sides:
        count = lax.axis_size(axis)
        ends = count - 1
        head = lax.slice_in_dim(cells, 0, width, axis=dim)
        tail = lax.slice_in_dim(cells, cells.shape[dim] - width, cells.shape[dim], axis=dim)
        cells = jnp.concatenate(
            [
                lax.ppermute(tail, axis, [(i, (i + 1) % count) for i in range(ends)]),
                cells,
                lax.ppermute(head, axis, [((i + 1) % count, i) for i in range(ends)]),
            ],
            axis=dim,
        )
    return cells


def batch_norm(values, gain, offset, entries):
    sums, squares = lax.psum(
        (jnp.sum(values, axis=(0, 1)), jnp.sum(values * values, axis=(0, 1))), ("dp", "seq")
    )
    center = sums / entries
    inverse = lax.rsqrt(squares / entries - center * center + epsilon)
    normed = (values - center) * inverse
    return (normed, inverse, normed * gain + offset)


def norm_back(grad_pre, normed, inverse, gain, entries):
    gain_grad, shift_grad = lax.psum(
        (jnp.sum(grad_pre * normed, axis=(0, 1)), jnp.sum(grad_pre, axis=(0, 1))), ("dp", "seq")
    )
    return (
        inverse * gain * (grad_pre - shift_grad / entries - normed * gain_grad / entries),
        gain_grad,
        shift_grad,
    )


def gelu_back(before, incoming):
    unused, pullback = jax.vjp(jax.nn.gelu, before)
    return pullback(incoming)[0]


def conv_forward(padded, weight, dilation, length):
    summed = jnp.einsum(
        "wtc,cd->wtd", padded[:, 0:length], weight[0], preferred_element_type=jnp.float32
    )
    for tap_index in range(1, weight.shape[0]):
        start = tap_index * dilation
        summed = summed + jnp.einsum(
            "wtc,cd->wtd",
            padded[:, start : start + length],
            weight[tap_index],
            preferred_element_type=jnp.float32,
        )
    return summed


def conv_weight_grad(padded, grad_low, dilation, length, taps):
    pieces = []
    for tap_index in range(taps):
        start = tap_index * dilation
        pieces.append(
            jnp.einsum(
                "wtc,wtd->cd",
                padded[:, start : start + length],
                grad_low,
                preferred_element_type=jnp.float32,
            )
        )
    return jnp.stack(pieces)


def conv_input_grad(padded_grad, weight, dilation, length):
    taps = weight.shape[0]
    summed = None
    for tap_index in range(taps):
        start = (taps - 1 - tap_index) * dilation
        term = jnp.einsum(
            "wtd,cd->wtc",
            padded_grad[:, start : start + length],
            weight[tap_index],
            preferred_element_type=jnp.float32,
        )
        summed = term if summed is None else summed + term
    return summed


def on_device(
    inputs,
    conv_one,
    conv_two,
    conv_three,
    gain_one,
    shift_one,
    gain_two,
    shift_two,
    gain_three,
    shift_three,
    cotangent,
):
    windows, length, channels = inputs.shape
    pooled_len = length // 2
    entries = windows * length * lax.axis_size("dp") * lax.axis_size("seq")
    half_entries = entries // 2
    normed_one, inverse_one, before_one = batch_norm(inputs, gain_one, shift_one, entries)
    hidden_one = jax.nn.gelu(before_one).astype(jnp.bfloat16)
    padded_one = with_halo(hidden_one, (("seq", 1),), 2)
    conv_out = conv_forward(padded_one, conv_one, 1, length)
    pairs = conv_out.reshape(windows, pooled_len, 2, channels)
    pooled = 0.5 * (pairs[:, :, 0] + pairs[:, :, 1])
    normed_two, inverse_two, before_two = batch_norm(pooled, gain_two, shift_two, half_entries)
    hidden_two = jax.nn.gelu(before_two).astype(jnp.bfloat16)
    padded_two = with_halo(hidden_two, (("seq", 1),), 5)
    narrow = conv_forward(padded_two, conv_two, 5, pooled_len)
    normed_three, inverse_three, before_three = batch_norm(
        narrow, gain_three, shift_three, half_entries
    )
    hidden_three = jax.nn.gelu(before_three).astype(jnp.bfloat16)
    branch = jnp.einsum("wtc,cd->wtd", hidden_three, conv_three, preferred_element_type=jnp.float32)
    outputs = pooled + branch
    branch_low = cotangent.astype(jnp.bfloat16)
    three_grad = jnp.einsum(
        "wtc,wtd->cd", hidden_three, branch_low, preferred_element_type=jnp.float32
    )
    grad_hidden_three = jnp.einsum(
        "wtd,cd->wtc", branch_low, conv_three, preferred_element_type=jnp.float32
    )
    grad_narrow, gain_three_grad, shift_three_grad = norm_back(
        gelu_back(before_three, grad_hidden_three),
        normed_three,
        inverse_three,
        gain_three,
        half_entries,
    )
    narrow_low = grad_narrow.astype(jnp.bfloat16)
    two_grad = conv_weight_grad(padded_two, narrow_low, 5, pooled_len, conv_two.shape[0])
    padded_back_two = with_halo(narrow_low, (("seq", 1),), 5)
    grad_hidden_two = conv_input_grad(padded_back_two, conv_two, 5, pooled_len)
    grad_norm_two, gain_two_grad, shift_two_grad = norm_back(
        gelu_back(before_two, grad_hidden_two), normed_two, inverse_two, gain_two, half_entries
    )
    grad_pooled = cotangent + grad_norm_two
    half_low = (0.5 * grad_pooled).astype(jnp.bfloat16)
    conv_low = jnp.broadcast_to(
        half_low[:, :, None, :], (windows, pooled_len, 2, channels)
    ).reshape(windows, length, channels)
    one_grad = conv_weight_grad(padded_one, conv_low, 1, length, conv_one.shape[0])
    padded_back_one = with_halo(conv_low, (("seq", 1),), 2)
    grad_hidden_one = conv_input_grad(padded_back_one, conv_one, 1, length)
    input_grad, gain_one_grad, shift_one_grad = norm_back(
        gelu_back(before_one, grad_hidden_one), normed_one, inverse_one, gain_one, entries
    )
    one_grad, two_grad, three_grad = lax.psum((one_grad, two_grad, three_grad), ("dp", "seq"))
    return (
        outputs,
        input_grad,
        one_grad,
        two_grad,
        three_grad,
        gain_one_grad,
        shift_one_grad,
        gain_two_grad,
        shift_two_grad,
        gain_three_grad,
        shift_three_grad,
    )


def solution(mesh):
    in_specs = (
        P("dp", "seq", None),
        P(),
        P(),
        P(),
        P(),
        P(),
        P(),
        P(),
        P(),
        P(),
        P("dp", "seq", None),
    )
    out_specs = (
        P("dp", "seq", None),
        P("dp", "seq", None),
        P(),
        P(),
        P(),
        P(),
        P(),
        P(),
        P(),
        P(),
        P(),
    )
    return jax.shard_map(
        on_device, mesh=mesh, in_specs=in_specs, out_specs=out_specs, check_vma=False
    )
```

profile of v0, /device:TPU:0, one launch (start us, length us, event | category | flops | bytes accessed | tf_op | source)
XLA Modules:
  0.0 1007.7 jit_solution(12366587737566768828)
XLA Ops:
  18.9 42.1 %all-reduce.5 = (f32[768]{0:T(1024)S(1)}, f32[768]{0:T(1024)S(1)}) all-reduce(f32[768]{0:T(1024)S(1)} %get-tuple-element.14, f32[768]{0:T(1024)S(1)} %get-tuple-element.13), channel_id=1, replica_groups=mesh['dp'=16,'seq'=2] {'dp','seq'}, use_global_device_ids=true, to_apply=%region_3.0 | all-reduce | flops 1536 | bytes 12288 | tf_op jit(solution)/shard_map/psum | solution.py:27
  61.6 14.3 %multiply_convert_fusion = bf16[2,4096,768]{2,1,0:T(8,128)(2,1)S(1)} fusion(f32[2,4096,768]{2,1,0:T(8,128)} %param.11, f32[768]{0:T(1024)S(1)} %copy-done.21, f32[768]{0:T(1024)S(1)} %copy-done.14, f32[768]{0:T(1024)S(1)} %get-tuple-element.50, f32[768]{0:T(1024)S(1)} %get-tuple-element.53), kind=kLoop, calls=%fused_computation.11 | loop fusion | flops 81788928 | bytes 37761024 | tf_op jit(solution)/shard_map/convert_element_type | solution.py:115
  78.6 15.3 %fusion.73 = f32[2,4096,768]{2,1,0:T(8,128)} fusion(bf16[2,4096,768]{2,1,0:T(8,128)(2,1)S(1)} %multiply_convert_fusion, bf16[5,768,768]{2,1,0:T(8,128)(2,1)} %param.12), kind=kOutput, calls=%fused_computation.116 | convolution fusion | flops 9663676416 | bytes 38928384 | tf_op jit(solution)/shard_map/wtc,cd->wtd/dot_general | solution.py:58
  93.9 18.0 %fusion.78 = f32[2,4096,768]{2,1,0:T(8,128)} fusion(bf16[5,768,768]{2,1,0:T(8,128)(2,1)} %param.12, bf16[2,2,768]{2,1,0:T(2,128)(2,1)S(1)} %collective-permute-done, bf16[2,4096,768]{2,1,0:T(8,128)(2,1)} %copy-done.4), kind=kOutput, calls=%fused_computation.121 | convolution fusion | flops 9688842240 | bytes 38934528 | tf_op jit(solution)/shard_map/wtc,cd->wtd/dot_general | solution.py:53
  111.9 18.2 %fusion.34 = f32[2,4096,768]{2,1,0:T(8,128)} fusion(bf16[2,4096,768]{2,1,0:T(8,128)(2,1)} %copy-done.4, bf16[2,2,768]{2,1,0:T(2,128)(2,1)S(1)} %collective-permute-done, bf16[5,768,768]{2,1,0:T(8,128)(2,1)} %param.12), kind=kOutput, calls=%fused_computation.64 | convolution fusion | flops 9688842240 | bytes 38934528 | tf_op jit(solution)/shard_map/wtc,cd->wtd/dot_general | solution.py:58
  130.1 19.2 %fusion.69 = f32[2,4096,768]{2,1,0:T(8,128)} fusion(bf16[5,768,768]{2,1,0:T(8,128)(2,1)} %param.12, bf16[2,4096,768]{2,1,0:T(8,128)(2,1)} %copy-done.4, bf16[2,2,768]{2,1,0:T(2,128)(2,1)S(1)} %collective-permute-done.1), kind=kOutput, calls=%fused_computation.112 | convolution fusion | flops 9688842240 | bytes 38934528 | tf_op jit(solution)/shard_map/wtc,cd->wtd/dot_general | solution.py:58
  149.4 47.3 %add_add_fusion = f32[2,4096,768]{2,1,0:T(8,128)} fusion(f32[2,4096,768]{2,1,0:T(8,128)} %fusion.69, f32[2,4096,768]{2,1,0:T(8,128)} %fusion.73, f32[2,4096,768]{2,1,0:T(8,128)} %fusion.78, f32[2,4096,768]{2,1,0:T(8,128)} %fusion.34, bf16[5,768,768]{2,1,0:T(8,128)(2,1)} %param.12, bf16[2,2,768]{2,1,0:T(2,128)(2,1)S(1)} %collective-permute-done.1, ...), kind=kOutput, calls=%fused_computation.10 | convolution fusion | flops 9714008064 | bytes 139597824 | tf_op jit(solution)/shard_map/wtc,cd->wtd/dot_general | solution.py:58
  196.6 29.1 %reshape.54 = f32[2,2048,2,768]{3,2,1,0:T(2,128)} reshape(f32[2,4096,768]{2,1,0:T(8,128)} %add_add_fusion) | data formatting | bytes 50331648 | tf_op jit(solution)/shard_map/reshape | solution.py:118
  225.8 25.3 %fusion.138 = (f32[2,2048,1,768]{3,2,1,0:T(1,128)}, f32[2,2048,1,768]{3,2,1,0:T(1,128)}) fusion(f32[2,2048,2,768]{3,2,1,0:T(2,128)} %reshape.54), kind=kLoop, calls=%fused_computation.184 | loop fusion | bytes 50331648 | tf_op jit(solution)/shard_map/slice | solution.py:119
  268.1 40.3 %all-reduce.4 = (f32[768]{0:T(1024)S(1)}, f32[768]{0:T(1024)S(1)}) all-reduce(f32[768]{0:T(1024)S(1)} %fusion.33, f32[768]{0:T(1024)S(1)} %get-tuple-element.37), channel_id=1, replica_groups=mesh['dp'=16,'seq'=2] {'dp','seq'}, use_global_device_ids=true, to_apply=%region_7.0 | all-reduce | flops 1536 | bytes 12288 | tf_op jit(solution)/shard_map/psum | solution.py:27
  341.8 40.0 %all-reduce.3 = (f32[384]{0:T(512)S(1)}, f32[384]{0:T(512)S(1)}) all-reduce(f32[384]{0:T(512)S(1)} %get-tuple-element.20, f32[384]{0:T(512)S(1)} %get-tuple-element.19), channel_id=1, replica_groups=mesh['dp'=16,'seq'=2] {'dp','seq'}, use_global_device_ids=true, to_apply=%region_11.0 | all-reduce | flops 768 | bytes 6144 | tf_op jit(solution)/shard_map/psum | solution.py:27
  406.0 40.3 %all-reduce.2 = (f32[384]{0:T(512)S(1)}, f32[384]{0:T(512)S(1)}) all-reduce(f32[384]{0:T(512)S(1)} %get-tuple-element.18, f32[384]{0:T(512)S(1)} %get-tuple-element.17), channel_id=1, replica_groups=mesh['dp'=16,'seq'=2] {'dp','seq'}, use_global_device_ids=true, to_apply=%region_15.0 | all-reduce | flops 768 | bytes 6144 | tf_op jit(solution)/shard_map/psum | solution.py:37
  502.7 19.3 %fusion.132 = (f32[768]{0:T(1024)S(1)}, f32[768]{0:T(1024)S(1)}, f32[2,2048,768]{2,1,0:T(8,128)}) fusion(f32[768]{0:T(1024)S(1)} %get-tuple-element.52, f32[768]{0:T(1024)S(1)} %get-tuple-element.54, f32[2,2048,1,768]{3,1,0,2:T(8,128)S(1)} %bitcast.128, f32[768]{0:T(1024)S(1)} %copy-done.25, f32[768]{0:T(1024)S(1)} %copy-done.16, ...), kind=kOutput, calls=%fused_computation.180 | convolution fusion | flops 2510289408 | bytes 54093312 | tf_op jit(solution)/shard_map/wtd,cd->wtc/dot_general | solution.py:87
  522.0 40.1 %all-reduce.1 = (f32[768]{0:T(1024)S(1)}, f32[768]{0:T(1024)S(1)}) all-reduce(f32[768]{0:T(1024)S(1)} %get-tuple-element.16, f32[768]{0:T(1024)S(1)} %get-tuple-element.15), channel_id=1, replica_groups=mesh['dp'=16,'seq'=2] {'dp','seq'}, use_global_device_ids=true, to_apply=%region_19.0 | all-reduce | flops 1536 | bytes 12288 | tf_op jit(solution)/shard_map/psum | solution.py:37
  583.7 26.1 %reshape.55 = bf16[2,4096,768]{2,1,0:T(8,128)(2,1)} reshape(bf16[2,2048,2,768]{3,2,1,0:T(2,128)(2,1)} %broadcast_in_dim.2) | data formatting | bytes 25165824 | tf_op jit(solution)/shard_map/reshape | solution.py:155
  621.1 17.9 %fusion.71 = f32[2,4096,768]{2,1,0:T(8,128)} fusion(bf16[2,4096,768]{2,1,0:T(8,128)(2,1)} %reshape.55, bf16[5,768,768]{2,1,0:T(8,128)(2,1)} %param.12), kind=kOutput, calls=%fused_computation.114 | convolution fusion | flops 9663676416 | bytes 38928384 | tf_op jit(solution)/shard_map/wtd,cd->wtc/dot_general | solution.py:87
  643.7 18.3 %bitcast_dynamic-update-slice_fusion.4 = f32[5,768,768]{2,1,0:T(8,128)} fusion(bf16[2,4096,768]{2,1,0:T(8,128)(2,1)} %reshape.55, bf16[2,2,768]{2,1,0:T(2,128)(2,1)S(1)} %copy-done.31, bf16[2,4096,768]{2,1,0:T(8,128)(2,1)} %copy-done.4), kind=kOutput, calls=%fused_computation.104 | convolution fusion | flops 9688842240 | bytes 27531264 | tf_op jit(solution)/shard_map/wtc,wtd->cd/dot_general | solution.py:72
  710.0 18.1 %fusion.27 = f32[2,4096,768]{2,1,0:T(8,128)} fusion(bf16[2,4098,768]{2,1,0:T(8,128)(2,1)} %constant_dynamic-update-slice_fusion, bf16[5,768,768]{2,1,0:T(8,128)(2,1)} %param.12), kind=kOutput, calls=%fused_computation.45 | convolution fusion | flops 9663676416 | bytes 38928384 | tf_op jit(solution)/shard_map/wtd,cd->wtc/dot_general | solution.py:87
  728.1 18.4 %fusion.29 = f32[2,4096,768]{2,1,0:T(8,128)} fusion(bf16[2,4098,768]{2,1,0:T(8,128)(2,1)} %constant_dynamic-update-slice_fusion, bf16[5,768,768]{2,1,0:T(8,128)(2,1)} %param.12), kind=kOutput, calls=%fused_computation.47 | convolution fusion | flops 9663676416 | bytes 38928384 | tf_op jit(solution)/shard_map/wtd,cd->wtc/dot_general | solution.py:87
  746.5 18.6 %fusion.7 = f32[2,4096,768]{2,1,0:T(8,128)} fusion(bf16[2,2,768]{2,1,0:T(2,128)(2,1)S(1)} %collective-permute-done.7, bf16[2,4096,768]{2,1,0:T(8,128)(2,1)} %reshape.55, bf16[5,768,768]{2,1,0:T(8,128)(2,1)} %param.12), kind=kOutput, calls=%fused_computation.25 | convolution fusion | flops 9688842240 | bytes 38934528 | tf_op jit(solution)/shard_map/wtd,cd->wtc/dot_general | solution.py:87
  765.1 57.2 %fusion.130 = (f32[768]{0:T(1024)S(1)}, f32[768]{0:T(1024)S(1)}, f32[2,4096,768]{2,1,0:T(8,128)}) fusion(f32[768]{0:T(1024)S(1)} %copy-done.10, f32[2,4096,768]{2,1,0:T(8,128)} %param.11, f32[768]{0:T(1024)S(1)} %copy-done.12, f32[768]{0:T(1024)S(1)} %copy-done.22, f32[768]{0:T(1024)S(1)} %copy-done.15, f32[2,4096,768]{2,1,0:T(8,128)} %fusion.7, ...), kind=kOutput, calls=%fused_computation.178 | convolution fusion | flops 9877583872 | bytes 164782080 | tf_op jit(solution)/shard_map/wtd,cd->wtc/dot_general | solution.py:87
  822.4 41.5 %all-reduce = (f32[768]{0:T(1024)S(1)}, f32[768]{0:T(1024)S(1)}) all-reduce(f32[768]{0:T(1024)S(1)} %get-tuple-element.12, f32[768]{0:T(1024)S(1)} %get-tuple-element.11), channel_id=1, replica_groups=mesh['dp'=16,'seq'=2] {'dp','seq'}, use_global_device_ids=true, to_apply=%region_23.0 | all-reduce | flops 1536 | bytes 12288 | tf_op jit(solution)/shard_map/psum | solution.py:37
  863.9 27.2 %subtract_multiply_fusion = f32[2,4096,768]{2,1,0:T(8,128)} fusion(f32[2,4096,768]{2,1,0:T(8,128)} %get-tuple-element.36, f32[2,4096,768]{2,1,0:T(8,128)} %param.11, f32[768]{0:T(1024)S(1)} %get-tuple-element.66, f32[768]{0:T(1024)S(1)} %broadcast_multiply_fusion.2, f32[768]{0:T(1024)S(1)} %copy-done.17, f32[768]{0:T(1024)S(1)} %copy-done.10, ...), kind=kLoop, calls=%fused_computation.8 | loop fusion | flops 44040192 | bytes 75512832 | tf_op jit(solution)/shard_map/mul | solution.py:41
  891.1 96.4 %all-reduce.9.cloned.1.call-done = (f32[5,768,768]{2,1,0:T(8,128)}, f32[3,768,384]{2,1,0:T(8,128)}, f32[384,768]{1,0:T(8,128)}) async-done(((f32[5,768,768]{2,1,0:T(8,128)}, f32[3,768,384]{2,1,0:T(8,128)}, f32[384,768]{1,0:T(8,128)}), (f32[5,768,768]{2,1,0:T(8,128)}, f32[3,768,384]{2,1,0:T(8,128)}, f32[384,768]{1,0:T(8,128)})) %all-reduce.9.cloned.1.call-update) | async-done | bytes 16515088 | tf_op jit(solution)/shard_map/psum | solution.py:162
  (151 shorter events, 244.3 us)
Async XLA Ops:
  7.2 386.0 %copy-start = (bf16[384,768]{1,0:T(8,128)(2,1)S(1)}, bf16[384,768]{1,0:T(8,128)(2,1)}, u32[]{:S(2)}) copy-start(bf16[384,768]{1,0:T(8,128)(2,1)} %param.14) | copy-start | bytes 1769476
  7.2 53.8 %copy-start.14 = (f32[768]{0:T(1024)S(1)}, f32[768]{0:T(1024)}, u32[]{:S(2)}) copy-start(f32[768]{0:T(1024)} %param.15) | copy-start | bytes 9220
  7.2 54.4 %copy-start.21 = (f32[768]{0:T(1024)S(1)}, f32[768]{0:T(1024)}, u32[]{:S(2)}) copy-start(f32[768]{0:T(1024)} %param.16) | copy-start | bytes 9220
  7.2 980.3 %all-reduce.9.cloned.1.call-start = ((), (), s32[]{:S(2)}) async-start(), calls=%async_computation | async-start | bytes 33030144 | tf_op jit(solution)/shard_map/psum | solution.py:162
  76.0 17.9 %collective-permute-start = (bf16[2,2,768]{2,1,0:T(2,128)(2,1)S(1)}, bf16[2,2,768]{2,1,0:T(2,128)(2,1)S(1)}, u32[]{:S(2)}, u32[]{:S(2)}) collective-permute-start(bf16[2,2,768]{2,1,0:T(2,128)(2,1)S(1)} %get-tuple-element.43), channel_id=1, source_target_pairs={{0,1},{2,3},{4,5},{6,7},{8,9},{10,11},{12,13},{14,15},{16,17},{18,... | collective-permute-start | bytes 18440 | tf_op jit(solution)/shard_map/ppermute | solution.py:17
  77.3 52.9 %collective-permute-start.1 = (bf16[2,2,768]{2,1,0:T(2,128)(2,1)S(1)}, bf16[2,2,768]{2,1,0:T(2,128)(2,1)S(1)}, u32[]{:S(2)}, u32[]{:S(2)}) collective-permute-start(bf16[2,2,768]{2,1,0:T(2,128)(2,1)S(1)} %get-tuple-element.44), channel_id=1, source_target_pairs={{1,0},{3,2},{5,4},{7,6},{9,8},{11,10},{13,12},{15,14},{17,16},{19,... | collective-permute-start | bytes 18440 | tf_op jit(solution)/shard_map/ppermute | solution.py:19
  262.4 46.0 %copy-start.16 = (f32[768]{0:T(1024)S(1)}, f32[768]{0:T(1024)}, u32[]{:S(2)}) copy-start(f32[768]{0:T(1024)} %param.17) | copy-start | bytes 9220
  262.4 46.0 %copy-start.25 = (f32[768]{0:T(1024)S(1)}, f32[768]{0:T(1024)}, u32[]{:S(2)}) copy-start(f32[768]{0:T(1024)} %param.18) | copy-start | bytes 9220
  268.1 53.8 %copy-start.8 = (bf16[3,768,384]{2,1,0:T(8,128)(2,1)S(1)}, bf16[3,768,384]{2,1,0:T(8,128)(2,1)}, u32[]{:S(2)}) copy-start(bf16[3,768,384]{2,1,0:T(8,128)(2,1)} %param.13) | copy-start | bytes 5308420
  317.1 16.5 %collective-permute-start.3 = (bf16[2,5,768]{2,1,0:T(8,128)(2,1)S(1)}, bf16[2,5,768]{2,1,0:T(8,128)(2,1)S(1)}, u32[]{:S(2)}, u32[]{:S(2)}) collective-permute-start(bf16[2,5,768]{2,1,0:T(8,128)(2,1)S(1)} %get-tuple-element.45), channel_id=1, source_target_pairs={{1,0},{3,2},{5,4},{7,6},{9,8},{11,10},{13,12},{15,14},{17,16},{19,... | collective-permute-start | bytes 46088 | tf_op jit(solution)/shard_map/ppermute | solution.py:19
  318.4 9.9 collective-permute-start.2
  333.6 48.3 %copy-start.13 = (f32[384]{0:T(512)S(1)}, f32[384]{0:T(512)}, u32[]{:S(2)}) copy-start(f32[384]{0:T(512)} %param.19) | copy-start | bytes 4612
  333.6 48.3 %copy-start.18 = (f32[384]{0:T(512)S(1)}, f32[384]{0:T(512)}, u32[]{:S(2)}) copy-start(f32[384]{0:T(512)} %param.20) | copy-start | bytes 4612
  341.8 51.4 %slice-start.9 = ((s8[6291456]{0:T(1024)(128)(4,1)}), s8[2097152]{0:T(1024)(128)(4,1)S(1)}, s32[]{:S(2)}) async-start(s8[6291456]{0:T(1024)(128)(4,1)} %bitcast.133), calls=%async_computation.10 | async-start | bytes 4194304
  479.8 23.0 %collective-permute-start.5 = (bf16[2,5,384]{2,1,0:T(8,128)(2,1)S(1)}, bf16[2,5,384]{2,1,0:T(8,128)(2,1)S(1)}, u32[]{:S(2)}, u32[]{:S(2)}) collective-permute-start(bf16[2,5,384]{2,1,0:T(8,128)(2,1)S(1)} %get-tuple-element.47), channel_id=1, source_target_pairs={{0,1},{2,3},{4,5},{6,7},{8,9},{10,11},{12,13},{14,15},{16,17},{18,... | collective-permute-start | bytes 23048 | tf_op jit(solution)/shard_map/ppermute | solution.py:17
  481.1 13.0 %collective-permute-start.4 = (bf16[2,5,384]{2,1,0:T(8,128)(2,1)S(1)}, bf16[2,5,384]{2,1,0:T(8,128)(2,1)S(1)}, u32[]{:S(2)}, u32[]{:S(2)}) collective-permute-start(bf16[2,5,384]{2,1,0:T(8,128)(2,1)S(1)} %get-tuple-element.48), channel_id=1, source_target_pairs={{1,0},{3,2},{5,4},{7,6},{9,8},{11,10},{13,12},{15,14},{17,16},{19,... | collective-permute-start | bytes 23048 | tf_op jit(solution)/shard_map/ppermute | solution.py:19
  621.1 22.6 %copy-start.31 = (bf16[2,2,768]{2,1,0:T(2,128)(2,1)S(1)}, bf16[2,2,768]{2,1,0:T(2,128)(2,1)}, u32[]{:S(2)}) copy-start(bf16[2,2,768]{2,1,0:T(2,128)(2,1)} %copy-done.30) | copy-start | bytes 18436
  638.9 70.4 %collective-permute-start.6 = (bf16[2,2,768]{2,1,0:T(2,128)(2,1)S(1)}, bf16[2,2,768]{2,1,0:T(2,128)(2,1)S(1)}, u32[]{:S(2)}, u32[]{:S(2)}) collective-permute-start(bf16[2,2,768]{2,1,0:T(2,128)(2,1)S(1)} %get-tuple-element.41), channel_id=1, source_target_pairs={{1,0},{3,2},{5,4},{7,6},{9,8},{11,10},{13,12},{15,14},{17,16},{19,... | collective-permute-start | bytes 18440 | tf_op jit(solution)/shard_map/ppermute | solution.py:19
  640.2 21.8 %slice-start.3 = ((s8[12582912]{0:T(1024)(128)(4,1)}), s8[4194304]{0:T(1024)(128)(4,1)S(1)}, s32[]{:S(2)}) async-start(s8[12582912]{0:T(1024)(128)(4,1)} %bitcast.129), calls=%async_computation.4 | async-start | bytes 8388608
  640.2 21.8 %slice-start.6 = ((s8[12582912]{0:T(1024)(128)(4,1)}), s8[4194304]{0:T(1024)(128)(4,1)S(1)}, s32[]{:S(2)}) async-start(s8[12582912]{0:T(1024)(128)(4,1)} %bitcast.131), calls=%async_computation.7 | async-start | bytes 8388608
  640.3 106.2 %collective-permute-start.7 = (bf16[2,2,768]{2,1,0:T(2,128)(2,1)S(1)}, bf16[2,2,768]{2,1,0:T(2,128)(2,1)S(1)}, u32[]{:S(2)}, u32[]{:S(2)}) collective-permute-start(bf16[2,2,768]{2,1,0:T(2,128)(2,1)S(1)} %get-tuple-element.42), channel_id=1, source_target_pairs={{0,1},{2,3},{4,5},{6,7},{8,9},{10,11},{12,13},{14,15},{16,17},{18,... | collective-permute-start | bytes 18440 | tf_op jit(solution)/shard_map/ppermute | solution.py:17
  765.1 98.8 %copy-start.17 = (f32[768]{0:T(1024)S(1)}, f32[768]{0:T(1024)}, u32[]{:S(2)}) copy-start(f32[768]{0:T(1024)} %get-tuple-element.49) | copy-start | bytes 9220
  863.9 27.2 %copy-start.24 = (f32[768]{0:T(1024)}, f32[768]{0:T(1024)S(1)}, u32[]{:S(2)}) copy-start(f32[768]{0:T(1024)S(1)} %get-tuple-element.67) | copy-start | bytes 9220
  863.9 27.2 %copy-start.27 = (f32[768]{0:T(1024)}, f32[768]{0:T(1024)S(1)}, u32[]{:S(2)}) copy-start(f32[768]{0:T(1024)S(1)} %get-tuple-element.66) | copy-start | bytes 9220
  (30 other events, 421.2 us)
Sparse Core Ops, SparseCore 0:
  709.5 277.9 all-reduce.8
where the time goes:
time: 1020 us; the launch traced here: 1010 us
  matrix products  421 us (41%)
  blocking collectives  244 us (24%)
  local copies, waits for them, and re-layouts  119 us (12%)
  other arithmetic  96.6 us (9%)
  waiting for transfers between devices  96.5 us (9%)
  starting transfers between devices  15.1 us (1%)
  between operations  14.9 us (1%)
    dot_general x8, matrix products, conv_input_grad(): jnp.einsum('wtd,cd->wtc', padded_grad[:, start:start + length], weight[ta...  166 us
    psum x3, blocking collectives, batch_norm(): lax.psum((jnp.sum(values, axis=(0, 1)), jnp.sum(values * values, axis=(0,...  122 us
    psum x3, blocking collectives, norm_back(): lax.psum((jnp.sum(grad_pre * normed, axis=(0, 1)), jnp.sum(grad_pre, axis...  122 us
    dot_general x6, matrix products, conv_forward(): jnp.einsum('wtc,cd->wtd', padded[:, start:start + length], weight[tap_ind...  115 us
    psum x1, waiting for transfers between devices, on_device(): lax.psum((one_grad, two_grad, three_grad), ('dp', 'seq'))  96.4 us
    dot_general x8, matrix products, conv_weight_grad(): jnp.einsum('wtc,wtd->cd', padded[:, start:start + length], grad_low, pref...  80.3 us
    reshape x1, local copies, waits for them, and re-layouts, on_device(): pairs = conv_out.reshape(windows, pooled_len, 2, channels)  29.1 us
    unnamed x94, local copies, waits for them, and re-layouts  29.1 us
  transfers between devices with their start and end apart: 9, of which 1 were waited for; matrix products, arithmetic and copies ran while one was open for 29% of the time, Pallas kernels for 0%

commit v1 on v0

v1 whole, which is shorter than its diff:
```python
import functools

import jax
import jax.numpy as jnp
from jax import lax
from jax.experimental import pallas as pl
from jax.experimental.pallas import tpu as pltpu
from jax.sharding import PartitionSpec as P

epsilon = 1e-05
bf16 = jnp.bfloat16
f32 = jnp.float32
LANES = 128
UNIT = 64
SUB = 32
EDGE = 8
MESH = pl.DeviceIdType.MESH
LINEAR = 0.7978845608028654
CUBIC = 0.7978845608028654 * 0.044715
VMEM_LIMIT = 60 << 20
NN = (((1,), (0,)), ((), ()))
NT = (((1,), (1,)), ((), ()))
TN = (((0,), (0,)), ((), ()))


def dot(a, b, dims=NN):
    return lax.dot_general(a, b, dims, preferred_element_type=f32)


def gelu(v):
    half = 0.5 * v
    return half + half * jnp.tanh(v * (LINEAR + CUBIC * (v * v)))


def gelu_both(v):
    square = v * v
    up = 0.5 + 0.5 * jnp.tanh(v * (LINEAR + CUBIC * square))
    value = v * up
    slope = up + value * (1.0 - up) * (2.0 * LINEAR + (6.0 * CUBIC) * square)
    return value, slope


def gelu_slope(v):
    square = v * v
    up = 0.5 + 0.5 * jnp.tanh(v * (LINEAR + CUBIC * square))
    return up + (v * up) * (1.0 - up) * (2.0 * LINEAR + (6.0 * CUBIC) * square)


def center_inverse(sums, entries):
    center = sums[0:1] / entries
    return center, lax.rsqrt(sums[1:2] / entries - center * center + epsilon)


def lanes(c, width=LANES):
    if isinstance(c, int):
        return pl.ds(c * width, width)
    return pl.ds(pl.multiple_of(c * width, width), width)


def folded(values):
    return jnp.sum(values.reshape(values.shape[0] // 8, 8, values.shape[1]), axis=0)


def interleave(pieces, units):
    done = 0
    for k, piece in enumerate(pieces):
        piece()
        until = (k + 1) * len(units) // len(pieces)
        for unit in units[done:until]:
            unit()
        done = until


def place_flags():
    return lax.axis_index("seq") == 0, lax.axis_index("seq") == lax.axis_size("seq") - 1


class Walk:
    def __init__(self, windows, length, tile):
        self.tile = tile
        self.per = length // tile
        self.count = windows * self.per
        self.at_start, self.at_end = place_flags()

    def where(self, i):
        return i // self.per, i % self.per

    def hide_left(self, i):
        return jnp.logical_and(i % self.per == 0, self.at_start)

    def hide_right(self, i):
        return jnp.logical_and(i % self.per == self.per - 1, self.at_end)

    def rows(self, i, scale=1):
        span = self.tile * scale
        return pl.ds(pl.multiple_of((i % self.per) * span, span), span)

    def fetch(self, i, src, left, right, dst, sem, scale=1):
        w, p = self.where(i)
        span = self.tile * scale
        low = pl.multiple_of(p * span, span)
        first, last = p == 0, p == self.per - 1
        pltpu.make_async_copy(src.at[w, pl.ds(low, span)], dst.at[pl.ds(EDGE, span)], sem).start()
        head, tail = dst.at[pl.ds(0, EDGE)], dst.at[pl.ds(EDGE + span, EDGE)]

        @pl.when(first)
        def _():
            pltpu.make_async_copy(left.at[w], head, sem).start()

        @pl.when(jnp.logical_not(first))
        def _():
            pltpu.make_async_copy(src.at[w, pl.ds(pl.multiple_of(low - EDGE, EDGE), EDGE)], head, sem).start()

        @pl.when(last)
        def _():
            pltpu.make_async_copy(right.at[w], tail, sem).start()

        @pl.when(jnp.logical_not(last))
        def _():
            pltpu.make_async_copy(src.at[w, pl.ds(pl.multiple_of(low + span, EDGE), EDGE)], tail, sem).start()


def wait_for(dst, sem):
    pltpu.make_async_copy(dst, dst, sem).wait()


ANY = pl.BlockSpec(memory_space=pl.ANY)
VM = pl.BlockSpec(memory_space=pltpu.VMEM)
DMA = pltpu.SemaphoreType.DMA


def params(flops=0, moved=0, waved=0):
    return dict(
        compiler_params=pltpu.CompilerParams(vmem_limit_bytes=VMEM_LIMIT),
        cost_estimate=pl.CostEstimate(flops=flops, bytes_accessed=moved, transcendentals=waved),
    )


def exchange_kernel(arrays, seqs, dps, *refs):
    stats = refs[0]
    sources = refs[1 : 1 + arrays]
    sums = refs[1 + arrays]
    outs = refs[2 + arrays : 2 + 3 * arrays]
    scratch = refs[2 + 3 * arrays :]
    lands = scratch[: 2 * arrays]
    message, near, far, near_send, near_recv, far_send, far_recv, edge_send, edge_recv = scratch[2 * arrays :]
    channels = stats.shape[2]
    slabs = channels // LANES
    seq, dp = lax.axis_index("seq"), lax.axis_index("dp")

    barrier = pltpu.get_barrier_semaphore()

    def greet_near(d, _):
        pl.semaphore_signal(barrier, inc=1, device_id={"seq": lax.rem(seq + d, seqs)}, device_id_type=MESH)
        return 0

    def greet_far(d, _):
        pl.semaphore_signal(barrier, inc=1, device_id={"dp": lax.rem(dp + d, dps)}, device_id_type=MESH)
        return 0

    lax.fori_loop(1, seqs, greet_near, 0)
    lax.fori_loop(1, dps, greet_far, 0)
    pl.semaphore_wait(barrier, seqs - 1 + dps - 1)

    def edge_copy(a, side):
        src = sources[a]
        length = src.shape[1]
        part = src.at[:, pl.ds(length - EDGE, EDGE)] if side == 0 else src.at[:, pl.ds(0, EDGE)]
        to = seq + 1 if side == 0 else seq - 1
        return pltpu.make_async_remote_copy(
            src_ref=part, dst_ref=lands[2 * a + side], send_sem=edge_send.at[2 * a + side],
            recv_sem=edge_recv.at[2 * a + side], device_id={"seq": to}, device_id_type=MESH,
        )

    message[...] = jnp.zeros_like(message)
    for row in range(2):
        total = jnp.sum(stats[row], axis=0, keepdims=True)
        for c in range(slabs):
            message[row * slabs + c : row * slabs + c + 1] = total[:, c * LANES : (c + 1) * LANES]

    def near_copy(d, to):
        return pltpu.make_async_remote_copy(
            src_ref=message, dst_ref=near.at[seq], send_sem=near_send.at[d], recv_sem=near_recv.at[d],
            device_id={"seq": to}, device_id_type=MESH,
        )

    def near_start(d, _):
        near_copy(d, lax.rem(seq + d, seqs)).start()
        return 0

    def near_wait(d, _):
        near_copy(d, lax.rem(seq + d, seqs)).wait()
        return 0

    lax.fori_loop(1, seqs, near_start, 0)

    for a in range(arrays):
        @pl.when(seq < seqs - 1)
        def _():
            edge_copy(a, 0).start()

        @pl.when(seq > 0)
        def _():
            edge_copy(a, 1).start()

    near[seq] = message[...]
    lax.fori_loop(1, seqs, near_wait, 0)
    far[dp] = lax.fori_loop(1, seqs, lambda s, t: t + near[s], near[0])

    def far_copy(d, to):
        return pltpu.make_async_remote_copy(
            src_ref=far.at[dp], dst_ref=far.at[dp], send_sem=far_send.at[d], recv_sem=far_recv.at[d],
            device_id={"dp": to}, device_id_type=MESH,
        )

    def far_start(d, _):
        far_copy(d, lax.rem(dp + d, dps)).start()
        return 0

    def far_wait(d, _):
        far_copy(d, lax.rem(dp + d, dps)).wait()
        return 0

    lax.fori_loop(1, dps, far_start, 0)

    for a in range(arrays):
        @pl.when(seq < seqs - 1)
        def _():
            edge_copy(a, 0).wait_send()
            edge_copy(a, 1).wait_recv()

        @pl.when(seq > 0)
        def _():
            edge_copy(a, 1).wait_send()
            edge_copy(a, 0).wait_recv()

        for side in range(2):
            outs[2 * a + side][...] = lands[2 * a + side][...]

    lax.fori_loop(1, dps, far_wait, 0)
    total = lax.fori_loop(1, dps, lambda s, t: t + far[s], far[0])
    sums[...] = jnp.zeros_like(sums)
    for row in range(2):
        for c in range(slabs):
            sums[row : row + 1, c * LANES : (c + 1) * LANES] = total[row * slabs + c : row * slabs + c + 1]


def exchange(stats, arrays, number):
    seqs, dps = lax.axis_size("seq"), lax.axis_size("dp")
    channels = stats.shape[2]
    rows = -(-2 * (channels // LANES) // 8) * 8
    edges = [jax.ShapeDtypeStruct((a.shape[0], EDGE, a.shape[2]), a.dtype) for a in arrays for _ in range(2)]
    got = pl.pallas_call(
        functools.partial(exchange_kernel, len(arrays), seqs, dps),
        out_shape=[jax.ShapeDtypeStruct((8, channels), f32)] + edges,
        in_specs=[VM] + [ANY] * len(arrays),
        out_specs=[VM] * (1 + len(edges)),
        scratch_shapes=[pltpu.VMEM(e.shape, e.dtype) for e in edges]
        + [
            pltpu.VMEM((rows, LANES), f32),
            pltpu.VMEM((seqs, rows, LANES), f32),
            pltpu.VMEM((dps, rows, LANES), f32),
            DMA((seqs,)),
            DMA((seqs,)),
            DMA((dps,)),
            DMA((dps,)),
            DMA((2 * max(len(arrays), 1),)),
            DMA((2 * max(len(arrays), 1),)),
        ],
        compiler_params=pltpu.CompilerParams(collective_id=number, has_side_effects=True),
        name=f"exchange_{number}",
    )(stats, *arrays)
    return got[0], got[1:]


def sums_kernel(x, stats):
    @pl.when(pl.program_id(0) == 0)
    def _():
        stats[...] = jnp.zeros_like(stats)

    channels = x.shape[2]
    for c in range(channels // LANES):
        total = jnp.zeros((8, LANES), f32)
        squares = jnp.zeros((8, LANES), f32)
        for r in range(0, x.shape[1], 128):
            v = x[0, r : r + 128, lanes(c)]
            total += folded(v)
            squares += folded(v * v)
        stats[0, :, lanes(c)] += total
        stats[1, :, lanes(c)] += squares


def input_sums(x):
    windows, length, channels = x.shape
    tile = min(1024, length)
    per = length // tile
    return pl.pallas_call(
        sums_kernel,
        grid=(windows * per,),
        out_shape=jax.ShapeDtypeStruct((2, 8, channels), f32),
        in_specs=[pl.BlockSpec((1, tile, channels), lambda i: (i // per, i % per, 0))],
        out_specs=pl.BlockSpec((2, 8, channels), lambda i: (0, 0, 0)),
        name="input_sums",
        **params(moved=4 * x.size),
    )(x)


def conv_one_kernel(
    tile, entries, x, left, right, sums, gain, shift, w_hbm, pooled, s_out, first_out, stats,
    xs, h_buf, lhs_a, lhs_b, outs, coef, w_ref, x_sem, s_sem, f_sem, o_sem, w_sem,
):
    windows, length, channels = x.shape
    slabs = channels // LANES
    span = 2 * tile
    walk = Walk(windows, length // 2, tile)
    tiles = walk.count
    lhs = (lhs_a, lhs_b)
    center, inverse = center_inverse(sums[...], entries)
    scale = inverse * gain[...]
    offset = shift[...] - center * scale
    for c in range(slabs):
        coef[c, 0:1] = scale[:, lanes_of(c)]
        coef[c, 1:2] = offset[:, lanes_of(c)]
    stats[...] = jnp.zeros_like(stats)

    def load(i, slot):
        walk.fetch(i, x, left, right, xs.at[slot], x_sem.at[slot], 2)

    def s_copy(i, slot, which):
        w, _ = walk.where(i)
        return pltpu.make_async_copy(
            lhs[slot].at[:, pl.ds((2 + which) * channels, channels)], s_out.at[which, w, walk.rows(i)],
            s_sem.at[slot, which],
        )

    def first_copy(i, slot):
        w, _ = walk.where(i)
        return pltpu.make_async_copy(
            lhs[slot].at[pl.ds(0, 16), pl.ds(channels, channels)], first_out.at[w], f_sem
        )

    def o_copy(i, slot):
        w, _ = walk.where(i)
        return pltpu.make_async_copy(outs.at[slot], pooled.at[w, walk.rows(i)], o_sem.at[slot])

    def activate(i, slot, c):
        scale = coef[c, 0:1]
        offset = coef[c, 1:2]
        src = xs.at[slot]
        dst = lhs[slot]
        cols = lanes(c)

        def ends():
            head = gelu(src[0:EDGE, cols] * scale + offset)
            h_buf[c, 0:EDGE] = jnp.where(walk.hide_left(i), 0.0, head)
            tail = gelu(src[EDGE + span : 2 * EDGE + span, cols] * scale + offset)
            h_buf[c, EDGE + span : 2 * EDGE + span] = jnp.where(walk.hide_right(i), 0.0, tail)

        def rows(r):
            def run():
                for q in range(EDGE + r, EDGE + r + 2 * UNIT, 2 * SUB):
                    h_buf[c, q : q + 2 * SUB] = gelu(src[q : q + 2 * SUB, cols] * scale + offset)

            return run

        def taps(r):
            def run():
                for q in range(r, r + UNIT, SUB):
                    h = [h_buf[c, pl.ds(EDGE + 2 * q + d, SUB, stride=2)] for d in range(-2, 4)]
                    for tap in range(5):
                        at = pl.ds(pl.multiple_of(tap * channels + c * LANES, LANES), LANES)
                        dst[q : q + SUB, at] = (h[tap] + h[tap + 1]).astype(bf16)

            return run

        units = [ends, rows(0)]
        for r in range(UNIT, tile, UNIT):
            units += [rows(2 * r), taps(r - UNIT)]
        return units + [taps(tile - UNIT)]

    def matmul(slot, n):
        cols = lanes(n, 256)
        src = lhs[slot]
        held = []

        def piece(k):
            def run():
                at = slice(k * channels, (k + 1) * channels)
                part = dot(src[:, at], w_ref[at, cols])
                held[:] = [held[0] + part] if held else [part]

            return run

        def finish():
            total = 0.5 * held[0]
            outs[slot, :, cols] = total
            stats[0, :, cols] += folded(total)
            stats[1, :, cols] += folded(total * total)

        return [piece(k) for k in range(5)], finish

    load(0, 0)
    wait_for(xs.at[0], x_sem.at[0])
    w_copy = pltpu.make_async_copy(w_hbm, w_ref, w_sem)
    w_copy.start()
    load(1, 1)

    def first_slab(c, _):
        for unit in activate(0, 0, c):
            unit()
        return 0

    lax.fori_loop(0, slabs, first_slab, 0)
    for which in range(2):
        s_copy(0, 0, which).start()
    first_copy(0, 0).start()
    w_copy.wait()

    def pair(j, _):
        for slot in range(2):
            i = 2 * j + slot
            other = 1 - slot

            @pl.when(i + 1 < tiles)
            def _():
                wait_for(xs.at[other], x_sem.at[other])

            @pl.when(i + 2 < tiles)
            def _():
                load(i + 2, slot)

            @pl.when(i >= 1)
            def _():
                for which in range(2):
                    s_copy(i - 1, other, which).wait()

                @pl.when((i - 1) % walk.per == 0)
                def _():
                    first_copy(i - 1, other).wait()

            @pl.when(i >= 2)
            def _():
                o_copy(i - 2, slot).wait()

            def part(n, _):
                pieces, finish = matmul(slot, n)
                units = []
                for c in range(2):
                    units += activate(i + 1, other, 2 * n + c)
                interleave(pieces, units)
                finish()
                return 0

            lax.fori_loop(0, channels // 256, part, 0)
            o_copy(i, slot).start()

            @pl.when(i + 1 < tiles)
            def _():
                for which in range(2):
                    s_copy(i + 1, other, which).start()

                @pl.when((i + 1) % walk.per == 0)
                def _():
                    first_copy(i + 1, other).start()

        return 0

    lax.fori_loop(0, tiles // 2, pair, 0)
    for which in range(2):
        s_copy(tiles - 1, 1, which).wait()
    if walk.per == 1:
        first_copy(tiles - 1, 1).wait()
    o_copy(tiles - 2, 0).wait()
    o_copy(tiles - 1, 1).wait()


def lanes_of(c):
    return slice(c * LANES, (c + 1) * LANES)


def conv_one_forward(x, left, right, sums, gain, shift, weight, entries):
    windows, length, channels = x.shape
    half = length // 2
    tile = min(512, half)
    slabs = channels // LANES
    return pl.pallas_call(
        functools.partial(conv_one_kernel, tile, entries),
        out_shape=(
            jax.ShapeDtypeStruct((windows, half, channels), f32),
            jax.ShapeDtypeStruct((2, windows, half, channels), bf16),
            jax.ShapeDtypeStruct((windows, 16, channels), bf16),
            jax.ShapeDtypeStruct((2, 8, channels), f32),
        ),
        in_specs=[ANY, ANY, ANY, VM, VM, VM, ANY],
        out_specs=(ANY, ANY, ANY, VM),
        scratch_shapes=[
            pltpu.VMEM((2, 2 * tile + 2 * EDGE, channels), f32),
            pltpu.VMEM((slabs, 2 * tile + 2 * EDGE, LANES), f32),
            pltpu.VMEM((tile, 5 * channels), bf16),
            pltpu.VMEM((tile, 5 * channels), bf16),
            pltpu.VMEM((2, tile, channels), f32),
            pltpu.VMEM((slabs, 8, LANES), f32),
            pltpu.VMEM((5 * channels, channels), bf16),
            DMA((2,)),
            DMA((2, 2)),
            DMA,
            DMA((2,)),
            DMA,
        ],
        name="conv_one_forward",
        **params(10 * windows * half * channels * channels, 8 * x.size, x.size),
    )(x, left, right, sums, gain, shift, weight.reshape(5 * channels, channels))


def conv_two_kernel(
    tile, entries, v, left, right, sums, gain, shift, w_hbm, narrow, h_out, stats,
    vs, h_buf, lhs_a, lhs_b, outs, w_ref, v_sem, h_sem, o_sem, w_sem,
):
    windows, length, channels = v.shape
    slabs = channels // LANES
    walk = Walk(windows, length, tile)
    tiles = walk.count
    lhs = (lhs_a, lhs_b)
    center, inverse = center_inverse(sums[...], entries)
    scale = inverse * gain[...]
    offset = shift[...] - center * scale
    stats[...] = jnp.zeros_like(stats)

    def load(i, slot):
        walk.fetch(i, v, left, right, vs.at[slot], v_sem.at[slot])

    def h_copy(i, slot):
        w, _ = walk.where(i)
        return pltpu.make_async_copy(
            lhs[slot].at[:, pl.ds(channels, channels)], h_out.at[w, walk.rows(i)], h_sem.at[slot]
        )

    def o_copy(i, slot):
        w, _ = walk.where(i)
        return pltpu.make_async_copy(outs.at[slot], narrow.at[w, walk.rows(i)], o_sem.at[slot])

    def activate(i, slot, c):
        a, b = scale[:, lanes_of(c)], offset[:, lanes_of(c)]
        src, dst, cols = vs.at[slot], lhs[slot], lanes(c)

        def ends():
            head = gelu(src[0:EDGE, cols] * a + b)
            h_buf[c, 0:EDGE] = jnp.where(walk.hide_left(i), 0.0, head)
            tail = gelu(src[EDGE + tile : 2 * EDGE + tile, cols] * a + b)
            h_buf[c, EDGE + tile : 2 * EDGE + tile] = jnp.where(walk.hide_right(i), 0.0, tail)

        def rows(r):
            def run():
                q = EDGE + r
                h_buf[c, q : q + UNIT] = gelu(src[q : q + UNIT, cols] * a + b)

            return run

        def taps(r):
            def run():
                for tap in range(3):
                    at = EDGE + r + 5 * (tap - 1)
                    dst[r : r + UNIT, lanes(tap * slabs + c)] = h_buf[c, at : at + UNIT].astype(bf16)

            return run

        units = [ends, rows(0)]
        for r in range(UNIT, tile, UNIT):
            units += [rows(r), taps(r - UNIT)]
        return units + [taps(tile - UNIT)]

    load(0, 0)
    wait_for(vs.at[0], v_sem.at[0])
    w_copy = pltpu.make_async_copy(w_hbm, w_ref, w_sem)
    w_copy.start()
    load(1, 1)
    for c in range(slabs):
        for unit in activate(0, 0, c):
            unit()
    h_copy(0, 0).start()
    w_copy.wait()

    def pair(j, _):
        for slot in range(2):
            i = 2 * j + slot
            other = 1 - slot

            @pl.when(i + 1 < tiles)
            def _():
                wait_for(vs.at[other], v_sem.at[other])

            @pl.when(i + 2 < tiles)
            def _():
                load(i + 2, slot)

            @pl.when(i >= 1)
            def _():
                h_copy(i - 1, other).wait()

            @pl.when(i >= 2)
            def _():
                o_copy(i - 2, slot).wait()

            held = []

            def piece(k):
                def run():
                    at = slice(k * channels, (k + 1) * channels)
                    part = dot(lhs[slot][:, at], w_ref[at])
                    held[:] = [held[0] + part] if held else [part]

                return run

            units = []
            for c in range(slabs):
                units += activate(i + 1, other, c)
            interleave([piece(k) for k in range(3)], units)
            total = held[0]
            outs[slot] = total
            stats[0] += folded(total)
            stats[1] += folded(total * total)
            o_copy(i, slot).start()

            @pl.when(i + 1 < tiles)
            def _():
                h_copy(i + 1, other).start()

        return 0

    lax.fori_loop(0, tiles // 2, pair, 0)
    h_copy(tiles - 1, 1).wait()
    o_copy(tiles - 2, 0).wait()
    o_copy(tiles - 1, 1).wait()


def conv_two_forward(v, left, right, sums, gain, shift, weight, entries):
    windows, length, channels = v.shape
    tile = min(512, length)
    slabs = channels // LANES
    width = weight.shape[2]
    return pl.pallas_call(
        functools.partial(conv_two_kernel, tile, entries),
        out_shape=(
            jax.ShapeDtypeStruct((windows, length, width), f32),
            jax.ShapeDtypeStruct((windows, length, channels), bf16),
            jax.ShapeDtypeStruct((2, 8, width), f32),
        ),
        in_specs=[ANY, ANY, ANY, VM, VM, VM, ANY],
        out_specs=(ANY, ANY, VM),
        scratch_shapes=[
            pltpu.VMEM((2, tile + 2 * EDGE, channels), f32),
            pltpu.VMEM((slabs, tile + 2 * EDGE, LANES), f32),
            pltpu.VMEM((tile, 3 * channels), bf16),
            pltpu.VMEM((tile, 3 * channels), bf16),
            pltpu.VMEM((2, tile, width), f32),
            pltpu.VMEM((3 * channels, width), bf16),
            DMA((2,)),
            DMA((2,)),
            DMA((2,)),
            DMA,
        ],
        name="conv_two_forward",
        **params(6 * v.size * width, 8 * v.size, v.size),
    )(v, left, right, sums, gain, shift, weight.reshape(3 * channels, width))


def conv_three_kernel(
    entries, narrow, cotangent, pooled, sums, gain, shift, w_ref, outputs, da, stats, w_grad,
    branch, grad, hidden, total,
):
    tile = narrow.shape[1]
    step = pl.program_id(0)
    center, inverse = center_inverse(sums[...], entries)

    @pl.when(step == 0)
    def _():
        stats[...] = jnp.zeros_like(stats)
        total[...] = jnp.zeros_like(total)

    branch[...] = cotangent[0].astype(bf16)
    grad[...] = dot(branch[...], w_ref[...], NT)
    for c in range(narrow.shape[2] // LANES):
        cols = lanes(c)
        at = lanes_of(c)
        m, inv, g, s = center[:, at], inverse[:, at], gain[:, at], shift[:, at]
        gains = jnp.zeros((8, LANES), f32)
        shifts = jnp.zeros((8, LANES), f32)
        for r in range(0, tile, UNIT):
            normed = (narrow[0, r : r + UNIT, cols] - m) * inv
            value, slope = gelu_both(normed * g + s)
            hidden[r : r + UNIT, cols] = value.astype(bf16)
            back = slope * grad[r : r + UNIT, cols]
            da[0, r : r + UNIT, cols] = back
            gains += folded(back * normed)
            shifts += folded(back)
        stats[0, :, cols] += gains
        stats[1, :, cols] += shifts
    outputs[0] = pooled[0] + dot(hidden[...], w_ref[...])
    total[...] += dot(hidden[...], branch[...], TN)

    @pl.when(step == pl.num_programs(0) - 1)
    def _():
        w_grad[...] = total[...].astype(bf16)


def conv_three_both(narrow, cotangent, pooled, sums, gain, shift, weight, entries):
    windows, length, width = narrow.shape
    channels = weight.shape[1]
    tile = min(512, length)
    per = length // tile
    rows = lambda i: (i // per, i % per, 0)
    whole = lambda i: (0, 0)
    return pl.pallas_call(
        functools.partial(conv_three_kernel, entries),
        grid=(windows * per,),
        out_shape=(
            jax.ShapeDtypeStruct((windows, length, channels), f32),
            jax.ShapeDtypeStruct((windows, length, width), f32),
            jax.ShapeDtypeStruct((2, 8, width), f32),
            jax.ShapeDtypeStruct((width, channels), bf16),
        ),
        in_specs=[
            pl.BlockSpec((1, tile, width), rows),
            pl.BlockSpec((1, tile, channels), rows),
            pl.BlockSpec((1, tile, channels), rows),
            pl.BlockSpec((8, width), whole),
            pl.BlockSpec((1, width), whole),
            pl.BlockSpec((1, width), whole),
            pl.BlockSpec((width, channels), whole),
        ],
        out_specs=(
            pl.BlockSpec((1, tile, channels), rows),
            pl.BlockSpec((1, tile, width), rows),
            pl.BlockSpec((2, 8, width), lambda i: (0, 0, 0)),
            pl.BlockSpec((width, channels), whole),
        ),
        scratch_shapes=[
            pltpu.VMEM((tile, channels), bf16),
            pltpu.VMEM((tile, width), f32),
            pltpu.VMEM((tile, width), bf16),
            pltpu.VMEM((width, channels), f32),
        ],
        name="conv_three_both",
        **params(6 * narrow.size * channels, 12 * cotangent.size, narrow.size),
    )(narrow, cotangent, pooled, sums, gain, shift, weight)


def conv_two_back_kernel(
    tile, entries, da, da_left, da_right, v, v_left, v_right, sums3, grads3, gain3, pooled, sums2, gain2, shift2,
    h, w_hbm, da_out, stats, w_grad,
    das, vs, ps, hs, low_buf, low_a, low_b, g_buf, outs, total, w_ref, w_flip,
    a_sem, v_sem, p_sem, h_sem, o_sem, w_sem,
):
    windows, length, width = da.shape
    channels = pooled.shape[2]
    thin, slabs = width // LANES, channels // LANES
    walk = Walk(windows, length, tile)
    tiles = walk.count
    low = (low_a, low_b)
    center3, inverse3 = center_inverse(sums3[...], entries)
    grads = grads3[...]
    scale3 = inverse3 * gain3[...]
    lean = scale3 * inverse3 * (grads[0:1] / entries)
    flat = scale3 * (grads[1:2] / entries)
    center, inverse = center_inverse(sums2[...], entries)
    stats[...] = jnp.zeros_like(stats)
    total[...] = jnp.zeros_like(total)

    def load(i, slot):
        walk.fetch(i, da, da_left, da_right, das.at[slot], a_sem.at[slot])
        walk.fetch(i, v, v_left, v_right, vs.at[slot], v_sem.at[slot])

    def wait_load(slot):
        wait_for(das.at[slot], a_sem.at[slot])
        wait_for(vs.at[slot], v_sem.at[slot])

    def late_copies(i, slot):
        w, _ = walk.where(i)
        return (
            pltpu.make_async_copy(pooled.at[w, walk.rows(i)], ps.at[slot], p_sem.at[slot]),
            pltpu.make_async_copy(h.at[w, walk.rows(i)], hs.at[slot], h_sem.at[slot]),
        )

    def o_copy(i, slot):
        w, _ = walk.where(i)
        return pltpu.make_async_copy(outs.at[slot], da_out.at[w, walk.rows(i)], o_sem.at[slot])

    def lower(i, slot, c):
        at, cols = lanes_of(c), lanes(c)
        m, s, l, f = center3[:, at], scale3[:, at], lean[:, at], flat[:, at]
        dst = low[slot]

        def value(q, size):
            return das[slot, q : q + size, cols] * s - (vs[slot, q : q + size, cols] - m) * l - f

        def ends():
            low_buf[c, 0:EDGE] = jnp.where(walk.hide_left(i), 0.0, value(0, EDGE))
            low_buf[c, EDGE + tile : 2 * EDGE + tile] = jnp.where(walk.hide_right(i), 0.0, value(EDGE + tile, EDGE))

        def rows(r):
            def run():
                low_buf[c, EDGE + r : EDGE + r + UNIT] = value(EDGE + r, UNIT)

            return run

        def taps(r):
            def run():
                for tap in range(3):
                    q = EDGE + r - 5 * (tap - 1)
                    dst[r : r + UNIT, lanes(tap * thin + c)] = low_buf[c, q : q + UNIT].astype(bf16)

            return run

        units = [ends, rows(0)]
        for r in range(UNIT, tile, UNIT):
            units += [rows(r), taps(r - UNIT)]
        return units + [taps(tile - UNIT)]

    def finish(slot, c):
        at, cols = lanes_of(c), lanes(c)
        m, inv, g, s = center[:, at], inverse[:, at], gain2[:, at], shift2[:, at]
        sums = [jnp.zeros((8, LANES), f32), jnp.zeros((8, LANES), f32)]

        def rows(r):
            def run():
                normed = (ps[slot, r : r + UNIT, cols] - m) * inv
                back = gelu_slope(normed * g + s) * g_buf[r : r + UNIT, cols]
                outs[slot, r : r + UNIT, cols] = back
                sums[0] = sums[0] + folded(back * normed)
                sums[1] = sums[1] + folded(back)

            return run

        def close():
            stats[0, :, cols] += sums[0]
            stats[1, :, cols] += sums[1]

        return [rows(r) for r in range(0, tile, UNIT)] + [close]

    load(0, 0)
    w_copy = pltpu.make_async_copy(w_hbm, w_ref, w_sem)
    w_copy.start()
    for copy in late_copies(0, 0):
        copy.start()
    wait_load(0)
    load(1, 1)
    for c in range(thin):
        for unit in lower(0, 0, c):
            unit()
    w_copy.wait()
    for k in range(3):
        w_flip[k * width : (k + 1) * width] = w_ref[k].T

    def pair(j, _):
        for slot in range(2):
            i = 2 * j + slot
            other = 1 - slot

            @pl.when(i + 1 < tiles)
            def _():
                wait_load(other)
                for copy in late_copies(i + 1, other):
                    copy.start()

            @pl.when(i + 2 < tiles)
            def _():
                load(i + 2, slot)

            for copy in late_copies(i, slot):
                copy.wait()

            @pl.when(i >= 2)
            def _():
                o_copy(i - 2, slot).wait()

            def back(n):
                def run():
                    cols = lanes(n, 256)
                    g_buf[:, cols] = dot(low[slot][...], w_flip[:, cols])

                return run

            def weigh(n):
                def run():
                    at = slice(n * 256, (n + 1) * 256)
                    total[at] += dot(hs[slot, :, at], low[slot][...], TN)

                return run

            units = []
            for c in range(thin):
                units += lower(i + 1, other, c)
            interleave([back(n) for n in range(channels // 256)], units)
            units = []
            for c in range(slabs):
                units += finish(slot, c)
            interleave([weigh(n) for n in range(channels // 256)], units)
            o_copy(i, slot).start()

        return 0

    lax.fori_loop(0, tiles // 2, pair, 0)
    for k in range(3):
        w_grad[k] = total[:, k * width : (k + 1) * width].astype(bf16)
    o_copy(tiles - 2, 0).wait()
    o_copy(tiles - 1, 1).wait()


def conv_two_back(da, da_sides, v, v_sides, sums3, grads3, gain3, pooled, sums2, gain2, shift2, h, weight, entries):
    windows, length, width = da.shape
    channels = pooled.shape[2]
    tile = min(512, length)
    thin, slabs = width // LANES, channels // LANES
    return pl.pallas_call(
        functools.partial(conv_two_back_kernel, tile, entries),
        out_shape=(
            jax.ShapeDtypeStruct((windows, length, channels), f32),
            jax.ShapeDtypeStruct((2, 8, channels), f32),
            jax.ShapeDtypeStruct(weight.shape, bf16),
        ),
        in_specs=[ANY] * 6 + [VM] * 3 + [ANY] + [VM] * 3 + [ANY] * 2,
        out_specs=(ANY, VM, VM),
        scratch_shapes=[
            pltpu.VMEM((2, tile + 2 * EDGE, width), f32),
            pltpu.VMEM((2, tile + 2 * EDGE, width), f32),
            pltpu.VMEM((2, tile, channels), f32),
            pltpu.VMEM((2, tile, channels), bf16),
            pltpu.VMEM((thin, tile + 2 * EDGE, LANES), f32),
            pltpu.VMEM((tile, 3 * width), bf16),
            pltpu.VMEM((tile, 3 * width), bf16),
            pltpu.VMEM((tile, channels), f32),
            pltpu.VMEM((2, tile, channels), f32),
            pltpu.VMEM((channels, 3 * width), f32),
            pltpu.VMEM(weight.shape, bf16),
            pltpu.VMEM((3 * width, channels), bf16),
            DMA((2,)),
            DMA((2,)),
            DMA((2,)),
            DMA((2,)),
            DMA((2,)),
            DMA,
        ],
        name="conv_two_back",
        **params(12 * pooled.size * width, 16 * pooled.size, pooled.size),
    )(da, *da_sides, v, *v_sides, sums3, grads3, gain3, pooled, sums2, gain2, shift2, h, weight)


def conv_one_back_kernel(
    tile, entries, da, da_left, da_right, v, v_left, v_right, ct, ct_left, ct_right, sums2, grads2, gain2,
    x, sums1, gain1, shift1, s, first, w_hbm, da_out, stats, w_grad,
    das, vs, cts, ss, xs, firsts, low_buf, low_a, low_b, g_buf, outs, total, w_ref,
    a_sem, v_sem, c_sem, s_sem, x_sem, f_sem, o_sem, w_sem, g_sem,
):
    windows, length, channels = da.shape
    slabs = channels // LANES
    span = 2 * tile
    walk = Walk(windows, length, tile)
    tiles = walk.count
    low = (low_a, low_b)
    half_entries = entries / 2
    center2, inverse2 = center_inverse(sums2[...], half_entries)
    grads = grads2[...]
    scale2 = 0.5 * inverse2 * gain2[...]
    lean = scale2 * inverse2 * (grads[0:1] / half_entries)
    flat = scale2 * (grads[1:2] / half_entries)
    center, inverse = center_inverse(sums1[...], entries)
    stats[...] = jnp.zeros_like(stats)

    def load(i, slot):
        walk.fetch(i, da, da_left, da_right, das.at[slot], a_sem.at[slot])
        walk.fetch(i, v, v_left, v_right, vs.at[slot], v_sem.at[slot])
        walk.fetch(i, ct, ct_left, ct_right, cts.at[slot], c_sem.at[slot])

    def wait_load(slot):
        wait_for(das.at[slot], a_sem.at[slot])
        wait_for(vs.at[slot], v_sem.at[slot])
        wait_for(cts.at[slot], c_sem.at[slot])

    def late_copies(i, slot):
        w, _ = walk.where(i)
        return (
            pltpu.make_async_copy(x.at[w, walk.rows(i, 2)], xs.at[slot], x_sem.at[slot]),
            pltpu.make_async_copy(s.at[:, w, walk.rows(i)], ss.at[slot], s_sem.at[slot]),
        )

    def o_copy(i, slot):
        w, _ = walk.where(i)
        return pltpu.make_async_copy(outs.at[slot], da_out.at[w, walk.rows(i, 2)], o_sem.at[slot])

    def lower(i, slot, c):
        at, cols = lanes_of(c), lanes(c)
        m, sc, l, f = center2[:, at], scale2[:, at], lean[:, at], flat[:, at]
        dst = low[slot]

        def value(q, size):
            rows = slice(q, q + size)
            return 0.5 * cts[slot, rows, cols] + das[slot, rows, cols] * sc - (vs[slot, rows, cols] - m) * l - f

        def ends():
            low_buf[c, 0:EDGE] = jnp.where(walk.hide_left(i), 0.0, value(0, EDGE))
            low_buf[c, EDGE + tile : 2 * EDGE + tile] = jnp.where(walk.hide_right(i), 0.0, value(EDGE + tile, EDGE))

        def rows(r):
            def run():
                low_buf[c, EDGE + r : EDGE + r + UNIT] = value(EDGE + r, UNIT)

            return run

        def taps(r):
            def run():
                for tap in range(3):
                    q = EDGE + r + 1 - tap
                    dst[r : r + UNIT, lanes(tap * slabs + c)] = low_buf[c, q : q + UNIT].astype(bf16)

            return run

        units = [ends, rows(0)]
        for r in range(UNIT, tile, UNIT):
            units += [rows(r), taps(r - UNIT)]
        return units + [taps(tile - UNIT)]

    def finish(slot, c):
        at, cols = lanes_of(c), lanes(c)
        m, inv, g, sh = center[:, at], inverse[:, at], gain1[:, at], shift1[:, at]
        sums = [jnp.zeros((8, LANES), f32), jnp.zeros((8, LANES), f32)]

        def rows(r):
            def run():
                normed = (xs[slot, r : r + UNIT, cols] - m) * inv
                incoming = g_buf[c, EDGE + r : EDGE + r + UNIT] + g_buf[c, EDGE + r - 1 : EDGE + r - 1 + UNIT]
                back = gelu_slope(normed * g + sh) * incoming
                outs[slot, r : r + UNIT, cols] = back.astype(bf16)
                sums[0] = sums[0] + folded(back * normed)
                sums[1] = sums[1] + folded(back)

            return run

        def close():
            stats[0, :, cols] += sums[0]
            stats[1, :, cols] += sums[1]

        return [rows(r) for r in range(0, span, UNIT)] + [close]

    load(0, 0)
    wait_load(0)
    w_copy = pltpu.make_async_copy(w_hbm, w_ref, w_sem)
    w_copy.start()
    for copy in late_copies(0, 0):
        copy.start()
    f_copy = pltpu.make_async_copy(first, firsts, f_sem)
    f_copy.start()
    load(1, 1)
    total[...] = jnp.zeros_like(total)
    for c in range(slabs):
        for unit in lower(0, 0, c):
            unit()
    w_copy.wait()
    f_copy.wait()

    def pair(j, _):
        for slot in range(2):
            i = 2 * j + slot
            other = 1 - slot
            w, p = walk.where(i)

            @pl.when(p == 0)
            def _():
                edge = low[slot][0:16, channels : 2 * channels]
                row = lax.broadcasted_iota(jnp.int32, (16, channels), 0)
                keep = jnp.logical_and(row == 0, walk.at_start)
                here = jnp.where(keep, firsts[w].astype(f32), 0.0).astype(bf16)
                total[1] += dot(here, edge, TN)
                part = dot(edge, w_ref[1], NT) + dot(low[slot][0:16, 2 * channels :], w_ref[3], NT)
                for c in range(slabs):
                    g_buf[c, EDGE + span - 1 : EDGE + span] = part[0:1, lanes_of(c)]

            @pl.when(i + 1 < tiles)
            def _():
                wait_load(other)
                for copy in late_copies(i + 1, other):
                    copy.start()

            @pl.when(i + 2 < tiles)
            def _():
                load(i + 2, slot)

            @pl.when(i >= 2)
            def _():
                o_copy(i - 2, slot).wait()

            for c in range(slabs):
                g_buf[c, 0:EDGE] = g_buf[c, span : span + EDGE]

            def spread(n):
                at = lanes(n, 256)

                def even():
                    part = dot(low[slot][:, 0:channels], w_ref[0, at], NT)
                    part += dot(low[slot][:, channels : 2 * channels], w_ref[2, at], NT)
                    part += dot(low[slot][:, 2 * channels : 3 * channels], w_ref[4, at], NT)
                    for c in range(2):
                        g_buf[2 * n + c, pl.ds(EDGE, tile, stride=2)] = part[:, lanes_of(c)]

                def odd():
                    part = dot(low[slot][:, 0:channels], w_ref[1, at], NT)
                    part += dot(low[slot][:, channels : 2 * channels], w_ref[3, at], NT)
                    for c in range(2):
                        g_buf[2 * n + c, pl.ds(EDGE + 1, tile, stride=2)] = part[:, lanes_of(c)]

                return [even, odd]

            for n in range(channels // 256):
                units = lower(i + 1, other, 2 * n) + lower(i + 1, other, 2 * n + 1)
                interleave(spread(n), units)

            for copy in late_copies(i, slot):
                copy.wait()

            for n in range(channels // 256):
                cols = lanes(n, 256)

                def weigh(k):
                    def run():
                        at = (k // 2) * channels + n * 256
                        total[k, :, cols] += dot(ss[slot, k % 2], low[slot][:, at : at + 256], TN)

                    return run

                interleave([weigh(k) for k in range(5)], finish(slot, 2 * n) + finish(slot, 2 * n + 1))
            o_copy(i, slot).start()

        return 0

    lax.fori_loop(0, tiles // 2, pair, 0)
    w_ref[...] = total[...].astype(bf16)
    g_copy = pltpu.make_async_copy(w_ref, w_grad, g_sem)
    g_copy.start()
    o_copy(tiles - 2, 0).wait()
    o_copy(tiles - 1, 1).wait()
    g_copy.wait()


def conv_one_back(
    da, da_sides, v, v_sides, ct, ct_sides, sums2, grads2, gain2, x, sums1, gain1, shift1, s, first, weight, entries
):
    windows, length, channels = da.shape
    tile = min(512, length)
    slabs = channels // LANES
    return pl.pallas_call(
        functools.partial(conv_one_back_kernel, tile, entries),
        out_shape=(
            jax.ShapeDtypeStruct((windows, 2 * length, channels), bf16),
            jax.ShapeDtypeStruct((2, 8, channels), f32),
            jax.ShapeDtypeStruct(weight.shape, bf16),
        ),
        in_specs=[ANY] * 9 + [VM] * 3 + [ANY] + [VM] * 3 + [ANY] * 3,
        out_specs=(ANY, VM, ANY),
        scratch_shapes=[
            pltpu.VMEM((2, tile + 2 * EDGE, channels), f32),
            pltpu.VMEM((2, tile + 2 * EDGE, channels), f32),
            pltpu.VMEM((2, tile + 2 * EDGE, channels), f32),
            pltpu.VMEM((2, 2, tile, channels), bf16),
            pltpu.VMEM((2, 2 * tile, channels), f32),
            pltpu.VMEM(first.shape, bf16),
            pltpu.VMEM((slabs, tile + 2 * EDGE, LANES), f32),
            pltpu.VMEM((tile, 3 * channels), bf16),
            pltpu.VMEM((tile, 3 * channels), bf16),
            pltpu.VMEM((slabs, 2 * tile + 2 * EDGE, LANES), f32),
            pltpu.VMEM((2, 2 * tile, channels), bf16),
            pltpu.VMEM(weight.shape, f32),
            pltpu.VMEM(weight.shape, bf16),
            DMA((2,)),
            DMA((2,)),
            DMA((2,)),
            DMA((2,)),
            DMA((2,)),
            DMA,
            DMA((2,)),
            DMA,
            DMA,
        ],
        name="conv_one_back",
        **params(20 * da.size * channels, 8 * x.size, x.size),
    )(da, *da_sides, v, *v_sides, ct, *ct_sides, sums2, grads2, gain2, x, sums1, gain1, shift1, s, first, weight)


def last_kernel(entries, x, da, sums, grads, gain, out):
    center, inverse = center_inverse(sums[...], entries)
    both = grads[...]
    scale = inverse * gain[...]
    lean = scale * inverse * (both[0:1] / entries)
    flat = scale * (both[1:2] / entries)
    for c in range(x.shape[2] // LANES):
        cols, at = lanes(c), lanes_of(c)
        m, s, l, f = center[:, at], scale[:, at], lean[:, at], flat[:, at]
        for r in range(0, x.shape[1], 128):
            rows = slice(r, r + 128)
            out[0, rows, cols] = da[0, rows, cols].astype(f32) * s - (x[0, rows, cols] - m) * l - f


def input_back(x, da, sums, grads, gain, entries):
    windows, length, channels = x.shape
    tile = min(512, length)
    per = length // tile
    rows = pl.BlockSpec((1, tile, channels), lambda i: (i // per, i % per, 0))
    whole = lambda i: (0, 0)
    return pl.pallas_call(
        functools.partial(last_kernel, entries),
        grid=(windows * per,),
        out_shape=jax.ShapeDtypeStruct(x.shape, f32),
        in_specs=[
            rows,
            rows,
            pl.BlockSpec((8, channels), whole),
            pl.BlockSpec((8, channels), whole),
            pl.BlockSpec((1, channels), whole),
        ],
        out_specs=rows,
        name="input_back",
        **params(moved=10 * x.size),
    )(x, da, sums, grads, gain)


def on_device(
    inputs,
    conv_one,
    conv_two,
    conv_three,
    gain_one,
    shift_one,
    gain_two,
    shift_two,
    gain_three,
    shift_three,
    cotangent,
):
    windows, length, channels = inputs.shape
    entries = float(windows * length * lax.axis_size("dp") * lax.axis_size("seq"))
    half = entries / 2
    gain_one, shift_one, gain_two, shift_two, gain_three, shift_three = (
        v.reshape(1, -1) for v in (gain_one, shift_one, gain_two, shift_two, gain_three, shift_three)
    )
    sums1, (x_left, x_right, c_left, c_right) = exchange(input_sums(inputs), [inputs, cotangent], 0)
    pooled, s, first, stats = conv_one_forward(
        inputs, x_left, x_right, sums1, gain_one, shift_one, conv_one, entries
    )
    sums2, p_sides = exchange(stats, [pooled], 1)
    narrow, hidden_two, stats = conv_two_forward(pooled, *p_sides, sums2, gain_two, shift_two, conv_two, half)
    sums3, n_sides = exchange(stats, [narrow], 2)
    outputs, da3, stats, three_grad = conv_three_both(
        narrow, cotangent, pooled, sums3, gain_three, shift_three, conv_three, half
    )
    grads3, a_sides = exchange(stats, [da3], 3)
    da2, stats, two_grad = conv_two_back(
        da3, a_sides, narrow, n_sides, sums3, grads3, gain_three, pooled, sums2, gain_two, shift_two,
        hidden_two, conv_two, half,
    )
    grads2, b_sides = exchange(stats, [da2], 4)
    da1, stats, one_grad = conv_one_back(
        da2, b_sides, pooled, p_sides, cotangent, (c_left, c_right), sums2, grads2, gain_two,
        inputs, sums1, gain_one, shift_one, s, first, conv_one, entries,
    )
    grads1, _ = exchange(stats, [], 5)
    input_grad = input_back(inputs, da1, sums1, grads1, gain_one, entries)
    two_grad, three_grad = lax.psum((two_grad, three_grad), ("dp", "seq"))
    one_grad = lax.psum(one_grad, ("dp", "seq"))
    return (
        outputs,
        input_grad,
        one_grad.astype(f32),
        two_grad.astype(f32),
        three_grad.astype(f32),
        grads1[0],
        grads1[1],
        grads2[0],
        grads2[1],
        grads3[0],
        grads3[1],
    )


def solution(mesh):
    rows = P("dp", "seq", None)
    in_specs = (rows,) + (P(),) * 9 + (rows,)
    out_specs = (rows, rows) + (P(),) * 9
    return jax.shard_map(on_device, mesh=mesh, in_specs=in_specs, out_specs=out_specs, check_vma=False)
```

time: 1020 us -> 508 us (0.50)
  matrix products: 421 us -> 0 us
  Pallas kernels: 0 us -> 332 us
  blocking collectives: 244 us -> 0 us
  local copies, waits for them, and re-layouts: 119 us -> 10.4 us
  other arithmetic: 96.6 us -> 11.4 us
  waiting for transfers between devices: 96.5 us -> 138 us
  starting transfers between devices: 15.1 us -> 0.04 us
    dot_general x27 -> x0, matrix products: 421 us -> none  [the longest x8 166 us: conv_input_grad(): jnp.einsum('wtd,cd->wtc', padded_grad[:, start:start + length], weight[ta...]
    pallas_call x0 -> x13, Pallas kernels: none -> 332 us  [the longest x1 104 us: conv_one_back(): pl.pallas_call(functools.partial(conv_one_back_kernel, tile, entries), ou...]
    psum x6 -> x0, blocking collectives: 244 us -> none  [the longest x3 122 us: batch_norm(): lax.psum((jnp.sum(values, axis=(0, 1)), jnp.sum(values * values, axis=(0,...]
    reshape x2 -> x6, local copies, waits for them, and re-layouts: 55.3 us -> 7.56 us  [on_device(): v.reshape(1, -1)]
    psum x1, waiting for transfers between devices: 96.4 us -> 138 us  [on_device(): one_grad = lax.psum(one_grad, ('dp', 'seq'))]
    convert_element_type x4 -> x3, other arithmetic: 42.9 us -> 11.4 us  [the longest x1 5.61 us: on_device(): one_grad.astype(f32)]
    unnamed x94 -> x2, local copies, waits for them, and re-layouts: 29.1 us -> 0.01 us
    mul x4 -> x0, other arithmetic: 27.8 us -> none  [norm_back(): inverse * gain]
  transfers between devices with their start and end apart: 9 -> 1, of which waited for: 1 -> 1; matrix products, arithmetic and copies ran while one was open for 29% -> 1% of each run, Pallas kernels for 0% -> 8%
where the time goes in v1:
time: 508 us; the launch traced here: 506 us
  Pallas kernels  332 us (65%)
  waiting for transfers between devices  138 us (27%)
  between operations  14.4 us (3%)
  other arithmetic  11.4 us (2%)
  local copies, waits for them, and re-layouts  10.4 us (2%)
    psum x1, waiting for transfers between devices, on_device(): one_grad = lax.psum(one_grad, ('dp', 'seq'))  138 us
    pallas_call x1, Pallas kernels, conv_one_back(): pl.pallas_call(functools.partial(conv_one_back_kernel, tile, entries), ou...  104 us
    pallas_call x6, Pallas kernels, exchange(): pl.pallas_call(functools.partial(exchange_kernel, len(arrays), seqs, dps)...  70.5 us
    pallas_call x1, Pallas kernels, conv_one_forward(): pl.pallas_call(functools.partial(conv_one_kernel, tile, entries), out_sha...  42.5 us
    pallas_call x1, Pallas kernels, conv_two_back(): pl.pallas_call(functools.partial(conv_two_back_kernel, tile, entries), ou...  30.5 us
    pallas_call x1, Pallas kernels, input_back(): pl.pallas_call(functools.partial(last_kernel, entries), grid=(windows * p...  26.6 us
    pallas_call x1, Pallas kernels, conv_three_both(): pl.pallas_call(functools.partial(conv_three_kernel, entries), grid=(windo...  23.9 us
    pallas_call x1, Pallas kernels, conv_two_forward(): pl.pallas_call(functools.partial(conv_two_kernel, tile, entries), out_sha...  22.7 us
  transfers between devices with their start and end apart: 1, of which 1 were waited for; matrix products, arithmetic and copies ran while one was open for 1% of the time, Pallas kernels for 8%

profile of v1, /device:TPU:0, one launch (start us, length us, event | category | flops | bytes accessed | tf_op | source)
XLA Modules:
  0.0 505.8 jit_solution(12797835770297833239)
XLA Ops:
  7.2 1.2 reshape.52.gain.gain3
  9.7 1.3 reshape.46.gain.gain1
  11.0 1.3 reshape.49.gain.gain2
  12.2 1.3 reshape.47.shift.shift1
  13.5 1.3 reshape.50.shift.shift2
  14.8 11.2 %input_sums.1.refs_0_ = f32[2,8,768]{2,1,0:T(8,128)} custom-call(f32[2,4096,768]{2,1,0:T(8,128)} %x.7), custom_call_target="tpu_custom_call" | custom-call | bytes 25165824 | tf_op jit(solution)/shard_map/input_sums/pallas_call | solution.py:297
  26.0 13.1 %exchange_0.1 = (f32[8,768]{1,0:T(8,128)}, f32[2,8,768]{2,1,0:T(8,128)}, f32[2,8,768]{2,1,0:T(8,128)}, f32[2,8,768]{2,1,0:T(8,128)}, f32[2,8,768]{2,1,0:T(8,128)}) custom-call(f32[2,8,768]{2,1,0:T(8,128)} %input_sums.1.refs_0_, f32[2,4096,768]{2,1,0:T(8,128)} %x.7, f32[2,2048,768]{2,1,0:T(8,128)} %ct.1), custom_call_target="tpu_custom_call" | custom-call | tf_op jit(solution)/shard_map/exchange_0/pallas_call | solution.py:253
  39.1 42.5 %conv_one_forward.1 = (f32[2,2048,768]{2,1,0:T(8,128)}, bf16[2,2,2048,768]{3,2,1,0:T(8,128)(2,1)}, bf16[2,16,768]{2,1,0:T(8,128)(2,1)}, f32[2,8,768]{2,1,0:T(8,128)}) custom-call(f32[2,4096,768]{2,1,0:T(8,128)} %x.7, f32[2,8,768]{2,1,0:T(8,128)} %get-tuple-element.45.left, f32[2,8,768]{2,1,0:T(8,128)} %get-tuple-element.46.right, ...), custom_call_target="tpu_custom_call" | custom-call | flops 24159191040 | bytes 50331648 | tf_op jit(solution)/shard_map/conv_one_forward/pallas_call | solution.py:486
  81.7 11.8 %exchange_1.1 = (f32[8,768]{1,0:T(8,128)}, f32[2,8,768]{2,1,0:T(8,128)}, f32[2,8,768]{2,1,0:T(8,128)}) custom-call(f32[2,8,768]{2,1,0:T(8,128)} %get-tuple-element.49.refs_0_, f32[2,2048,768]{2,1,0:T(8,128)} %get-tuple-element.48.refs_1_.v.pooled), custom_call_target="tpu_custom_call" | custom-call | tf_op jit(solution)/shard_map/exchange_1/pallas_call | solution.py:253
  93.5 22.7 %conv_two_forward.1 = (f32[2,2048,384]{2,1,0:T(8,128)}, bf16[2,2048,768]{2,1,0:T(8,128)(2,1)}, f32[2,8,384]{2,1,0:T(8,128)}) custom-call(f32[2,2048,768]{2,1,0:T(8,128)} %get-tuple-element.48.refs_1_.v.pooled, f32[2,8,768]{2,1,0:T(8,128)} %get-tuple-element.50.left.v_left, f32[2,8,768]{2,1,0:T(8,128)} %get-tuple-element.51.right.v_right, ...), custom_call_target="tpu_custom_call" | custom-call | flops 7247757312 | bytes 25165824 | tf_op jit(solution)/shard_map/conv_two_forward/pallas_call | solution.py:641
  116.1 10.9 %exchange_2.1 = (f32[8,384]{1,0:T(8,128)}, f32[2,8,384]{2,1,0:T(8,128)}, f32[2,8,384]{2,1,0:T(8,128)}) custom-call(f32[2,8,384]{2,1,0:T(8,128)} %get-tuple-element.54.refs_0_, f32[2,2048,384]{2,1,0:T(8,128)} %get-tuple-element.53.refs_1_.narrow.v), custom_call_target="tpu_custom_call" | custom-call | tf_op jit(solution)/shard_map/exchange_2/pallas_call | solution.py:253
  127.0 23.9 %conv_three_both.1 = (f32[2,2048,768]{2,1,0:T(8,128)}, f32[2,2048,384]{2,1,0:T(8,128)}, f32[2,8,384]{2,1,0:T(8,128)}, bf16[384,768]{1,0:T(8,128)(2,1)}) custom-call(f32[2,2048,384]{2,1,0:T(8,128)} %get-tuple-element.53.refs_1_.narrow.v, f32[2,2048,768]{2,1,0:T(8,128)} %ct.1, f32[2,2048,768]{2,1,0:T(8,128)} %get-tuple-element.48.refs_1_.v.pooled, ...), custom_call_target="tpu_custom_call" | custom-call | flops 7247757312 | bytes 37748736 | tf_op jit(solution)/shard_map/conv_three_both/pallas_call | solution.py:713
  150.9 10.5 %exchange_3.1 = (f32[8,384]{1,0:T(8,128)}, f32[2,8,384]{2,1,0:T(8,128)}, f32[2,8,384]{2,1,0:T(8,128)}) custom-call(f32[2,8,384]{2,1,0:T(8,128)} %get-tuple-element.58.refs_0_, f32[2,2048,384]{2,1,0:T(8,128)} %get-tuple-element.57.refs_1_.da), custom_call_target="tpu_custom_call" | custom-call | tf_op jit(solution)/shard_map/exchange_3/pallas_call | solution.py:253
  161.5 30.5 %conv_two_back.1 = (f32[2,2048,768]{2,1,0:T(8,128)}, f32[2,8,768]{2,1,0:T(8,128)}, bf16[3,768,384]{2,1,0:T(8,128)(2,1)}) custom-call(f32[2,2048,384]{2,1,0:T(8,128)} %get-tuple-element.57.refs_1_.da, f32[2,8,384]{2,1,0:T(8,128)} %get-tuple-element.59.da_left, f32[2,8,384]{2,1,0:T(8,128)} %get-tuple-element.60.da_right, ...), custom_call_target="tpu_custom_call" | custom-call | flops 14495514624 | bytes 50331648 | tf_op jit(solution)/shard_map/conv_two_back/pallas_call | solution.py:914
  191.9 11.3 %exchange_4.1 = (f32[8,768]{1,0:T(8,128)}, f32[2,8,768]{2,1,0:T(8,128)}, f32[2,8,768]{2,1,0:T(8,128)}) custom-call(f32[2,8,768]{2,1,0:T(8,128)} %get-tuple-element.66.refs_0_, f32[2,2048,768]{2,1,0:T(8,128)} %get-tuple-element.65.refs_1_.da), custom_call_target="tpu_custom_call" | custom-call | tf_op jit(solution)/shard_map/exchange_4/pallas_call | solution.py:253
  203.3 104.0 %conv_one_back.1 = (bf16[2,4096,768]{2,1,0:T(8,128)(2,1)}, f32[2,8,768]{2,1,0:T(8,128)}, bf16[5,768,768]{2,1,0:T(8,128)(2,1)}) custom-call(f32[2,2048,768]{2,1,0:T(8,128)} %get-tuple-element.65.refs_1_.da, f32[2,8,768]{2,1,0:T(8,128)} %get-tuple-element.67.da_left, f32[2,8,768]{2,1,0:T(8,128)} %get-tuple-element.68.da_right, ...), custom_call_target="tpu_custom_call" | custom-call | flops 48318382080 | bytes 50331648 | tf_op jit(solution)/shard_map/conv_one_back/pallas_call | solution.py:1149
  307.3 12.8 %exchange_5.1.grads = f32[8,768]{1,0:T(8,128)} custom-call(f32[2,8,768]{2,1,0:T(8,128)} %get-tuple-element.75.refs_0_), custom_call_target="tpu_custom_call" | custom-call | tf_op jit(solution)/shard_map/exchange_5/pallas_call | solution.py:253
  320.2 26.6 %input_back.1 = f32[2,4096,768]{2,1,0:T(8,128)} custom-call(f32[2,4096,768]{2,1,0:T(8,128)} %x.7, bf16[2,4096,768]{2,1,0:T(8,128)(2,1)} %get-tuple-element.74.da, f32[8,768]{1,0:T(8,128)} %get-tuple-element.47.sums.sums1, f32[8,768]{1,0:T(8,128)} %exchange_5.1.grads, f32[1,768]{1,0:T(1,128)} %reshape.46.gain.gain1), custom_call_target="tpu_custom_call" | custom-call | bytes 62914560 | tf_op jit(solution)/shard_map/input_back/pallas_call | solution.py:1207
  346.8 1.4 slice_reduce_fusion.4
  348.2 1.5 slice_reduce_fusion
  349.7 137.6 %all-reduce.3.cloned.1.call-done = (bf16[5,768,768]{2,1,0:T(8,128)(2,1)}, bf16[3,768,384]{2,1,0:T(8,128)(2,1)}, bf16[384,768]{1,0:T(8,128)(2,1)}) async-done(((bf16[5,768,768]{2,1,0:T(8,128)(2,1)}, bf16[3,768,384]{2,1,0:T(8,128)(2,1)}, bf16[384,768]{1,0:T(8,128)(2,1)}), (bf16[5,768,768]{2,1,0:T(8,128)(2,1)}, bf16[3,768,384]{2,1,0:T(8,128)(2,1)}, bf16[384,768]{1,0:T(8,128)(2,1)})) %all-reduce.3.cloned.1.call-update) | async-done | bytes 8257552 | tf_op jit(solution)/shard_map/psum | solution.py:1266
  487.3 2.3 convert_element_type.11
  489.6 3.5 convert_element_type.10
  493.1 5.6 %convert_element_type.9 = f32[5,768,768]{2,1,0:T(8,128)} convert(bf16[5,768,768]{2,1,0:T(8,128)(2,1)S(1)} %copy-done) | non-fusion elementwise | flops 2949120 | bytes 17694720 | tf_op jit(solution)/shard_map/convert_element_type | solution.py:1270
  (5 shorter events, 1.3 us)
Async XLA Ops:
  7.2 480.1 %all-reduce.3.cloned.1.call-start = ((), (), s32[]{:S(2)}) async-start(), calls=%async_computation | async-start | bytes 16515072 | tf_op jit(solution)/shard_map/psum | solution.py:1266
  487.3 5.8 %copy-start = (bf16[5,768,768]{2,1,0:T(8,128)(2,1)S(1)}, bf16[5,768,768]{2,1,0:T(8,128)(2,1)}, u32[]{:S(2)}) copy-start(bf16[5,768,768]{2,1,0:T(8,128)(2,1)} %get-tuple-element.85) | copy-start | bytes 17694724
Sparse Core Ops, SparseCore 0:
  307.5 179.7 all-reduce.2

commit v2 on v1

--- a/solution.py
+++ b/solution.py
@@ -18,6 +18,7 @@
 LINEAR = 0.7978845608028654
 CUBIC = 0.7978845608028654 * 0.044715
 VMEM_LIMIT = 60 << 20
+EARLY = 3
 NN = (((1,), (0,)), ((), ()))
 NT = (((1,), (1,)), ((), ()))
 TN = (((0,), (0,)), ((), ()))
@@ -49,6 +50,10 @@
 def center_inverse(sums, entries):
     center = sums[0:1] / entries
     return center, lax.rsqrt(sums[1:2] / entries - center * center + epsilon)
+
+
+def flat_row(v):
+    return v[...].reshape(1, v.shape[0])
 
 
 def lanes(c, width=LANES):
@@ -316,8 +321,8 @@
     tiles = walk.count
     lhs = (lhs_a, lhs_b)
     center, inverse = center_inverse(sums[...], entries)
-    scale = inverse * gain[...]
-    offset = shift[...] - center * scale
+    scale = inverse * flat_row(gain)
+    offset = flat_row(shift) - center * scale
     for c in range(slabs):
         coef[c, 0:1] = scale[:, lanes_of(c)]
         coef[c, 1:2] = offset[:, lanes_of(c)]
@@ -522,8 +527,8 @@
     tiles = walk.count
     lhs = (lhs_a, lhs_b)
     center, inverse = center_inverse(sums[...], entries)
-    scale = inverse * gain[...]
-    offset = shift[...] - center * scale
+    scale = inverse * flat_row(gain)
+    offset = flat_row(shift) - center * scale
     stats[...] = jnp.zeros_like(stats)
 
     def load(i, slot):
@@ -682,7 +687,7 @@
     for c in range(narrow.shape[2] // LANES):
         cols = lanes(c)
         at = lanes_of(c)
-        m, inv, g, s = center[:, at], inverse[:, at], gain[:, at], shift[:, at]
+        m, inv, g, s = center[:, at], inverse[:, at], gain[at][None], shift[at][None]
         gains = jnp.zeros((8, LANES), f32)
         shifts = jnp.zeros((8, LANES), f32)
         for r in range(0, tile, UNIT):
@@ -700,7 +705,8 @@
 
     @pl.when(step == pl.num_programs(0) - 1)
     def _():
-        w_grad[...] = total[...].astype(bf16)
+        for c in range(total.shape[1] // LANES):
+            w_grad[c] = total[:, lanes_of(c)].astype(bf16)
 
 
 def conv_three_both(narrow, cotangent, pooled, sums, gain, shift, weight, entries):
@@ -717,22 +723,22 @@
             jax.ShapeDtypeStruct((windows, length, channels), f32),
             jax.ShapeDtypeStruct((windows, length, width), f32),
             jax.ShapeDtypeStruct((2, 8, width), f32),
-            jax.ShapeDtypeStruct((width, channels), bf16),
+            jax.ShapeDtypeStruct((channels // LANES, width, LANES), bf16),
         ),
         in_specs=[
             pl.BlockSpec((1, tile, width), rows),
             pl.BlockSpec((1, tile, channels), rows),
             pl.BlockSpec((1, tile, channels), rows),
             pl.BlockSpec((8, width), whole),
-            pl.BlockSpec((1, width), whole),
-            pl.BlockSpec((1, width), whole),
+            pl.BlockSpec((width,), lambda i: (0,)),
+            pl.BlockSpec((width,), lambda i: (0,)),
             pl.BlockSpec((width, channels), whole),
         ],
         out_specs=(
             pl.BlockSpec((1, tile, channels), rows),
             pl.BlockSpec((1, tile, width), rows),
             pl.BlockSpec((2, 8, width), lambda i: (0, 0, 0)),
-            pl.BlockSpec((width, channels), whole),
+            pl.BlockSpec((channels // LANES, width, LANES), lambda i: (0, 0, 0)),
         ),
         scratch_shapes=[
             pltpu.VMEM((tile, channels), bf16),
@@ -759,7 +765,7 @@
     low = (low_a, low_b)
     center3, inverse3 = center_inverse(sums3[...], entries)
     grads = grads3[...]
-    scale3 = inverse3 * gain3[...]
+    scale3 = inverse3 * flat_row(gain3)
     lean = scale3 * inverse3 * (grads[0:1] / entries)
     flat = scale3 * (grads[1:2] / entries)
     center, inverse = center_inverse(sums2[...], entries)
@@ -818,7 +824,7 @@
 
     def finish(slot, c):
         at, cols = lanes_of(c), lanes(c)
-        m, inv, g, s = center[:, at], inverse[:, at], gain2[:, at], shift2[:, at]
+        m, inv, g, s = center[:, at], inverse[:, at], gain2[at][None], shift2[at][None]
         sums = [jnp.zeros((8, LANES), f32), jnp.zeros((8, LANES), f32)]
 
         def rows(r):
@@ -900,8 +906,8 @@
         return 0
 
     lax.fori_loop(0, tiles // 2, pair, 0)
-    for k in range(3):
-        w_grad[k] = total[:, k * width : (k + 1) * width].astype(bf16)
+    for c in range(3 * thin):
+        w_grad[c] = total[:, lanes_of(c)].astype(bf16)
     o_copy(tiles - 2, 0).wait()
     o_copy(tiles - 1, 1).wait()
 
@@ -916,7 +922,7 @@
         out_shape=(
             jax.ShapeDtypeStruct((windows, length, channels), f32),
             jax.ShapeDtypeStruct((2, 8, channels), f32),
-            jax.ShapeDtypeStruct(weight.shape, bf16),
+            jax.ShapeDtypeStruct((3 * thin, channels, LANES), bf16),
         ),
         in_specs=[ANY] * 6 + [VM] * 3 + [ANY] + [VM] * 3 + [ANY] * 2,
         out_specs=(ANY, VM, VM),
@@ -945,26 +951,152 @@
     )(da, *da_sides, v, *v_sides, sums3, grads3, gain3, pooled, sums2, gain2, shift2, h, weight)
 
 
-def conv_one_back_kernel(
-    tile, entries, da, da_left, da_right, v, v_left, v_right, ct, ct_left, ct_right, sums2, grads2, gain2,
-    x, sums1, gain1, shift1, s, first, w_hbm, da_out, stats, w_grad,
-    das, vs, cts, ss, xs, firsts, low_buf, low_a, low_b, g_buf, outs, total, w_ref,
-    a_sem, v_sem, c_sem, s_sem, x_sem, f_sem, o_sem, w_sem, g_sem,
+class Reduction:
+    STAGES = 8
+    LAG = 3
+
+    def __init__(self, data, done, lands, send, recv):
+        self.data, self.done, self.lands, self.send, self.recv = data, done, lands, send, recv
+        self.chunks, self.rows = data.shape[0], data.shape[1]
+        self.steps = self.chunks + self.LAG * self.STAGES
+        self.planes = lax.axis_size("dp") // 4
+        seq, dp = lax.axis_index("seq"), lax.axis_index("dp")
+        self.seq, self.dp = seq, dp
+        one, two = dp % 2, (dp // 2) % 2
+        swap = seq == 1
+        first_bit, second_bit = jnp.where(swap, two, one), jnp.where(swap, one, two)
+        to_one, to_two = dp + 1 - 2 * one, dp + 2 - 4 * two
+        first_peer, second_peer = jnp.where(swap, to_two, to_one), jnp.where(swap, to_one, to_two)
+        self.peers = ({"seq": 1 - seq}, {"dp": first_peer}, {"dp": second_peer})
+        self.plane = dp // 4
+        rows = self.rows
+        self.size = [rows // 2, rows // 4, rows // 8, rows // 8 // self.planes]
+        self.base = [seq * self.size[0]]
+        self.away = [(1 - seq) * self.size[0]]
+        for bit, size in ((first_bit, self.size[1]), (second_bit, self.size[2])):
+            self.away.append(self.base[-1] + (1 - bit) * size)
+            self.base.append(self.base[-1] + bit * size)
+
+    def part(self, ref, c, start, size):
+        return ref.at[c, pl.ds(pl.multiple_of(start, 16), size)]
+
+    def copy(self, c, number, src, dst, peer):
+        return pltpu.make_async_remote_copy(
+            src_ref=src, dst_ref=dst, send_sem=self.send.at[c, number], recv_sem=self.recv.at[c, number],
+            device_id=peer, device_id_type=MESH,
+        )
+
+    def copies(self, c, stage):
+        size, base = self.size, self.base
+        if stage < 3:
+            src = self.part(self.data, c, self.away[stage], size[stage])
+            return [self.copy(c, stage, src, self.lands[stage].at[c], self.peers[stage])]
+        if stage == 3 or stage == 4:
+            out = []
+            for d in range(1, self.planes):
+                there = (self.plane + d) % self.planes
+                peer = {"dp": self.dp + (there - self.plane) * 4}
+                if stage == 3:
+                    src = self.part(self.data, c, base[2] + there * size[3], size[3])
+                    dst = self.lands[3].at[c, d - 1]
+                else:
+                    src = dst = self.part(self.done, c, base[2] + self.plane * size[3], size[3])
+                out.append(self.copy(c, 3 + (stage - 3) * (self.planes - 1) + d - 1, src, dst, peer))
+            return out
+        level = 7 - stage
+        mine = self.part(self.done, c, base[level], size[level])
+        return [self.copy(c, 2 * (self.planes - 1) + stage - 2, mine, mine, self.peers[level])]
+
+    def launch(self, c, stage):
+        for copy in self.copies(c, stage):
+            copy.start()
+
+    def arrive(self, c, stage):
+        for copy in self.copies(c, stage):
+            copy.wait()
+        size, base = self.size, self.base
+        if stage < 3:
+            unit = self.rows // 8
+
+            def add(r, _):
+                at = pl.ds(pl.multiple_of(base[stage] + r * unit, 16), unit)
+                got = self.lands[stage][c, pl.ds(pl.multiple_of(r * unit, 16), unit)].astype(f32)
+                self.data[c, at] = (self.data[c, at].astype(f32) + got).astype(bf16)
+                return 0
+
+            lax.fori_loop(0, size[stage] // unit, add, 0)
+        elif stage == 3:
+            at = pl.ds(pl.multiple_of(base[2] + self.plane * size[3], 16), size[3])
+            total = self.data[c, at].astype(f32)
+            for d in range(1, self.planes):
+                total += self.lands[3][c, d - 1].astype(f32)
+            self.done[c, at] = total.astype(bf16)
+
+    def step(self, t):
+        for stage in range(self.STAGES, -1, -1):
+            c = t - self.LAG * stage
+
+            @pl.when(jnp.logical_and(c >= 0, c < self.chunks))
+            def _():
+                if stage > 0:
+                    self.arrive(c, stage - 1)
+                if stage < self.STAGES:
+                    self.launch(c, stage)
+
+    @staticmethod
+    def fits(rows):
+        dps = lax.axis_size("dp")
+        return lax.axis_size("seq") == 2 and dps % 4 == 0 and dps > 4 and rows % (128 * (dps // 4)) == 0
+
+    @staticmethod
+    def scratch(chunks, rows):
+        planes = lax.axis_size("dp") // 4
+        copies = 2 * (planes - 1) + 6
+        shapes = [(chunks, rows, LANES)] + [(chunks, rows >> (n + 1), LANES) for n in range(3)]
+        shapes += [(chunks, planes - 1, rows // 8 // planes, LANES)]
+        return [pltpu.VMEM(shape, bf16) for shape in shapes] + [DMA((chunks, copies)), DMA((chunks, copies))]
+
+    @staticmethod
+    def of(data, refs):
+        return Reduction(data, refs[0], refs[1:5], refs[5], refs[6])
+
+
+def greet(seqs, dps):
+    seq, dp = lax.axis_index("seq"), lax.axis_index("dp")
+    barrier = pltpu.get_barrier_semaphore()
+
+    def near(d, _):
+        pl.semaphore_signal(barrier, inc=1, device_id={"seq": lax.rem(seq + d, seqs)}, device_id_type=MESH)
+        return 0
+
+    def far(d, _):
+        pl.semaphore_signal(barrier, inc=1, device_id={"dp": lax.rem(dp + d, dps)}, device_id_type=MESH)
+        return 0
+
+    lax.fori_loop(1, seqs, near, 0)
+    lax.fori_loop(1, dps, far, 0)
+    pl.semaphore_wait(barrier, seqs - 1 + dps - 1)
+
+
+def conv_one_weigh_kernel(
+    tile, entries, joined, seqs, dps, da, da_left, da_right, v, v_left, v_right, ct, ct_left, ct_right, sums2, grads2,
+    gain2, s, first, two, three, low_out, w_grad, small, das, vs, cts, ss, firsts, low_buf, low_a, low_b, coef, total,
+    packed, data, a_sem, v_sem, c_sem, s_sem, f_sem, l_sem, g_sem, d_sem, *reduction,
 ):
     windows, length, channels = da.shape
     slabs = channels // LANES
-    span = 2 * tile
     walk = Walk(windows, length, tile)
     tiles = walk.count
     low = (low_a, low_b)
     half_entries = entries / 2
     center2, inverse2 = center_inverse(sums2[...], half_entries)
     grads = grads2[...]
-    scale2 = 0.5 * inverse2 * gain2[...]
+    scale2 = 0.5 * inverse2 * flat_row(gain2)
     lean = scale2 * inverse2 * (grads[0:1] / half_entries)
     flat = scale2 * (grads[1:2] / half_entries)
-    center, inverse = center_inverse(sums1[...], entries)
-    stats[...] = jnp.zeros_like(stats)
+    for c in range(slabs):
+        for row, values in enumerate((scale2, lean, center2 * lean - flat)):
+            coef[c, row : row + 1] = values[:, lanes_of(c)]
 
     def load(i, slot):
         walk.fetch(i, da, da_left, da_right, das.at[slot], a_sem.at[slot])
@@ -976,25 +1108,22 @@
         wait_for(vs.at[slot], v_sem.at[slot])
         wait_for(cts.at[slot], c_sem.at[slot])
 
-    def late_copies(i, slot):
+    def s_copy(i, slot):
         w, _ = walk.where(i)
-        return (
-            pltpu.make_async_copy(x.at[w, walk.rows(i, 2)], xs.at[slot], x_sem.at[slot]),
-            pltpu.make_async_copy(s.at[:, w, walk.rows(i)], ss.at[slot], s_sem.at[slot]),
-        )
-
-    def o_copy(i, slot):
+        return pltpu.make_async_copy(s.at[:, w, walk.rows(i)], ss.at[slot], s_sem.at[slot])
+
+    def l_copy(i, slot):
         w, _ = walk.where(i)
-        return pltpu.make_async_copy(outs.at[slot], da_out.at[w, walk.rows(i, 2)], o_sem.at[slot])
+        return pltpu.make_async_copy(low[slot], low_out.at[w, walk.rows(i)], l_sem.at[slot])
 
     def lower(i, slot, c):
-        at, cols = lanes_of(c), lanes(c)
-        m, sc, l, f = center2[:, at], scale2[:, at], lean[:, at], flat[:, at]
+        cols = lanes(c)
+        sc, l, f = coef[c, 0:1], coef[c, 1:2], coef[c, 2:3]
         dst = low[slot]
 
         def value(q, size):
             rows = slice(q, q + size)
-            return 0.5 * cts[slot, rows, cols] + das[slot, rows, cols] * sc - (vs[slot, rows, cols] - m) * l - f
+            return 0.5 * cts[slot, rows, cols] + das[slot, rows, cols] * sc - vs[slot, rows, cols] * l + f
 
         def ends():
             low_buf[c, 0:EDGE] = jnp.where(walk.hide_left(i), 0.0, value(0, EDGE))
@@ -1010,7 +1139,8 @@
             def run():
                 for tap in range(3):
                     q = EDGE + r + 1 - tap
-                    dst[r : r + UNIT, lanes(tap * slabs + c)] = low_buf[c, q : q + UNIT].astype(bf16)
+                    at = pl.ds(pl.multiple_of(tap * channels + c * LANES, LANES), LANES)
+                    dst[r : r + UNIT, at] = low_buf[c, q : q + UNIT].astype(bf16)
 
             return run
 
@@ -1019,43 +1149,33 @@
             units += [rows(r), taps(r - UNIT)]
         return units + [taps(tile - UNIT)]
 
-    def finish(slot, c):
-        at, cols = lanes_of(c), lanes(c)
-        m, inv, g, sh = center[:, at], inverse[:, at], gain1[:, at], shift1[:, at]
-        sums = [jnp.zeros((8, LANES), f32), jnp.zeros((8, LANES), f32)]
-
-        def rows(r):
-            def run():
-                normed = (xs[slot, r : r + UNIT, cols] - m) * inv
-                incoming = g_buf[c, EDGE + r : EDGE + r + UNIT] + g_buf[c, EDGE + r - 1 : EDGE + r - 1 + UNIT]
-                back = gelu_slope(normed * g + sh) * incoming
-                outs[slot, r : r + UNIT, cols] = back.astype(bf16)
-                sums[0] = sums[0] + folded(back * normed)
-                sums[1] = sums[1] + folded(back)
-
-            return run
-
-        def close():
-            stats[0, :, cols] += sums[0]
-            stats[1, :, cols] += sums[1]
-
-        return [rows(r) for r in range(0, span, UNIT)] + [close]
-
     load(0, 0)
     wait_load(0)
-    w_copy = pltpu.make_async_copy(w_hbm, w_ref, w_sem)
-    w_copy.start()
-    for copy in late_copies(0, 0):
-        copy.start()
+    s_copy(0, 0).start()
     f_copy = pltpu.make_async_copy(first, firsts, f_sem)
     f_copy.start()
     load(1, 1)
+    at = 0
+    for src in (two, three):
+        size = src.shape[1]
+        for c in range(src.shape[0]):
+            chunk, start = divmod(at, data.shape[1])
+            pltpu.make_async_copy(src.at[c], data.at[chunk, pl.ds(start, size)], d_sem).start()
+            at += size
+    if joined:
+        greet(seqs, dps)
+        sharing = Reduction.of(data, reduction)
     total[...] = jnp.zeros_like(total)
-    for c in range(slabs):
+
+    def first_slab(c, _):
         for unit in lower(0, 0, c):
             unit()
-    w_copy.wait()
+        return 0
+
+    lax.fori_loop(0, slabs, first_slab, 0)
+    l_copy(0, 0).start()
     f_copy.wait()
+    wait_for(data, d_sem)
 
     def pair(j, _):
         for slot in range(2):
@@ -1063,131 +1183,431 @@
             other = 1 - slot
             w, p = walk.where(i)
 
-            @pl.when(p == 0)
-            def _():
-                edge = low[slot][0:16, channels : 2 * channels]
+            @pl.when(jnp.logical_and(p == 0, walk.at_start))
+            def _():
                 row = lax.broadcasted_iota(jnp.int32, (16, channels), 0)
-                keep = jnp.logical_and(row == 0, walk.at_start)
-                here = jnp.where(keep, firsts[w].astype(f32), 0.0).astype(bf16)
-                total[1] += dot(here, edge, TN)
-                part = dot(edge, w_ref[1], NT) + dot(low[slot][0:16, 2 * channels :], w_ref[3], NT)
-                for c in range(slabs):
-                    g_buf[c, EDGE + span - 1 : EDGE + span] = part[0:1, lanes_of(c)]
+                here = jnp.where(row == 0, firsts[w].astype(f32), 0.0).astype(bf16)
+                total[1] += dot(here, low[slot][0:16, channels : 2 * channels], TN)
 
             @pl.when(i + 1 < tiles)
             def _():
                 wait_load(other)
-                for copy in late_copies(i + 1, other):
-                    copy.start()
+                s_copy(i + 1, other).start()
 
             @pl.when(i + 2 < tiles)
             def _():
                 load(i + 2, slot)
 
-            @pl.when(i >= 2)
-            def _():
-                o_copy(i - 2, slot).wait()
-
-            for c in range(slabs):
-                g_buf[c, 0:EDGE] = g_buf[c, span : span + EDGE]
-
-            def spread(n):
-                at = lanes(n, 256)
-
-                def even():
-                    part = dot(low[slot][:, 0:channels], w_ref[0, at], NT)
-                    part += dot(low[slot][:, channels : 2 * channels], w_ref[2, at], NT)
-                    part += dot(low[slot][:, 2 * channels : 3 * channels], w_ref[4, at], NT)
-                    for c in range(2):
-                        g_buf[2 * n + c, pl.ds(EDGE, tile, stride=2)] = part[:, lanes_of(c)]
-
-                def odd():
-                    part = dot(low[slot][:, 0:channels], w_ref[1, at], NT)
-                    part += dot(low[slot][:, channels : 2 * channels], w_ref[3, at], NT)
-                    for c in range(2):
-                        g_buf[2 * n + c, pl.ds(EDGE + 1, tile, stride=2)] = part[:, lanes_of(c)]
-
-                return [even, odd]
-
-            for n in range(channels // 256):
-                units = lower(i + 1, other, 2 * n) + lower(i + 1, other, 2 * n + 1)
-                interleave(spread(n), units)
-
-            for copy in late_copies(i, slot):
-                copy.wait()
-
-            for n in range(channels // 256):
+            @pl.when(i >= 1)
+            def _():
+                l_copy(i - 1, other).wait()
+
+            s_copy(i, slot).wait()
+
+            def part(n, _):
                 cols = lanes(n, 256)
 
                 def weigh(k):
                     def run():
-                        at = (k // 2) * channels + n * 256
-                        total[k, :, cols] += dot(ss[slot, k % 2], low[slot][:, at : at + 256], TN)
+                        at = pl.ds(pl.multiple_of((k // 2) * channels + n * 256, 256), 256)
+                        total[k, :, cols] += dot(ss[slot, k % 2], low[slot][:, at], TN)
 
                     return run
 
-                interleave([weigh(k) for k in range(5)], finish(slot, 2 * n) + finish(slot, 2 * n + 1))
-            o_copy(i, slot).start()
+                units = lower(i + 1, other, 2 * n) + lower(i + 1, other, 2 * n + 1)
+                interleave([weigh(k) for k in range(EARLY)], units)
+                if joined:
+                    sharing.step(i * (channels // 256) + n)
+                return 0
+
+            lax.fori_loop(0, channels // 256, part, 0)
+
+            @pl.when(i + 1 < tiles)
+            def _():
+                l_copy(i + 1, other).start()
 
         return 0
 
     lax.fori_loop(0, tiles // 2, pair, 0)
-    w_ref[...] = total[...].astype(bf16)
-    g_copy = pltpu.make_async_copy(w_ref, w_grad, g_sem)
+    l_copy(tiles - 1, 1).wait()
+    for k in range(EARLY):
+        for c in range(slabs):
+            packed[k, c] = total[k, :, lanes_of(c)].astype(bf16)
+    g_copy = pltpu.make_async_copy(packed, w_grad, g_sem)
     g_copy.start()
-    o_copy(tiles - 2, 0).wait()
-    o_copy(tiles - 1, 1).wait()
+    if joined:
+        def more(t, _):
+            sharing.step(t)
+            return 0
+
+        lax.fori_loop(tiles * (channels // 256), sharing.steps, more, 0)
+        d_copy = pltpu.make_async_copy(sharing.done, small, d_sem)
+    else:
+        d_copy = pltpu.make_async_copy(data, small, d_sem)
+    d_copy.start()
+    d_copy.wait()
     g_copy.wait()
 
 
-def conv_one_back(
-    da, da_sides, v, v_sides, ct, ct_sides, sums2, grads2, gain2, x, sums1, gain1, shift1, s, first, weight, entries
-):
+def conv_one_weigh(da, da_sides, v, v_sides, ct, ct_sides, sums2, grads2, gain2, s, first, two, three, entries, number):
     windows, length, channels = da.shape
     tile = min(512, length)
     slabs = channels // LANES
-    return pl.pallas_call(
-        functools.partial(conv_one_back_kernel, tile, entries),
+    packed = (EARLY, slabs, channels, LANES)
+    rows = 2 * channels
+    chunks = (two.shape[0] * two.shape[1] + three.shape[0] * three.shape[1]) // rows
+    joined = Reduction.fits(rows)
+    estimate = params(4 * EARLY * da.size * channels, 24 * da.size, 0)
+    if joined:
+        estimate["compiler_params"] = pltpu.CompilerParams(
+            vmem_limit_bytes=VMEM_LIMIT, collective_id=number, has_side_effects=True
+        )
+    low, parts, small = pl.pallas_call(
+        functools.partial(conv_one_weigh_kernel, tile, entries, joined, lax.axis_size("seq"), lax.axis_size("dp")),
         out_shape=(
-            jax.ShapeDtypeStruct((windows, 2 * length, channels), bf16),
-            jax.ShapeDtypeStruct((2, 8, channels), f32),
-            jax.ShapeDtypeStruct(weight.shape, bf16),
+            jax.ShapeDtypeStruct((windows, length, 3 * channels), bf16),
+            jax.ShapeDtypeStruct(packed, bf16),
+            jax.ShapeDtypeStruct((chunks, rows, LANES), bf16),
         ),
-        in_specs=[ANY] * 9 + [VM] * 3 + [ANY] + [VM] * 3 + [ANY] * 3,
-        out_specs=(ANY, VM, ANY),
+        in_specs=[ANY] * 9 + [VM] * 3 + [ANY] * 4,
+        out_specs=(ANY, ANY, ANY),
         scratch_shapes=[
             pltpu.VMEM((2, tile + 2 * EDGE, channels), f32),
             pltpu.VMEM((2, tile + 2 * EDGE, channels), f32),
             pltpu.VMEM((2, tile + 2 * EDGE, channels), f32),
             pltpu.VMEM((2, 2, tile, channels), bf16),
-            pltpu.VMEM((2, 2 * tile, channels), f32),
             pltpu.VMEM(first.shape, bf16),
             pltpu.VMEM((slabs, tile + 2 * EDGE, LANES), f32),
             pltpu.VMEM((tile, 3 * channels), bf16),
             pltpu.VMEM((tile, 3 * channels), bf16),
-            pltpu.VMEM((slabs, 2 * tile + 2 * EDGE, LANES), f32),
+            pltpu.VMEM((slabs, 8, LANES), f32),
+            pltpu.VMEM((EARLY, channels, channels), f32),
+            pltpu.VMEM(packed, bf16),
+            pltpu.VMEM((chunks, rows, LANES), bf16),
+        ]
+        + [DMA((2,))] * 4
+        + [DMA, DMA((2,)), DMA, DMA]
+        + (Reduction.scratch(chunks, rows) if joined else []),
+        name="conv_one_weigh",
+        **estimate,
+    )(da, *da_sides, v, *v_sides, ct, *ct_sides, sums2, grads2, gain2, s, first, two, three)
+    if not joined:
+        small = lax.psum(small, ("dp", "seq"))
+    return low, parts, small
+
+
+def conv_one_spread_kernel(
+    tile, entries, joined, seqs, dps, low, x, sums1, gain1, shift1, w_hbm, s, parts, da_out, stats, w_grad,
+    lows, xs, g_buf, outs, coef, w_ref, total, ss, ls, data, l_sem, x_sem, o_sem, w_sem, d_sem, t_sem, *reduction,
+):
+    windows, length, _ = low.shape
+    channels = x.shape[2]
+    slabs = channels // LANES
+    span = 2 * tile
+    walk = Walk(windows, length, tile)
+    tiles = walk.count
+    center, inverse = center_inverse(sums1[...], entries)
+    for c in range(slabs):
+        for row, values in enumerate((center, inverse, flat_row(gain1), flat_row(shift1))):
+            coef[c, row : row + 1] = values[:, lanes_of(c)]
+    stats[...] = jnp.zeros_like(stats)
+
+    def l_copy(i, slot):
+        w, _ = walk.where(i)
+        return pltpu.make_async_copy(low.at[w, walk.rows(i)], lows.at[slot], l_sem.at[slot])
+
+    def x_copy(i, slot):
+        w, _ = walk.where(i)
+        return pltpu.make_async_copy(x.at[w, walk.rows(i, 2)], xs.at[slot], x_sem.at[slot])
+
+    def o_copy(i, slot):
+        w, _ = walk.where(i)
+        return pltpu.make_async_copy(outs.at[slot], da_out.at[w, walk.rows(i, 2)], o_sem.at[slot])
+
+    def t_copies(g, slot):
+        k = EARLY + g // tiles
+        w, _ = walk.where(g % tiles)
+        rows = walk.rows(g % tiles)
+        at = pl.ds(pl.multiple_of((k // 2) * channels, channels), channels)
+        return (
+            pltpu.make_async_copy(s.at[k % 2, w, rows], ss.at[slot], t_sem.at[slot, 0]),
+            pltpu.make_async_copy(low.at[w, rows, at], ls.at[slot], t_sem.at[slot, 1]),
+        )
+
+    d_copy = pltpu.make_async_copy(parts, data.at[pl.ds(0, EARLY * slabs // 2)], d_sem)
+    d_copy.start()
+    for copy in t_copies(0, 0):
+        copy.start()
+    if joined:
+        greet(seqs, dps)
+    d_copy.wait()
+    l_copy(0, 0).start()
+    w_copy = pltpu.make_async_copy(w_hbm, w_ref, w_sem)
+    w_copy.start()
+    if joined:
+        sharing = Reduction.of(data, reduction)
+        sharing.step(0)
+
+    late = (5 - EARLY) * tiles
+    triple = slabs // 2
+
+    def due(g):
+        whole, part = g // tiles, g % tiles
+        first = jnp.where(whole == 0, 1, (EARLY + whole - 1) * triple)
+        count = jnp.where(whole == 0, EARLY * triple - 1, triple)
+        return first + count * part // tiles, first + count * (part + 1) // tiles
+
+    def weigh(g, _):
+        slot = g % 2
+        for copy in t_copies(g, slot):
+            copy.wait()
+
+        @pl.when(g + 1 < late)
+        def _():
+            for copy in t_copies(g + 1, 1 - slot):
+                copy.start()
+
+        @pl.when(g % tiles == 0)
+        def _():
+            total[...] = dot(ss[slot], ls[slot], TN)
+
+        @pl.when(g % tiles > 0)
+        def _():
+            total[...] += dot(ss[slot], ls[slot], TN)
+
+        @pl.when(g % tiles == tiles - 1)
+        def _():
+            for c in range(slabs):
+                at = slice((c % 2) * channels, (c % 2 + 1) * channels)
+                data[(EARLY + g // tiles) * triple + c // 2, at] = total[:, lanes_of(c)].astype(bf16)
+
+        if joined:
+            def take(t, _):
+                sharing.step(t)
+                return 0
+
+            lax.fori_loop(*due(g), take, 0)
+
+        return 0
+
+    lax.fori_loop(0, late, weigh, 0)
+    w_copy.wait()
+
+    def finish(slot, c):
+        cols = lanes(c)
+        m, inv, g, sh = (coef[c, row : row + 1] for row in range(4))
+        held = [jnp.zeros((8, LANES), f32), jnp.zeros((8, LANES), f32)]
+
+        def rows(r):
+            def run():
+                normed = (xs[slot, r : r + UNIT, cols] - m) * inv
+                incoming = g_buf[slot, c, EDGE + r : EDGE + r + UNIT] + g_buf[slot, c, EDGE + r - 1 : EDGE + r - 1 + UNIT]
+                back = gelu_slope(normed * g + sh) * incoming
+                outs[slot, r : r + UNIT, cols] = back.astype(bf16)
+                held[0] = held[0] + folded(back * normed)
+                held[1] = held[1] + folded(back)
+
+            return run
+
+        def close():
+            stats[0, :, cols] += held[0]
+            stats[1, :, cols] += held[1]
+
+        return [rows(r) for r in range(0, span, UNIT)] + [close]
+
+    def spread(slot, n):
+        at = lanes(n, 256)
+
+        def even():
+            part = dot(lows[slot, :, 0:channels], w_ref[0, at], NT)
+            part += dot(lows[slot, :, channels : 2 * channels], w_ref[2, at], NT)
+            part += dot(lows[slot, :, 2 * channels : 3 * channels], w_ref[4, at], NT)
+            for c in range(2):
+                g_buf[slot, 2 * n + c, pl.ds(EDGE, tile, stride=2)] = part[:, lanes_of(c)]
+
+        def odd():
+            part = dot(lows[slot, :, 0:channels], w_ref[1, at], NT)
+            part += dot(lows[slot, :, channels : 2 * channels], w_ref[3, at], NT)
+            for c in range(2):
+                g_buf[slot, 2 * n + c, pl.ds(EDGE + 1, tile, stride=2)] = part[:, lanes_of(c)]
+
+        return [even, odd]
+
+    def turn(i, slot, last):
+        other = 1 - slot
+        w, p = walk.where(i)
+        if not last:
+            l_copy(i, slot).wait()
+
+            @pl.when(i + 1 < tiles)
+            def _():
+                l_copy(i + 1, other).start()
+
+            @pl.when(p == 0)
+            def _():
+                edge = lows[slot, 0:16]
+                part = dot(edge[:, channels : 2 * channels], w_ref[1], NT) + dot(edge[:, 2 * channels :], w_ref[3], NT)
+                for c in range(slabs):
+                    g_buf[slot, c, EDGE - 1 : EDGE] = part[0:1, lanes_of(c)]
+
+            @pl.when(p > 0)
+            def _():
+                for c in range(slabs):
+                    g_buf[slot, c, EDGE - 1 : EDGE] = g_buf[other, c, EDGE + span - 1 : EDGE + span]
+
+        @pl.when(i >= 1)
+        def _():
+            x_copy(i - 1, other).wait()
+
+        @pl.when(i >= 3)
+        def _():
+            o_copy(i - 3, other).wait()
+
+        if not last:
+            x_copy(i, slot).start()
+
+        def part(n, _):
+            units = finish(other, 2 * n) + finish(other, 2 * n + 1)
+            interleave([] if last else spread(slot, n), units)
+            if last:
+                for unit in units:
+                    unit()
+            elif joined:
+                sharing.step(4 * triple + i * (channels // 256) + n)
+            return 0
+
+        lax.fori_loop(0, channels // 256, part, 0)
+
+        @pl.when(i >= 1)
+        def _():
+            o_copy(i - 1, other).start()
+
+    xs[1] = jnp.zeros(xs.shape[1:], f32)
+    g_buf[1] = jnp.zeros(g_buf.shape[1:], f32)
+
+    def pair(j, _):
+        for slot in range(2):
+            turn(2 * j + slot, slot, False)
+        return 0
+
+    lax.fori_loop(0, tiles // 2, pair, 0)
+    turn(tiles, 0, True)
+    o_copy(tiles - 2, 0).wait()
+    o_copy(tiles - 1, 1).wait()
+    if joined:
+        def more(t, _):
+            sharing.step(t)
+            return 0
+
+        lax.fori_loop(4 * triple + tiles * (channels // 256), sharing.steps, more, 0)
+    d_copy = pltpu.make_async_copy(sharing.done if joined else data, w_grad, d_sem)
+    d_copy.start()
+    d_copy.wait()
+
+
+def conv_one_spread(low, x, sums1, gain1, shift1, weight, s, parts, entries, number):
+    windows, length, _ = low.shape
+    channels = x.shape[2]
+    tile = min(512, length)
+    slabs = channels // LANES
+    rows, chunks = 2 * channels, 5 * slabs // 2
+    parts = parts.reshape(EARLY * slabs // 2, rows, LANES)
+    joined = Reduction.fits(rows)
+    estimate = params(10 * low.size * channels // 3, 12 * x.size, x.size)
+    if joined:
+        estimate["compiler_params"] = pltpu.CompilerParams(
+            vmem_limit_bytes=VMEM_LIMIT, collective_id=number, has_side_effects=True
+        )
+    da, stats, grad = pl.pallas_call(
+        functools.partial(conv_one_spread_kernel, tile, entries, joined, lax.axis_size("seq"), lax.axis_size("dp")),
+        out_shape=(
+            jax.ShapeDtypeStruct((windows, 2 * length, channels), bf16),
+            jax.ShapeDtypeStruct((2, 8, channels), f32),
+            jax.ShapeDtypeStruct((chunks, rows, LANES), bf16),
+        ),
+        in_specs=[ANY] * 2 + [VM] * 3 + [ANY] * 3,
+        out_specs=(ANY, VM, ANY),
+        scratch_shapes=[
+            pltpu.VMEM((2, tile, 3 * channels), bf16),
+            pltpu.VMEM((2, 2 * tile, channels), f32),
+            pltpu.VMEM((2, slabs, 2 * tile + 2 * EDGE, LANES), f32),
             pltpu.VMEM((2, 2 * tile, channels), bf16),
-            pltpu.VMEM(weight.shape, f32),
+            pltpu.VMEM((slabs, 8, LANES), f32),
             pltpu.VMEM(weight.shape, bf16),
-            DMA((2,)),
-            DMA((2,)),
+            pltpu.VMEM((channels, channels), f32),
+            pltpu.VMEM((2, tile, channels), bf16),
+            pltpu.VMEM((2, tile, channels), bf16),
+            pltpu.VMEM((chunks, rows, LANES), bf16),
             DMA((2,)),
             DMA((2,)),
             DMA((2,)),
             DMA,
-            DMA((2,)),
             DMA,
-            DMA,
-        ],
-        name="conv_one_back",
-        **params(20 * da.size * channels, 8 * x.size, x.size),
-    )(da, *da_sides, v, *v_sides, ct, *ct_sides, sums2, grads2, gain2, x, sums1, gain1, shift1, s, first, weight)
+            DMA((2, 2)),
+        ]
+        + (Reduction.scratch(chunks, rows) if joined else []),
+        name="conv_one_spread",
+        **estimate,
+    )(low, x, sums1, gain1, shift1, weight, s, parts)
+    if not joined:
+        grad = lax.psum(grad, ("dp", "seq"))
+    return da, stats, grad
+
+
+def widen_kernel(one, small, grads1, grads2, grads3, one_out, two_out, three_out, *vectors):
+    for c in range(one.shape[1]):
+        one_out[0, :, lanes_of(c)] = one[0, c].astype(f32)
+
+    @pl.when(pl.program_id(0) == 0)
+    def _():
+        taps, rows, width = two_out.shape
+        at = 0
+        for k in range(taps):
+            for c in range(width // LANES):
+                two_out[k, :, lanes_of(c)] = small[at : at + rows].astype(f32)
+                at += rows
+        rows = three_out.shape[0]
+        for c in range(three_out.shape[1] // LANES):
+            three_out[:, lanes_of(c)] = small[at : at + rows].astype(f32)
+            at += rows
+        for n, grads in enumerate((grads1, grads2, grads3)):
+            vectors[2 * n][...] = grads[0]
+            vectors[2 * n + 1][...] = grads[1]
+
+
+def widen(one, small, two_shape, three_shape, grads):
+    channels = two_shape[1]
+    slabs = channels // LANES
+    one = one.reshape(5, slabs, channels, LANES)
+    small = small.reshape(-1, LANES)
+    flat = lambda k: (0, 0)
+    lengths = [g.shape[1] for g in grads for _ in range(2)]
+    return pl.pallas_call(
+        widen_kernel,
+        grid=(5,),
+        out_shape=[
+            jax.ShapeDtypeStruct((5, channels, channels), f32),
+            jax.ShapeDtypeStruct(two_shape, f32),
+            jax.ShapeDtypeStruct(three_shape, f32),
+        ]
+        + [jax.ShapeDtypeStruct((n,), f32) for n in lengths],
+        in_specs=[pl.BlockSpec((1, slabs, channels, LANES), lambda k: (k, 0, 0, 0)), pl.BlockSpec(small.shape, flat)]
+        + [pl.BlockSpec(g.shape, flat) for g in grads],
+        out_specs=[
+            pl.BlockSpec((1, channels, channels), lambda k: (k, 0, 0)),
+            pl.BlockSpec(two_shape, lambda k: (0, 0, 0)),
+            pl.BlockSpec(three_shape, flat),
+        ]
+        + [pl.BlockSpec((n,), lambda k: (0,)) for n in lengths],
+        name="widen",
+        **params(moved=6 * one.size),
+    )(one, small, *grads)
 
 
 def last_kernel(entries, x, da, sums, grads, gain, out):
     center, inverse = center_inverse(sums[...], entries)
     both = grads[...]
-    scale = inverse * gain[...]
+    scale = inverse * flat_row(gain)
     lean = scale * inverse * (both[0:1] / entries)
     flat = scale * (both[1:2] / entries)
     for c in range(x.shape[2] // LANES):
@@ -1213,7 +1633,7 @@
             rows,
             pl.BlockSpec((8, channels), whole),
             pl.BlockSpec((8, channels), whole),
-            pl.BlockSpec((1, channels), whole),
+            pl.BlockSpec((channels,), lambda i: (0,)),
         ],
         out_specs=rows,
         name="input_back",
@@ -1237,9 +1657,6 @@
     windows, length, channels = inputs.shape
     entries = float(windows * length * lax.axis_size("dp") * lax.axis_size("seq"))
     half = entries / 2
-    gain_one, shift_one, gain_two, shift_two, gain_three, shift_three = (
-        v.reshape(1, -1) for v in (gain_one, shift_one, gain_two, shift_two, gain_three, shift_three)
-    )
     sums1, (x_left, x_right, c_left, c_right) = exchange(input_sums(inputs), [inputs, cotangent], 0)
     pooled, s, first, stats = conv_one_forward(
         inputs, x_left, x_right, sums1, gain_one, shift_one, conv_one, entries
@@ -1256,27 +1673,17 @@
         hidden_two, conv_two, half,
     )
     grads2, b_sides = exchange(stats, [da2], 4)
-    da1, stats, one_grad = conv_one_back(
-        da2, b_sides, pooled, p_sides, cotangent, (c_left, c_right), sums2, grads2, gain_two,
-        inputs, sums1, gain_one, shift_one, s, first, conv_one, entries,
+    low, parts, small = conv_one_weigh(
+        da2, b_sides, pooled, p_sides, cotangent, (c_left, c_right), sums2, grads2, gain_two, s, first,
+        two_grad, three_grad, entries, 7,
+    )
+    da1, stats, one_grad = conv_one_spread(
+        low, inputs, sums1, gain_one, shift_one, conv_one, s, parts, entries, 6
     )
     grads1, _ = exchange(stats, [], 5)
     input_grad = input_back(inputs, da1, sums1, grads1, gain_one, entries)
-    two_grad, three_grad = lax.psum((two_grad, three_grad), ("dp", "seq"))
-    one_grad = lax.psum(one_grad, ("dp", "seq"))
-    return (
-        outputs,
-        input_grad,
-        one_grad.astype(f32),
-        two_grad.astype(f32),
-        three_grad.astype(f32),
-        grads1[0],
-        grads1[1],
-        grads2[0],
-        grads2[1],
-        grads3[0],
-        grads3[1],
-    )
+    small_grads = widen(one_grad, small, conv_two.shape, conv_three.shape, (grads1, grads2, grads3))
+    return (outputs, input_grad, *small_grads)
 
 
 def solution(mesh):

time: 508 us -> 371 us (0.73)
  waiting for transfers between devices: 138 us -> 0 us
  Pallas kernels: 332 us -> 369 us
  between operations: 14.4 us -> 0.74 us
  other arithmetic: 11.4 us -> 0 us
  local copies, waits for them, and re-layouts: 10.4 us -> 0 us
    psum x1 -> x0, waiting for transfers between devices: 138 us -> none  [on_device(): one_grad = lax.psum(one_grad, ('dp', 'seq'))]
    pallas_call x1 -> x3, Pallas kernels: 104 us -> 142 us  [the longest x1 81.3 us: conv_one_spread(): pl.pallas_call(functools.partial(conv_one_spread_kernel, tile, entries, j...]
    convert_element_type x3 -> x0, other arithmetic: 11.4 us -> none  [the longest x1 5.61 us: on_device(): one_grad.astype(f32)]
    reshape x6 -> x0, local copies, waits for them, and re-layouts: 7.56 us -> none  [on_device(): v.reshape(1, -1)]
  transfers between devices with their start and end apart: 1 -> 0, of which waited for: 1 -> 0; matrix products, arithmetic and copies ran while one was open for 1% -> 0% of each run, Pallas kernels for 8% -> 0%
where the time goes in v2:
time: 371 us; the launch traced here: 369 us
  Pallas kernels  369 us (99%)
    pallas_call x1, Pallas kernels, conv_one_spread(): pl.pallas_call(functools.partial(conv_one_spread_kernel, tile, entries, j...  81.3 us
    pallas_call x6, Pallas kernels, exchange(): pl.pallas_call(functools.partial(exchange_kernel, len(arrays), seqs, dps)...  69 us
    pallas_call x1, Pallas kernels, conv_one_weigh(): pl.pallas_call(functools.partial(conv_one_weigh_kernel, tile, entries, jo...  50.9 us
    pallas_call x1, Pallas kernels, conv_one_forward(): pl.pallas_call(functools.partial(conv_one_kernel, tile, entries), out_sha...  42.5 us
    pallas_call x1, Pallas kernels, conv_two_back(): pl.pallas_call(functools.partial(conv_two_back_kernel, tile, entries), ou...  30.5 us
    pallas_call x1, Pallas kernels, input_back(): pl.pallas_call(functools.partial(last_kernel, entries), grid=(windows * p...  26.2 us
    pallas_call x1, Pallas kernels, conv_three_both(): pl.pallas_call(functools.partial(conv_three_kernel, entries), grid=(windo...  23.9 us
    pallas_call x1, Pallas kernels, conv_two_forward(): pl.pallas_call(functools.partial(conv_two_kernel, tile, entries), out_sha...  22.7 us

profile of v2, /device:TPU:0, one launch (start us, length us, event | category | flops | bytes accessed | tf_op | source)
XLA Modules:
  0.0 369.3 jit_solution(17703160330238289216)
XLA Ops:
  0.6 11.3 %input_sums.1.refs_0_ = f32[2,8,768]{2,1,0:T(8,128)} custom-call(f32[2,4096,768]{2,1,0:T(8,128)} %x.7), custom_call_target="tpu_custom_call" | custom-call | bytes 25165824 | tf_op jit(solution)/shard_map/input_sums/pallas_call | solution.py:302
  11.9 13.1 %exchange_0.1 = (f32[8,768]{1,0:T(8,128)}, f32[2,8,768]{2,1,0:T(8,128)}, f32[2,8,768]{2,1,0:T(8,128)}, f32[2,8,768]{2,1,0:T(8,128)}, f32[2,8,768]{2,1,0:T(8,128)}) custom-call(f32[2,8,768]{2,1,0:T(8,128)} %input_sums.1.refs_0_, f32[2,4096,768]{2,1,0:T(8,128)} %x.7, f32[2,2048,768]{2,1,0:T(8,128)} %ct.1), custom_call_target="tpu_custom_call" | custom-call | tf_op jit(solution)/shard_map/exchange_0/pallas_call | solution.py:258
  25.0 42.5 %conv_one_forward.1 = (f32[2,2048,768]{2,1,0:T(8,128)}, bf16[2,2,2048,768]{3,2,1,0:T(8,128)(2,1)}, bf16[2,16,768]{2,1,0:T(8,128)(2,1)}, f32[2,8,768]{2,1,0:T(8,128)}) custom-call(f32[2,4096,768]{2,1,0:T(8,128)} %x.7, f32[2,8,768]{2,1,0:T(8,128)} %get-tuple-element.57.left, f32[2,8,768]{2,1,0:T(8,128)} %get-tuple-element.58.right, ...), custom_call_target="tpu_custom_call" | custom-call | flops 24159191040 | bytes 50331648 | tf_op jit(solution)/shard_map/conv_one_forward/pallas_call | solution.py:491
  67.6 11.8 %exchange_1.1 = (f32[8,768]{1,0:T(8,128)}, f32[2,8,768]{2,1,0:T(8,128)}, f32[2,8,768]{2,1,0:T(8,128)}) custom-call(f32[2,8,768]{2,1,0:T(8,128)} %get-tuple-element.61.refs_0_, f32[2,2048,768]{2,1,0:T(8,128)} %get-tuple-element.60.refs_1_.v.pooled), custom_call_target="tpu_custom_call" | custom-call | tf_op jit(solution)/shard_map/exchange_1/pallas_call | solution.py:258
  79.4 22.7 %conv_two_forward.1 = (f32[2,2048,384]{2,1,0:T(8,128)}, bf16[2,2048,768]{2,1,0:T(8,128)(2,1)}, f32[2,8,384]{2,1,0:T(8,128)}) custom-call(f32[2,2048,768]{2,1,0:T(8,128)} %get-tuple-element.60.refs_1_.v.pooled, f32[2,8,768]{2,1,0:T(8,128)} %get-tuple-element.62.left.v_left, f32[2,8,768]{2,1,0:T(8,128)} %get-tuple-element.63.right.v_right, ...), custom_call_target="tpu_custom_call" | custom-call | flops 7247757312 | bytes 25165824 | tf_op jit(solution)/shard_map/conv_two_forward/pallas_call | solution.py:646
  102.0 10.9 %exchange_2.1 = (f32[8,384]{1,0:T(8,128)}, f32[2,8,384]{2,1,0:T(8,128)}, f32[2,8,384]{2,1,0:T(8,128)}) custom-call(f32[2,8,384]{2,1,0:T(8,128)} %get-tuple-element.66.refs_0_, f32[2,2048,384]{2,1,0:T(8,128)} %get-tuple-element.65.refs_1_.narrow.v), custom_call_target="tpu_custom_call" | custom-call | tf_op jit(solution)/shard_map/exchange_2/pallas_call | solution.py:258
  113.0 23.9 %conv_three_both.1 = (f32[2,2048,768]{2,1,0:T(8,128)}, f32[2,2048,384]{2,1,0:T(8,128)}, f32[2,8,384]{2,1,0:T(8,128)}, bf16[6,384,128]{2,1,0:T(8,128)(2,1)}) custom-call(f32[2,2048,384]{2,1,0:T(8,128)} %get-tuple-element.65.refs_1_.narrow.v, f32[2,2048,768]{2,1,0:T(8,128)} %ct.1, f32[2,2048,768]{2,1,0:T(8,128)} %get-tuple-element.60.refs_1_.v.pooled, ...), custom_call_target="tpu_custom_call" | custom-call | flops 7247757312 | bytes 37748736 | tf_op jit(solution)/shard_map/conv_three_both/pallas_call | solution.py:719
  136.9 10.5 %exchange_3.1 = (f32[8,384]{1,0:T(8,128)}, f32[2,8,384]{2,1,0:T(8,128)}, f32[2,8,384]{2,1,0:T(8,128)}) custom-call(f32[2,8,384]{2,1,0:T(8,128)} %get-tuple-element.70.refs_0_, f32[2,2048,384]{2,1,0:T(8,128)} %get-tuple-element.69.refs_1_.da), custom_call_target="tpu_custom_call" | custom-call | tf_op jit(solution)/shard_map/exchange_3/pallas_call | solution.py:258
  147.4 30.5 %conv_two_back.1 = (f32[2,2048,768]{2,1,0:T(8,128)}, f32[2,8,768]{2,1,0:T(8,128)}, bf16[9,768,128]{2,1,0:T(8,128)(2,1)}) custom-call(f32[2,2048,384]{2,1,0:T(8,128)} %get-tuple-element.69.refs_1_.da, f32[2,8,384]{2,1,0:T(8,128)} %get-tuple-element.71.da_left, f32[2,8,384]{2,1,0:T(8,128)} %get-tuple-element.72.da_right, ...), custom_call_target="tpu_custom_call" | custom-call | flops 14495514624 | bytes 50331648 | tf_op jit(solution)/shard_map/conv_two_back/pallas_call | solution.py:920
  177.9 11.3 %exchange_4.1 = (f32[8,768]{1,0:T(8,128)}, f32[2,8,768]{2,1,0:T(8,128)}, f32[2,8,768]{2,1,0:T(8,128)}) custom-call(f32[2,8,768]{2,1,0:T(8,128)} %get-tuple-element.78.refs_0_, f32[2,2048,768]{2,1,0:T(8,128)} %get-tuple-element.77.refs_1_.da), custom_call_target="tpu_custom_call" | custom-call | tf_op jit(solution)/shard_map/exchange_4/pallas_call | solution.py:258
  189.3 50.9 %conv_one_weigh.1 = (bf16[2,2048,2304]{2,1,0:T(8,128)(2,1)}, bf16[3,6,768,128]{3,2,1,0:T(8,128)(2,1)}, bf16[6,1536,128]{2,1,0:T(8,128)(2,1)}) custom-call(f32[2,2048,768]{2,1,0:T(8,128)} %get-tuple-element.77.refs_1_.da, f32[2,8,768]{2,1,0:T(8,128)} %get-tuple-element.79.da_left, f32[2,8,768]{2,1,0:T(8,128)} %get-tuple-element.80.da_right, ...), custom_call_target="tpu_custom_call" | custom-call | flops 28991029248 | bytes 75497472 | tf_op jit(solution)/shard_map/conv_one_weigh/pallas_call | solution.py:1265
  240.2 81.3 %conv_one_spread.1 = (bf16[2,4096,768]{2,1,0:T(8,128)(2,1)}, f32[2,8,768]{2,1,0:T(8,128)}, bf16[15,1536,128]{2,1,0:T(8,128)(2,1)}) custom-call(bf16[2,2048,2304]{2,1,0:T(8,128)(2,1)} %get-tuple-element.88.low, f32[2,4096,768]{2,1,0:T(8,128)} %x.7, f32[8,768]{1,0:T(8,128)} %get-tuple-element.59.sums.sums1, f32[768]{0:T(1024)} %gain.7, f32[768]{0:T(1024)} %shift1.1, ...), custom_call_target="tpu_custom_call" | custom-call | flops 24159191040 | bytes 75497472 | tf_op jit(solution)/shard_map/conv_one_spread/pallas_call | solution.py:1521
  321.6 11.3 %exchange_5.1.grads.grads1 = f32[8,768]{1,0:T(8,128)} custom-call(f32[2,8,768]{2,1,0:T(8,128)} %get-tuple-element.91.refs_0_), custom_call_target="tpu_custom_call" | custom-call | tf_op jit(solution)/shard_map/exchange_5/pallas_call | solution.py:258
  332.9 10.2 %widen.1 = (f32[5,768,768]{2,1,0:T(8,128)}, f32[3,768,384]{2,1,0:T(8,128)}, f32[384,768]{1,0:T(8,128)}, f32[768]{0:T(1024)}, f32[768]{0:T(1024)}, /*index=5*/f32...) custom-call(bf16[5,6,768,128]{3,2,1,0:T(8,128)(2,1)} %bitcast.5, bf16[9216,128]{1,0:T(8,128)(2,1)} %bitcast.6, ...), custom_call_target="tpu_custom_call" | custom-call | bytes 17694720 | tf_op jit(solution)/shard_map/widen/pallas_call | solution.py:1585
  343.1 26.2 %input_back.1 = f32[2,4096,768]{2,1,0:T(8,128)} custom-call(f32[2,4096,768]{2,1,0:T(8,128)} %x.7, bf16[2,4096,768]{2,1,0:T(8,128)(2,1)} %get-tuple-element.90.da, f32[8,768]{1,0:T(8,128)} %get-tuple-element.59.sums.sums1, f32[8,768]{1,0:T(8,128)} %exchange_5.1.grads.grads1, f32[768]{0:T(1024)} %gain.7), custom_call_target="tpu_custom_call" | custom-call | bytes 62914560 | tf_op jit(solution)/shard_map/input_back/pallas_call | solution.py:1627

commit v3 on v2

--- a/solution.py
+++ b/solution.py
@@ -19,6 +19,7 @@
 CUBIC = 0.7978845608028654 * 0.044715
 VMEM_LIMIT = 60 << 20
 EARLY = 3
+AHEAD = 3
 NN = (((1,), (0,)), ((), ()))
 NT = (((1,), (1,)), ((), ()))
 TN = (((0,), (0,)), ((), ()))
@@ -31,6 +32,20 @@
 def gelu(v):
     half = 0.5 * v
     return half + half * jnp.tanh(v * (LINEAR + CUBIC * (v * v)))
+
+
+ROOT = CUBIC ** (1.0 / 3.0)
+BEND = LINEAR / ROOT
+
+
+def gelu_scaled(q):
+    return q * (1.0 + jnp.tanh(q * (BEND + q * q)))
+
+
+def slope_scaled(q):
+    square = q * q
+    th = jnp.tanh(q * (BEND + square))
+    return (1.0 + th) * (1.0 + (1.0 - th) * (q * (BEND + 3.0 * square)))
 
 
 def gelu_both(v):
@@ -141,127 +156,38 @@
     )
 
 
-def exchange_kernel(arrays, seqs, dps, *refs):
-    stats = refs[0]
-    sources = refs[1 : 1 + arrays]
-    sums = refs[1 + arrays]
-    outs = refs[2 + arrays : 2 + 3 * arrays]
-    scratch = refs[2 + 3 * arrays :]
-    lands = scratch[: 2 * arrays]
-    message, near, far, near_send, near_recv, far_send, far_recv, edge_send, edge_recv = scratch[2 * arrays :]
-    channels = stats.shape[2]
-    slabs = channels // LANES
+def greet(seqs, dps):
     seq, dp = lax.axis_index("seq"), lax.axis_index("dp")
-
     barrier = pltpu.get_barrier_semaphore()
 
-    def greet_near(d, _):
+    def near(d, _):
         pl.semaphore_signal(barrier, inc=1, device_id={"seq": lax.rem(seq + d, seqs)}, device_id_type=MESH)
         return 0
 
-    def greet_far(d, _):
+    def far(d, _):
         pl.semaphore_signal(barrier, inc=1, device_id={"dp": lax.rem(dp + d, dps)}, device_id_type=MESH)
         return 0
 
-    lax.fori_loop(1, seqs, greet_near, 0)
-    lax.fori_loop(1, dps, greet_far, 0)
+    lax.fori_loop(1, seqs, near, 0)
+    lax.fori_loop(1, dps, far, 0)
     pl.semaphore_wait(barrier, seqs - 1 + dps - 1)
 
-    def edge_copy(a, side):
-        src = sources[a]
-        length = src.shape[1]
-        part = src.at[:, pl.ds(length - EDGE, EDGE)] if side == 0 else src.at[:, pl.ds(0, EDGE)]
-        to = seq + 1 if side == 0 else seq - 1
-        return pltpu.make_async_remote_copy(
-            src_ref=part, dst_ref=lands[2 * a + side], send_sem=edge_send.at[2 * a + side],
-            recv_sem=edge_recv.at[2 * a + side], device_id={"seq": to}, device_id_type=MESH,
-        )
-
-    message[...] = jnp.zeros_like(message)
-    for row in range(2):
-        total = jnp.sum(stats[row], axis=0, keepdims=True)
-        for c in range(slabs):
-            message[row * slabs + c : row * slabs + c + 1] = total[:, c * LANES : (c + 1) * LANES]
-
-    def near_copy(d, to):
-        return pltpu.make_async_remote_copy(
-            src_ref=message, dst_ref=near.at[seq], send_sem=near_send.at[d], recv_sem=near_recv.at[d],
-            device_id={"seq": to}, device_id_type=MESH,
-        )
-
-    def near_start(d, _):
-        near_copy(d, lax.rem(seq + d, seqs)).start()
-        return 0
-
-    def near_wait(d, _):
-        near_copy(d, lax.rem(seq + d, seqs)).wait()
-        return 0
-
-    lax.fori_loop(1, seqs, near_start, 0)
-
-    for a in range(arrays):
-        @pl.when(seq < seqs - 1)
-        def _():
-            edge_copy(a, 0).start()
-
-        @pl.when(seq > 0)
-        def _():
-            edge_copy(a, 1).start()
-
-    near[seq] = message[...]
-    lax.fori_loop(1, seqs, near_wait, 0)
-    far[dp] = lax.fori_loop(1, seqs, lambda s, t: t + near[s], near[0])
-
-    def far_copy(d, to):
-        return pltpu.make_async_remote_copy(
-            src_ref=far.at[dp], dst_ref=far.at[dp], send_sem=far_send.at[d], recv_sem=far_recv.at[d],
-            device_id={"dp": to}, device_id_type=MESH,
-        )
-
-    def far_start(d, _):
-        far_copy(d, lax.rem(dp + d, dps)).start()
-        return 0
-
-    def far_wait(d, _):
-        far_copy(d, lax.rem(dp + d, dps)).wait()
-        return 0
-
-    lax.fori_loop(1, dps, far_start, 0)
-
-    for a in range(arrays):
-        @pl.when(seq < seqs - 1)
-        def _():
-            edge_copy(a, 0).wait_send()
-            edge_copy(a, 1).wait_recv()
-
-        @pl.when(seq > 0)
-        def _():
-            edge_copy(a, 1).wait_send()
-            edge_copy(a, 0).wait_recv()
-
-        for side in range(2):
-            outs[2 * a + side][...] = lands[2 * a + side][...]
-
-    lax.fori_loop(1, dps, far_wait, 0)
-    total = lax.fori_loop(1, dps, lambda s, t: t + far[s], far[0])
-    sums[...] = jnp.zeros_like(sums)
-    for row in range(2):
-        for c in range(slabs):
-            sums[row : row + 1, c * LANES : (c + 1) * LANES] = total[row * slabs + c : row * slabs + c + 1]
-
-
-def exchange(stats, arrays, number):
-    seqs, dps = lax.axis_size("seq"), lax.axis_size("dp")
-    channels = stats.shape[2]
-    rows = -(-2 * (channels // LANES) // 8) * 8
-    edges = [jax.ShapeDtypeStruct((a.shape[0], EDGE, a.shape[2]), a.dtype) for a in arrays for _ in range(2)]
-    got = pl.pallas_call(
-        functools.partial(exchange_kernel, len(arrays), seqs, dps),
-        out_shape=[jax.ShapeDtypeStruct((8, channels), f32)] + edges,
-        in_specs=[VM] + [ANY] * len(arrays),
-        out_specs=[VM] * (1 + len(edges)),
-        scratch_shapes=[pltpu.VMEM(e.shape, e.dtype) for e in edges]
-        + [
+
+class Exchange:
+    SUMS = 7
+
+    def __init__(self, refs, edge_refs=()):
+        self.message, self.near, self.far, self.near_send, self.near_recv, self.far_send, self.far_recv = refs
+        self.seqs, self.dps = self.near.shape[0], self.far.shape[0]
+        self.seq, self.dp = lax.axis_index("seq"), lax.axis_index("dp")
+        if edge_refs:
+            self.lands, (self.edge_send, self.edge_recv) = edge_refs[:-2], edge_refs[-2:]
+
+    @staticmethod
+    def scratch(channels):
+        seqs, dps = lax.axis_size("seq"), lax.axis_size("dp")
+        rows = -(-2 * (channels // LANES) // 8) * 8
+        return [
             pltpu.VMEM((rows, LANES), f32),
             pltpu.VMEM((seqs, rows, LANES), f32),
             pltpu.VMEM((dps, rows, LANES), f32),
@@ -269,50 +195,136 @@
             DMA((seqs,)),
             DMA((dps,)),
             DMA((dps,)),
-            DMA((2 * max(len(arrays), 1),)),
-            DMA((2 * max(len(arrays), 1),)),
-        ],
+        ]
+
+    @staticmethod
+    def edges(arrays):
+        return [jax.ShapeDtypeStruct((a.shape[0], EDGE, a.shape[2]), a.dtype) for a in arrays for _ in range(2)]
+
+    @staticmethod
+    def edge_scratch(arrays):
+        edges = Exchange.edges(arrays)
+        return [pltpu.VMEM(e.shape, e.dtype) for e in edges] + [DMA((len(edges),)), DMA((len(edges),))]
+
+    def edge_copy(self, n, src):
+        length = src.shape[1]
+        part = src.at[:, pl.ds(length - EDGE, EDGE)] if n % 2 == 0 else src.at[:, pl.ds(0, EDGE)]
+        to = self.seq + 1 if n % 2 == 0 else self.seq - 1
+        return pltpu.make_async_remote_copy(
+            src_ref=part, dst_ref=self.lands[n], send_sem=self.edge_send.at[n], recv_sem=self.edge_recv.at[n],
+            device_id={"seq": to}, device_id_type=MESH,
+        )
+
+    def start_edges(self, sources):
+        for a, src in enumerate(sources):
+            @pl.when(self.seq < self.seqs - 1)
+            def _():
+                self.edge_copy(2 * a, src).start()
+
+            @pl.when(self.seq > 0)
+            def _():
+                self.edge_copy(2 * a + 1, src).start()
+
+    def finish_edges(self, sources):
+        for a, src in enumerate(sources):
+            @pl.when(self.seq < self.seqs - 1)
+            def _():
+                self.edge_copy(2 * a, src).wait_send()
+                self.edge_copy(2 * a + 1, src).wait_recv()
+
+            @pl.when(self.seq > 0)
+            def _():
+                self.edge_copy(2 * a + 1, src).wait_send()
+                self.edge_copy(2 * a, src).wait_recv()
+
+    def near_copy(self, d):
+        return pltpu.make_async_remote_copy(
+            src_ref=self.message, dst_ref=self.near.at[self.seq], send_sem=self.near_send.at[d],
+            recv_sem=self.near_recv.at[d], device_id={"seq": lax.rem(self.seq + d, self.seqs)}, device_id_type=MESH,
+        )
+
+    def far_copy(self, d):
+        mine = self.far.at[self.dp]
+        return pltpu.make_async_remote_copy(
+            src_ref=mine, dst_ref=mine, send_sem=self.far_send.at[d], recv_sem=self.far_recv.at[d],
+            device_id={"dp": lax.rem(self.dp + d, self.dps)}, device_id_type=MESH,
+        )
+
+    def each(self, count, run):
+        def body(d, _):
+            run(d)
+            return 0
+
+        lax.fori_loop(1, count, body, 0)
+
+    def start_sums(self, stats):
+        slabs = stats.shape[2] // LANES
+        self.message[...] = jnp.zeros_like(self.message)
+        for row in range(2):
+            total = jnp.sum(stats[row], axis=0, keepdims=True)
+            for c in range(slabs):
+                self.message[row * slabs + c : row * slabs + c + 1] = total[:, lanes_of(c)]
+        self.each(self.seqs, lambda d: self.near_copy(d).start())
+        self.near[self.seq] = self.message[...]
+        self.each(self.seqs, lambda d: self.near_copy(d).wait())
+        self.far[self.dp] = lax.fori_loop(1, self.seqs, lambda n, t: t + self.near[n], self.near[0])
+        self.each(self.dps, lambda d: self.far_copy(d).start())
+
+    def finish_sums(self, sums):
+        slabs = sums.shape[1] // LANES
+        self.each(self.dps, lambda d: self.far_copy(d).wait())
+        total = lax.fori_loop(1, self.dps, lambda n, t: t + self.far[n], self.far[0])
+        sums[...] = jnp.zeros_like(sums)
+        for row in range(2):
+            for c in range(slabs):
+                sums[row : row + 1, lanes_of(c)] = total[row * slabs + c : row * slabs + c + 1]
+
+
+def lanes_of(c):
+    return slice(c * LANES, (c + 1) * LANES)
+
+
+def exchange_kernel(arrays, *refs):
+    stats, sources, sums = refs[0], refs[1 : 1 + arrays], refs[1 + arrays]
+    outs, scratch = refs[2 + arrays : 2 + 3 * arrays], refs[2 + 3 * arrays :]
+    talk = Exchange(scratch[: Exchange.SUMS], scratch[Exchange.SUMS :])
+    greet(talk.seqs, talk.dps)
+    talk.start_edges(sources)
+    talk.start_sums(stats)
+    talk.finish_edges(sources)
+    for out, land in zip(outs, talk.lands):
+        out[...] = land[...]
+    talk.finish_sums(sums)
+
+
+def exchange(stats, arrays, number):
+    channels = stats.shape[2]
+    edges = Exchange.edges(arrays)
+    got = pl.pallas_call(
+        functools.partial(exchange_kernel, len(arrays)),
+        out_shape=[jax.ShapeDtypeStruct((8, channels), f32)] + edges,
+        in_specs=[VM] + [ANY] * len(arrays),
+        out_specs=[VM] * (1 + len(edges)),
+        scratch_shapes=Exchange.scratch(channels) + Exchange.edge_scratch(arrays),
         compiler_params=pltpu.CompilerParams(collective_id=number, has_side_effects=True),
         name=f"exchange_{number}",
     )(stats, *arrays)
     return got[0], got[1:]
 
 
-def sums_kernel(x, stats):
-    @pl.when(pl.program_id(0) == 0)
-    def _():
-        stats[...] = jnp.zeros_like(stats)
-
-    channels = x.shape[2]
-    for c in range(channels // LANES):
-        total = jnp.zeros((8, LANES), f32)
-        squares = jnp.zeros((8, LANES), f32)
-        for r in range(0, x.shape[1], 128):
-            v = x[0, r : r + 128, lanes(c)]
-            total += folded(v)
-            squares += folded(v * v)
-        stats[0, :, lanes(c)] += total
-        stats[1, :, lanes(c)] += squares
-
-
-def input_sums(x):
-    windows, length, channels = x.shape
-    tile = min(1024, length)
-    per = length // tile
-    return pl.pallas_call(
-        sums_kernel,
-        grid=(windows * per,),
-        out_shape=jax.ShapeDtypeStruct((2, 8, channels), f32),
-        in_specs=[pl.BlockSpec((1, tile, channels), lambda i: (i // per, i % per, 0))],
-        out_specs=pl.BlockSpec((2, 8, channels), lambda i: (0, 0, 0)),
-        name="input_sums",
-        **params(moved=4 * x.size),
-    )(x)
+def joining(estimate, number):
+    return dict(
+        estimate,
+        compiler_params=pltpu.CompilerParams(
+            vmem_limit_bytes=VMEM_LIMIT, collective_id=number, has_side_effects=True
+        ),
+    )
 
 
 def conv_one_kernel(
-    tile, entries, x, left, right, sums, gain, shift, w_hbm, pooled, s_out, first_out, stats,
-    xs, h_buf, lhs_a, lhs_b, outs, coef, w_ref, x_sem, s_sem, f_sem, o_sem, w_sem,
+    tile, entries, x, cotangent, gain, shift, w_hbm,
+    pooled, s_out, first_out, sums1, sums2, c_left, c_right, p_left, p_right,
+    xs, h_buf, lhs_a, lhs_b, outs, coef, w_ref, stats, x_sem, s_sem, f_sem, o_sem, w_sem, *talks,
 ):
     windows, length, channels = x.shape
     slabs = channels // LANES
@@ -320,13 +332,48 @@
     walk = Walk(windows, length // 2, tile)
     tiles = walk.count
     lhs = (lhs_a, lhs_b)
-    center, inverse = center_inverse(sums[...], entries)
-    scale = inverse * flat_row(gain)
-    offset = flat_row(shift) - center * scale
-    for c in range(slabs):
-        coef[c, 0:1] = scale[:, lanes_of(c)]
-        coef[c, 1:2] = offset[:, lanes_of(c)]
+    n = Exchange.SUMS
+    talk1 = Exchange(talks[:n], talks[2 * n : 2 * n + 6])
+    talk2 = Exchange(talks[n : 2 * n], talks[2 * n + 6 :])
+    left, right = talk1.lands[:2]
+
+    def scan_copy(i, slot):
+        w, _ = walk.where(i)
+        return pltpu.make_async_copy(x.at[w, walk.rows(i, 2)], xs.at[slot, pl.ds(EDGE, span)], x_sem.at[slot])
+
+    scan_copy(0, 0).start()
+    scan_copy(1, 1).start()
+    greet(talk1.seqs, talk1.dps)
+    talk1.start_edges((x, cotangent))
     stats[...] = jnp.zeros_like(stats)
+
+    def scan(i, _):
+        slot = i % 2
+        scan_copy(i, slot).wait()
+
+        def slab(c, _):
+            cols = lanes(c)
+            total = jnp.zeros((8, LANES), f32)
+            squares = jnp.zeros((8, LANES), f32)
+            for r in range(EDGE, EDGE + span, 128):
+                v = xs[slot, r : r + 128, cols]
+                total += folded(v)
+                squares += folded(v * v)
+            stats[0, :, cols] += total
+            stats[1, :, cols] += squares
+            return 0
+
+        lax.fori_loop(0, slabs, slab, 0)
+
+        @pl.when(i + 2 < tiles)
+        def _():
+            scan_copy(i + 2, slot).start()
+
+        return 0
+
+    lax.fori_loop(0, tiles, scan, 0)
+    talk1.start_sums(stats)
+    w_copy = pltpu.make_async_copy(w_hbm, w_ref, w_sem)
 
     def load(i, slot):
         walk.fetch(i, x, left, right, xs.at[slot], x_sem.at[slot], 2)
@@ -356,15 +403,15 @@
         cols = lanes(c)
 
         def ends():
-            head = gelu(src[0:EDGE, cols] * scale + offset)
+            head = gelu_scaled(src[0:EDGE, cols] * scale + offset)
             h_buf[c, 0:EDGE] = jnp.where(walk.hide_left(i), 0.0, head)
-            tail = gelu(src[EDGE + span : 2 * EDGE + span, cols] * scale + offset)
+            tail = gelu_scaled(src[EDGE + span : 2 * EDGE + span, cols] * scale + offset)
             h_buf[c, EDGE + span : 2 * EDGE + span] = jnp.where(walk.hide_right(i), 0.0, tail)
 
         def rows(r):
             def run():
                 for q in range(EDGE + r, EDGE + r + 2 * UNIT, 2 * SUB):
-                    h_buf[c, q : q + 2 * SUB] = gelu(src[q : q + 2 * SUB, cols] * scale + offset)
+                    h_buf[c, q : q + 2 * SUB] = gelu_scaled(src[q : q + 2 * SUB, cols] * scale + offset)
 
             return run
 
@@ -397,18 +444,28 @@
             return run
 
         def finish():
-            total = 0.5 * held[0]
+            total = (0.25 / ROOT) * held[0]
             outs[slot, :, cols] = total
             stats[0, :, cols] += folded(total)
             stats[1, :, cols] += folded(total * total)
 
         return [piece(k) for k in range(5)], finish
 
+    talk1.finish_edges((x, cotangent))
+    c_left[...] = talk1.lands[2][...]
+    c_right[...] = talk1.lands[3][...]
     load(0, 0)
+    load(1, 1)
+    w_copy.start()
+    talk1.finish_sums(sums1)
+    center, inverse = center_inverse(sums1[...], entries)
+    scale = inverse * flat_row(gain)
+    offset = flat_row(shift) - center * scale
+    for c in range(slabs):
+        coef[c, 0:1] = ROOT * scale[:, lanes_of(c)]
+        coef[c, 1:2] = ROOT * offset[:, lanes_of(c)]
+    stats[...] = jnp.zeros_like(stats)
     wait_for(xs.at[0], x_sem.at[0])
-    w_copy = pltpu.make_async_copy(w_hbm, w_ref, w_sem)
-    w_copy.start()
-    load(1, 1)
 
     def first_slab(c, _):
         for unit in activate(0, 0, c):
@@ -477,27 +534,33 @@
         first_copy(tiles - 1, 1).wait()
     o_copy(tiles - 2, 0).wait()
     o_copy(tiles - 1, 1).wait()
-
-
-def lanes_of(c):
-    return slice(c * LANES, (c + 1) * LANES)
-
-
-def conv_one_forward(x, left, right, sums, gain, shift, weight, entries):
+    talk2.start_edges((pooled,))
+    talk2.start_sums(stats)
+    talk2.finish_edges((pooled,))
+    p_left[...] = talk2.lands[0][...]
+    p_right[...] = talk2.lands[1][...]
+    talk2.finish_sums(sums2)
+
+
+def conv_one_forward(x, cotangent, gain, shift, weight, entries, number):
     windows, length, channels = x.shape
     half = length // 2
     tile = min(512, half)
     slabs = channels // LANES
-    return pl.pallas_call(
+    pooled = jax.ShapeDtypeStruct((windows, half, channels), f32)
+    edges = Exchange.edges([cotangent, pooled])
+    got = pl.pallas_call(
         functools.partial(conv_one_kernel, tile, entries),
-        out_shape=(
-            jax.ShapeDtypeStruct((windows, half, channels), f32),
+        out_shape=[
+            pooled,
             jax.ShapeDtypeStruct((2, windows, half, channels), bf16),
             jax.ShapeDtypeStruct((windows, 16, channels), bf16),
-            jax.ShapeDtypeStruct((2, 8, channels), f32),
-        ),
-        in_specs=[ANY, ANY, ANY, VM, VM, VM, ANY],
-        out_specs=(ANY, ANY, ANY, VM),
+            jax.ShapeDtypeStruct((8, channels), f32),
+            jax.ShapeDtypeStruct((8, channels), f32),
+        ]
+        + edges,
+        in_specs=[ANY, ANY, VM, VM, ANY],
+        out_specs=[ANY] * 3 + [VM] * 6,
         scratch_shapes=[
             pltpu.VMEM((2, 2 * tile + 2 * EDGE, channels), f32),
             pltpu.VMEM((slabs, 2 * tile + 2 * EDGE, LANES), f32),
@@ -506,20 +569,25 @@
             pltpu.VMEM((2, tile, channels), f32),
             pltpu.VMEM((slabs, 8, LANES), f32),
             pltpu.VMEM((5 * channels, channels), bf16),
+            pltpu.VMEM((2, 8, channels), f32),
             DMA((2,)),
             DMA((2, 2)),
             DMA,
             DMA((2,)),
             DMA,
-        ],
+        ]
+        + Exchange.scratch(channels) * 2
+        + Exchange.edge_scratch([x, cotangent])
+        + Exchange.edge_scratch([pooled]),
         name="conv_one_forward",
-        **params(10 * windows * half * channels * channels, 8 * x.size, x.size),
-    )(x, left, right, sums, gain, shift, weight.reshape(5 * channels, channels))
+        **joining(params(10 * windows * half * channels * channels, 12 * x.size, x.size), number),
+    )(x, cotangent, gain, shift, weight.reshape(5 * channels, channels))
+    return got[:5], got[5:7], got[7:9]
 
 
 def conv_two_kernel(
-    tile, entries, v, left, right, sums, gain, shift, w_hbm, narrow, h_out, stats,
-    vs, h_buf, lhs_a, lhs_b, outs, w_ref, v_sem, h_sem, o_sem, w_sem,
+    tile, entries, v, left, right, sums, gain, shift, w_hbm, narrow, h_out, sums3, n_left, n_right,
+    vs, h_buf, lhs_a, lhs_b, outs, w_ref, stats, v_sem, h_sem, o_sem, w_sem, *talks,
 ):
     windows, length, channels = v.shape
     slabs = channels // LANES
@@ -529,6 +597,7 @@
     center, inverse = center_inverse(sums[...], entries)
     scale = inverse * flat_row(gain)
     offset = flat_row(shift) - center * scale
+    scale, offset = ROOT * scale, ROOT * offset
     stats[...] = jnp.zeros_like(stats)
 
     def load(i, slot):
@@ -549,15 +618,15 @@
         src, dst, cols = vs.at[slot], lhs[slot], lanes(c)
 
         def ends():
-            head = gelu(src[0:EDGE, cols] * a + b)
+            head = gelu_scaled(src[0:EDGE, cols] * a + b)
             h_buf[c, 0:EDGE] = jnp.where(walk.hide_left(i), 0.0, head)
-            tail = gelu(src[EDGE + tile : 2 * EDGE + tile, cols] * a + b)
+            tail = gelu_scaled(src[EDGE + tile : 2 * EDGE + tile, cols] * a + b)
             h_buf[c, EDGE + tile : 2 * EDGE + tile] = jnp.where(walk.hide_right(i), 0.0, tail)
 
         def rows(r):
             def run():
                 q = EDGE + r
-                h_buf[c, q : q + UNIT] = gelu(src[q : q + UNIT, cols] * a + b)
+                h_buf[c, q : q + UNIT] = gelu_scaled(src[q : q + UNIT, cols] * a + b)
 
             return run
 
@@ -575,6 +644,8 @@
         return units + [taps(tile - UNIT)]
 
     load(0, 0)
+    talk = Exchange(talks[: Exchange.SUMS], talks[Exchange.SUMS :])
+    greet(talk.seqs, talk.dps)
     wait_for(vs.at[0], v_sem.at[0])
     w_copy = pltpu.make_async_copy(w_hbm, w_ref, w_sem)
     w_copy.start()
@@ -620,7 +691,7 @@
             for c in range(slabs):
                 units += activate(i + 1, other, c)
             interleave([piece(k) for k in range(3)], units)
-            total = held[0]
+            total = (0.5 / ROOT) * held[0]
             outs[slot] = total
             stats[0] += folded(total)
             stats[1] += folded(total * total)
@@ -636,22 +707,30 @@
     h_copy(tiles - 1, 1).wait()
     o_copy(tiles - 2, 0).wait()
     o_copy(tiles - 1, 1).wait()
-
-
-def conv_two_forward(v, left, right, sums, gain, shift, weight, entries):
+    talk.start_edges((narrow,))
+    talk.start_sums(stats)
+    talk.finish_edges((narrow,))
+    n_left[...] = talk.lands[0][...]
+    n_right[...] = talk.lands[1][...]
+    talk.finish_sums(sums3)
+
+
+def conv_two_forward(v, left, right, sums, gain, shift, weight, entries, number):
     windows, length, channels = v.shape
     tile = min(512, length)
     slabs = channels // LANES
     width = weight.shape[2]
-    return pl.pallas_call(
+    narrow = jax.ShapeDtypeStruct((windows, length, width), f32)
+    got = pl.pallas_call(
         functools.partial(conv_two_kernel, tile, entries),
-        out_shape=(
-            jax.ShapeDtypeStruct((windows, length, width), f32),
+        out_shape=[
+            narrow,
             jax.ShapeDtypeStruct((windows, length, channels), bf16),
-            jax.ShapeDtypeStruct((2, 8, width), f32),
-        ),
+            jax.ShapeDtypeStruct((8, width), f32),
+        ]
+        + Exchange.edges([narrow]),
         in_specs=[ANY, ANY, ANY, VM, VM, VM, ANY],
-        out_specs=(ANY, ANY, VM),
+        out_specs=[ANY, ANY, VM, VM, VM],
         scratch_shapes=[
             pltpu.VMEM((2, tile + 2 * EDGE, channels), f32),
             pltpu.VMEM((slabs, tile + 2 * EDGE, LANES), f32),
@@ -659,14 +738,18 @@
             pltpu.VMEM((tile, 3 * channels), bf16),
             pltpu.VMEM((2, tile, width), f32),
             pltpu.VMEM((3 * channels, width), bf16),
+            pltpu.VMEM((2, 8, width), f32),
             DMA((2,)),
             DMA((2,)),
             DMA((2,)),
             DMA,
-        ],
+        ]
+        + Exchange.scratch(width)
+        + Exchange.edge_scratch([narrow]),
         name="conv_two_forward",
-        **params(6 * v.size * width, 8 * v.size, v.size),
+        **joining(params(6 * v.size * width, 8 * v.size, v.size), number),
     )(v, left, right, sums, gain, shift, weight.reshape(3 * channels, width))
+    return got[:3], got[3:]
 
 
 def conv_three_kernel(
@@ -753,9 +836,9 @@
 
 def conv_two_back_kernel(
     tile, entries, da, da_left, da_right, v, v_left, v_right, sums3, grads3, gain3, pooled, sums2, gain2, shift2,
-    h, w_hbm, da_out, stats, w_grad,
-    das, vs, ps, hs, low_buf, low_a, low_b, g_buf, outs, total, w_ref, w_flip,
-    a_sem, v_sem, p_sem, h_sem, o_sem, w_sem,
+    h, w_hbm, da_out, w_grad, grads2, b_left, b_right,
+    das, vs, ps, hs, low_buf, low_a, low_b, g_buf, outs, total, w_ref, w_flip, stats,
+    a_sem, v_sem, p_sem, h_sem, o_sem, w_sem, *talks,
 ):
     windows, length, width = da.shape
     channels = pooled.shape[2]
@@ -769,6 +852,9 @@
     lean = scale3 * inverse3 * (grads[0:1] / entries)
     flat = scale3 * (grads[1:2] / entries)
     center, inverse = center_inverse(sums2[...], entries)
+    scale = inverse * flat_row(gain2)
+    offset = ROOT * (flat_row(shift2) - center * scale)
+    scale = ROOT * scale
     stats[...] = jnp.zeros_like(stats)
     total[...] = jnp.zeros_like(total)
 
@@ -824,15 +910,15 @@
 
     def finish(slot, c):
         at, cols = lanes_of(c), lanes(c)
-        m, inv, g, s = center[:, at], inverse[:, at], gain2[at][None], shift2[at][None]
+        a, b = scale[:, at], offset[:, at]
         sums = [jnp.zeros((8, LANES), f32), jnp.zeros((8, LANES), f32)]
 
         def rows(r):
             def run():
-                normed = (ps[slot, r : r + UNIT, cols] - m) * inv
-                back = gelu_slope(normed * g + s) * g_buf[r : r + UNIT, cols]
+                q = ps[slot, r : r + UNIT, cols] * a + b
+                back = slope_scaled(q) * g_buf[r : r + UNIT, cols]
                 outs[slot, r : r + UNIT, cols] = back
-                sums[0] = sums[0] + folded(back * normed)
+                sums[0] = sums[0] + folded(back * q)
                 sums[1] = sums[1] + folded(back)
 
             return run
@@ -848,6 +934,8 @@
     w_copy.start()
     for copy in late_copies(0, 0):
         copy.start()
+    talk = Exchange(talks[: Exchange.SUMS], talks[Exchange.SUMS :])
+    greet(talk.seqs, talk.dps)
     wait_load(0)
     load(1, 1)
     for c in range(thin):
@@ -906,26 +994,37 @@
         return 0
 
     lax.fori_loop(0, tiles // 2, pair, 0)
-    for c in range(3 * thin):
-        w_grad[c] = total[:, lanes_of(c)].astype(bf16)
+    shifts = 0.5 * stats[1]
+    stats[0] = (0.5 / ROOT * stats[0] - shifts * flat_row(shift2)) / flat_row(gain2)
+    stats[1] = shifts
     o_copy(tiles - 2, 0).wait()
     o_copy(tiles - 1, 1).wait()
-
-
-def conv_two_back(da, da_sides, v, v_sides, sums3, grads3, gain3, pooled, sums2, gain2, shift2, h, weight, entries):
+    talk.start_edges((da_out,))
+    talk.start_sums(stats)
+    for c in range(3 * thin):
+        w_grad[c] = ((0.5 / ROOT) * total[:, lanes_of(c)]).astype(bf16)
+    talk.finish_edges((da_out,))
+    b_left[...] = talk.lands[0][...]
+    b_right[...] = talk.lands[1][...]
+    talk.finish_sums(grads2)
+
+
+def conv_two_back(da, da_sides, v, v_sides, sums3, grads3, gain3, pooled, sums2, gain2, shift2, h, weight, entries, number):
     windows, length, width = da.shape
     channels = pooled.shape[2]
     tile = min(512, length)
     thin, slabs = width // LANES, channels // LANES
-    return pl.pallas_call(
+    back = jax.ShapeDtypeStruct((windows, length, channels), f32)
+    got = pl.pallas_call(
         functools.partial(conv_two_back_kernel, tile, entries),
-        out_shape=(
-            jax.ShapeDtypeStruct((windows, length, channels), f32),
-            jax.ShapeDtypeStruct((2, 8, channels), f32),
+        out_shape=[
+            back,
             jax.ShapeDtypeStruct((3 * thin, channels, LANES), bf16),
-        ),
+            jax.ShapeDtypeStruct((8, channels), f32),
+        ]
+        + Exchange.edges([back]),
         in_specs=[ANY] * 6 + [VM] * 3 + [ANY] + [VM] * 3 + [ANY] * 2,
-        out_specs=(ANY, VM, VM),
+        out_specs=[ANY] + [VM] * 4,
         scratch_shapes=[
             pltpu.VMEM((2, tile + 2 * EDGE, width), f32),
             pltpu.VMEM((2, tile + 2 * EDGE, width), f32),
@@ -939,16 +1038,20 @@
             pltpu.VMEM((channels, 3 * width), f32),
             pltpu.VMEM(weight.shape, bf16),
             pltpu.VMEM((3 * width, channels), bf16),
+            pltpu.VMEM((2, 8, channels), f32),
             DMA((2,)),
             DMA((2,)),
             DMA((2,)),
             DMA((2,)),
             DMA((2,)),
             DMA,
-        ],
+        ]
+        + Exchange.scratch(channels)
+        + Exchange.edge_scratch([back]),
         name="conv_two_back",
-        **params(12 * pooled.size * width, 16 * pooled.size, pooled.size),
+        **joining(params(12 * pooled.size * width, 16 * pooled.size, pooled.size), number),
     )(da, *da_sides, v, *v_sides, sums3, grads3, gain3, pooled, sums2, gain2, shift2, h, weight)
+    return got[:3], got[3:]
 
 
 class Reduction:
@@ -1061,23 +1164,6 @@
         return Reduction(data, refs[0], refs[1:5], refs[5], refs[6])
 
 
-def greet(seqs, dps):
-    seq, dp = lax.axis_index("seq"), lax.axis_index("dp")
-    barrier = pltpu.get_barrier_semaphore()
-
-    def near(d, _):
-        pl.semaphore_signal(barrier, inc=1, device_id={"seq": lax.rem(seq + d, seqs)}, device_id_type=MESH)
-        return 0
-
-    def far(d, _):
-        pl.semaphore_signal(barrier, inc=1, device_id={"dp": lax.rem(dp + d, dps)}, device_id_type=MESH)
-        return 0
-
-    lax.fori_loop(1, seqs, near, 0)
-    lax.fori_loop(1, dps, far, 0)
-    pl.semaphore_wait(barrier, seqs - 1 + dps - 1)
-
-
 def conv_one_weigh_kernel(
     tile, entries, joined, seqs, dps, da, da_left, da_right, v, v_left, v_right, ct, ct_left, ct_right, sums2, grads2,
     gain2, s, first, two, three, low_out, w_grad, small, das, vs, cts, ss, firsts, low_buf, low_a, low_b, coef, total,
@@ -1095,7 +1181,7 @@
     lean = scale2 * inverse2 * (grads[0:1] / half_entries)
     flat = scale2 * (grads[1:2] / half_entries)
     for c in range(slabs):
-        for row, values in enumerate((scale2, lean, center2 * lean - flat)):
+        for row, values in enumerate((0.5 * scale2, lean, center2 * lean - flat)):
             coef[c, row : row + 1] = values[:, lanes_of(c)]
 
     def load(i, slot):
@@ -1232,7 +1318,7 @@
     l_copy(tiles - 1, 1).wait()
     for k in range(EARLY):
         for c in range(slabs):
-            packed[k, c] = total[k, :, lanes_of(c)].astype(bf16)
+            packed[k, c] = ((0.5 / ROOT) * total[k, :, lanes_of(c)]).astype(bf16)
     g_copy = pltpu.make_async_copy(packed, w_grad, g_sem)
     g_copy.start()
     if joined:
@@ -1259,9 +1345,7 @@
     joined = Reduction.fits(rows)
     estimate = params(4 * EARLY * da.size * channels, 24 * da.size, 0)
     if joined:
-        estimate["compiler_params"] = pltpu.CompilerParams(
-            vmem_limit_bytes=VMEM_LIMIT, collective_id=number, has_side_effects=True
-        )
+        estimate = joining(estimate, number)
     low, parts, small = pl.pallas_call(
         functools.partial(conv_one_weigh_kernel, tile, entries, joined, lax.axis_size("seq"), lax.axis_size("dp")),
         out_shape=(
@@ -1297,8 +1381,8 @@
 
 
 def conv_one_spread_kernel(
-    tile, entries, joined, seqs, dps, low, x, sums1, gain1, shift1, w_hbm, s, parts, da_out, stats, w_grad,
-    lows, xs, g_buf, outs, coef, w_ref, total, ss, ls, data, l_sem, x_sem, o_sem, w_sem, d_sem, t_sem, *reduction,
+    tile, entries, joined, low, x, sums1, gain1, shift1, w_hbm, s, parts, da_out, w_grad, grads1,
+    lows, xs, g_buf, outs, coef, w_ref, total, ss, ls, data, stats, l_sem, x_sem, o_sem, w_sem, d_sem, t_sem, *refs,
 ):
     windows, length, _ = low.shape
     channels = x.shape[2]
@@ -1307,8 +1391,10 @@
     walk = Walk(windows, length, tile)
     tiles = walk.count
     center, inverse = center_inverse(sums1[...], entries)
+    scale = inverse * flat_row(gain1)
+    offset = flat_row(shift1) - center * scale
     for c in range(slabs):
-        for row, values in enumerate((center, inverse, flat_row(gain1), flat_row(shift1))):
+        for row, values in enumerate((ROOT * scale, ROOT * offset)):
             coef[c, row : row + 1] = values[:, lanes_of(c)]
     stats[...] = jnp.zeros_like(stats)
 
@@ -1336,10 +1422,11 @@
 
     d_copy = pltpu.make_async_copy(parts, data.at[pl.ds(0, EARLY * slabs // 2)], d_sem)
     d_copy.start()
-    for copy in t_copies(0, 0):
-        copy.start()
-    if joined:
-        greet(seqs, dps)
+    for g in range(AHEAD):
+        for copy in t_copies(g, g):
+            copy.start()
+    talk, reduction = Exchange(refs[: Exchange.SUMS]), refs[Exchange.SUMS :]
+    greet(talk.seqs, talk.dps)
     d_copy.wait()
     l_copy(0, 0).start()
     w_copy = pltpu.make_async_copy(w_hbm, w_ref, w_sem)
@@ -1358,13 +1445,13 @@
         return first + count * part // tiles, first + count * (part + 1) // tiles
 
     def weigh(g, _):
-        slot = g % 2
+        slot = g % (AHEAD + 1)
         for copy in t_copies(g, slot):
             copy.wait()
 
-        @pl.when(g + 1 < late)
+        @pl.when(g + AHEAD < late)
         def _():
-            for copy in t_copies(g + 1, 1 - slot):
+            for copy in t_copies(g + AHEAD, (g + AHEAD) % (AHEAD + 1)):
                 copy.start()
 
         @pl.when(g % tiles == 0)
@@ -1379,7 +1466,7 @@
         def _():
             for c in range(slabs):
                 at = slice((c % 2) * channels, (c % 2 + 1) * channels)
-                data[(EARLY + g // tiles) * triple + c // 2, at] = total[:, lanes_of(c)].astype(bf16)
+                data[(EARLY + g // tiles) * triple + c // 2, at] = ((0.5 / ROOT) * total[:, lanes_of(c)]).astype(bf16)
 
         if joined:
             def take(t, _):
@@ -1395,16 +1482,16 @@
 
     def finish(slot, c):
         cols = lanes(c)
-        m, inv, g, sh = (coef[c, row : row + 1] for row in range(4))
+        a, b = coef[c, 0:1], coef[c, 1:2]
         held = [jnp.zeros((8, LANES), f32), jnp.zeros((8, LANES), f32)]
 
         def rows(r):
             def run():
-                normed = (xs[slot, r : r + UNIT, cols] - m) * inv
+                q = xs[slot, r : r + UNIT, cols] * a + b
                 incoming = g_buf[slot, c, EDGE + r : EDGE + r + UNIT] + g_buf[slot, c, EDGE + r - 1 : EDGE + r - 1 + UNIT]
-                back = gelu_slope(normed * g + sh) * incoming
+                back = slope_scaled(q) * incoming
                 outs[slot, r : r + UNIT, cols] = back.astype(bf16)
-                held[0] = held[0] + folded(back * normed)
+                held[0] = held[0] + folded(back * q)
                 held[1] = held[1] + folded(back)
 
             return run
@@ -1414,6 +1501,11 @@
             stats[1, :, cols] += held[1]
 
         return [rows(r) for r in range(0, span, UNIT)] + [close]
+
+    def settle():
+        shifts = 0.5 * stats[1]
+        stats[0] = (0.5 / ROOT * stats[0] - shifts * flat_row(shift1)) / flat_row(gain1)
+        stats[1] = shifts
 
     def spread(slot, n):
         at = lanes(n, 256)
@@ -1492,6 +1584,8 @@
 
     lax.fori_loop(0, tiles // 2, pair, 0)
     turn(tiles, 0, True)
+    settle()
+    talk.start_sums(stats)
     o_copy(tiles - 2, 0).wait()
     o_copy(tiles - 1, 1).wait()
     if joined:
@@ -1502,6 +1596,7 @@
         lax.fori_loop(4 * triple + tiles * (channels // 256), sharing.steps, more, 0)
     d_copy = pltpu.make_async_copy(sharing.done if joined else data, w_grad, d_sem)
     d_copy.start()
+    talk.finish_sums(grads1)
     d_copy.wait()
 
 
@@ -1514,19 +1609,15 @@
     parts = parts.reshape(EARLY * slabs // 2, rows, LANES)
     joined = Reduction.fits(rows)
     estimate = params(10 * low.size * channels // 3, 12 * x.size, x.size)
-    if joined:
-        estimate["compiler_params"] = pltpu.CompilerParams(
-            vmem_limit_bytes=VMEM_LIMIT, collective_id=number, has_side_effects=True
-        )
-    da, stats, grad = pl.pallas_call(
-        functools.partial(conv_one_spread_kernel, tile, entries, joined, lax.axis_size("seq"), lax.axis_size("dp")),
+    da, grad, grads1 = pl.pallas_call(
+        functools.partial(conv_one_spread_kernel, tile, entries, joined),
         out_shape=(
             jax.ShapeDtypeStruct((windows, 2 * length, channels), bf16),
-            jax.ShapeDtypeStruct((2, 8, channels), f32),
             jax.ShapeDtypeStruct((chunks, rows, LANES), bf16),
+            jax.ShapeDtypeStruct((8, channels), f32),
         ),
         in_specs=[ANY] * 2 + [VM] * 3 + [ANY] * 3,
-        out_specs=(ANY, VM, ANY),
+        out_specs=(ANY, ANY, VM),
         scratch_shapes=[
             pltpu.VMEM((2, tile, 3 * channels), bf16),
             pltpu.VMEM((2, 2 * tile, channels), f32),
@@ -1535,23 +1626,25 @@
             pltpu.VMEM((slabs, 8, LANES), f32),
             pltpu.VMEM(weight.shape, bf16),
             pltpu.VMEM((channels, channels), f32),
-            pltpu.VMEM((2, tile, channels), bf16),
-            pltpu.VMEM((2, tile, channels), bf16),
+            pltpu.VMEM((AHEAD + 1, tile, channels), bf16),
+            pltpu.VMEM((AHEAD + 1, tile, channels), bf16),
             pltpu.VMEM((chunks, rows, LANES), bf16),
+            pltpu.VMEM((2, 8, channels), f32),
             DMA((2,)),
             DMA((2,)),
             DMA((2,)),
             DMA,
             DMA,
-            DMA((2, 2)),
+            DMA((AHEAD + 1, 2)),
         ]
+        + Exchange.scratch(channels)
         + (Reduction.scratch(chunks, rows) if joined else []),
         name="conv_one_spread",
-        **estimate,
+        **joining(estimate, number),
     )(low, x, sums1, gain1, shift1, weight, s, parts)
     if not joined:
         grad = lax.psum(grad, ("dp", "seq"))
-    return da, stats, grad
+    return da, grad, grads1
 
 
 def widen_kernel(one, small, grads1, grads2, grads3, one_out, two_out, three_out, *vectors):
@@ -1615,12 +1708,12 @@
         m, s, l, f = center[:, at], scale[:, at], lean[:, at], flat[:, at]
         for r in range(0, x.shape[1], 128):
             rows = slice(r, r + 128)
-            out[0, rows, cols] = da[0, rows, cols].astype(f32) * s - (x[0, rows, cols] - m) * l - f
+            out[0, rows, cols] = da[0, rows, cols].astype(f32) * (0.5 * s) - (x[0, rows, cols] - m) * l - f
 
 
 def input_back(x, da, sums, grads, gain, entries):
     windows, length, channels = x.shape
-    tile = min(512, length)
+    tile = min(1024, length)
     per = length // tile
     rows = pl.BlockSpec((1, tile, channels), lambda i: (i // per, i % per, 0))
     whole = lambda i: (0, 0)
@@ -1657,30 +1750,27 @@
     windows, length, channels = inputs.shape
     entries = float(windows * length * lax.axis_size("dp") * lax.axis_size("seq"))
     half = entries / 2
-    sums1, (x_left, x_right, c_left, c_right) = exchange(input_sums(inputs), [inputs, cotangent], 0)
-    pooled, s, first, stats = conv_one_forward(
-        inputs, x_left, x_right, sums1, gain_one, shift_one, conv_one, entries
+    (pooled, s, first, sums1, sums2), c_sides, p_sides = conv_one_forward(
+        inputs, cotangent, gain_one, shift_one, conv_one, entries, 0
     )
-    sums2, p_sides = exchange(stats, [pooled], 1)
-    narrow, hidden_two, stats = conv_two_forward(pooled, *p_sides, sums2, gain_two, shift_two, conv_two, half)
-    sums3, n_sides = exchange(stats, [narrow], 2)
+    (narrow, hidden_two, sums3), n_sides = conv_two_forward(
+        pooled, *p_sides, sums2, gain_two, shift_two, conv_two, half, 1
+    )
     outputs, da3, stats, three_grad = conv_three_both(
         narrow, cotangent, pooled, sums3, gain_three, shift_three, conv_three, half
     )
-    grads3, a_sides = exchange(stats, [da3], 3)
-    da2, stats, two_grad = conv_two_back(
+    grads3, a_sides = exchange(stats, [da3], 2)
+    (da2, two_grad, grads2), b_sides = conv_two_back(
         da3, a_sides, narrow, n_sides, sums3, grads3, gain_three, pooled, sums2, gain_two, shift_two,
-        hidden_two, conv_two, half,
+        hidden_two, conv_two, half, 3,
     )
-    grads2, b_sides = exchange(stats, [da2], 4)
     low, parts, small = conv_one_weigh(
-        da2, b_sides, pooled, p_sides, cotangent, (c_left, c_right), sums2, grads2, gain_two, s, first,
-        two_grad, three_grad, entries, 7,
+        da2, b_sides, pooled, p_sides, cotangent, c_sides, sums2, grads2, gain_two, s, first,
+        two_grad, three_grad, entries, 4,
     )
-    da1, stats, one_grad = conv_one_spread(
-        low, inputs, sums1, gain_one, shift_one, conv_one, s, parts, entries, 6
+    da1, one_grad, grads1 = conv_one_spread(
+        low, inputs, sums1, gain_one, shift_one, conv_one, s, parts, entries, 5
     )
-    grads1, _ = exchange(stats, [], 5)
     input_grad = input_back(inputs, da1, sums1, grads1, gain_one, entries)
     small_grads = widen(one_grad, small, conv_two.shape, conv_three.shape, (grads1, grads2, grads3))
     return (outputs, input_grad, *small_grads)

time: 371 us -> 330 us (0.89)
  Pallas kernels: 369 us -> 329 us
    pallas_call x7 -> x1, Pallas kernels: 80.3 us -> 10.1 us  [exchange(): pl.pallas_call(functools.partial(exchange_kernel, len(arrays)), out_shape...]
    pallas_call x1, Pallas kernels: 42.5 us -> 67.1 us  [conv_one_forward(): pl.pallas_call(functools.partial(conv_one_kernel, tile, entries), out_sha...]
    pallas_call x1, Pallas kernels: 22.7 us -> 29.4 us  [conv_two_forward(): pl.pallas_call(functools.partial(conv_two_kernel, tile, entries), out_sha...]
    pallas_call x1, Pallas kernels: 30.5 us -> 37.1 us  [conv_two_back(): pl.pallas_call(functools.partial(conv_two_back_kernel, tile, entries), ou...]
    pallas_call x1, Pallas kernels: 26.2 us -> 22.2 us  [input_back(): pl.pallas_call(functools.partial(last_kernel, entries), grid=(windows * p...]
where the time goes in v3:
time: 330 us; the launch traced here: 329 us
  Pallas kernels  329 us (100%)
    pallas_call x1, Pallas kernels, conv_one_spread(): pl.pallas_call(functools.partial(conv_one_spread_kernel, tile, entries, j...  78.7 us
    pallas_call x1, Pallas kernels, conv_one_forward(): pl.pallas_call(functools.partial(conv_one_kernel, tile, entries), out_sha...  67.1 us
    pallas_call x1, Pallas kernels, conv_one_weigh(): pl.pallas_call(functools.partial(conv_one_weigh_kernel, tile, entries, jo...  49.9 us
    pallas_call x1, Pallas kernels, conv_two_back(): pl.pallas_call(functools.partial(conv_two_back_kernel, tile, entries), ou...  37.1 us
    pallas_call x1, Pallas kernels, conv_two_forward(): pl.pallas_call(functools.partial(conv_two_kernel, tile, entries), out_sha...  29.4 us
    pallas_call x1, Pallas kernels, conv_three_both(): pl.pallas_call(functools.partial(conv_three_kernel, entries), grid=(windo...  23.9 us
    pallas_call x1, Pallas kernels, input_back(): pl.pallas_call(functools.partial(last_kernel, entries), grid=(windows * p...  22.2 us
    pallas_call x1, Pallas kernels, widen(): pl.pallas_call(widen_kernel, grid=(5,), out_shape=[jax.ShapeDtypeStruct((...  10.2 us

profile of v3, /device:TPU:0, one launch (start us, length us, event | category | flops | bytes accessed | tf_op | source)
XLA Modules:
  0.0 329.2 jit_solution(5071484342756658297)
XLA Ops:
  0.6 67.1 %conv_one_forward.1 = (f32[2,2048,768]{2,1,0:T(8,128)}, bf16[2,2,2048,768]{3,2,1,0:T(8,128)(2,1)}, bf16[2,16,768]{2,1,0:T(8,128)(2,1)}, f32[8,768]{1,0:T(8,128)}...) custom-call(f32[2,4096,768]{2,1,0:T(8,128)} %x.5, ...), custom_call_target="tpu_custom_call" | custom-call | flops 24159191040 | bytes 75497472 | tf_op jit(solution)/shard_map/conv_one_forward/pallas_call | solution.py:552
  67.7 29.4 %conv_two_forward.1 = (f32[2,2048,384]{2,1,0:T(8,128)}, bf16[2,2048,768]{2,1,0:T(8,128)(2,1)}, f32[8,384]{1,0:T(8,128)}, f32[2,8,384]{2,1,0:T(8,128)}, f32[2,8,384]{2,1,0:T(8,128)}) custom-call(f32[2,2048,768]{2,1,0:T(8,128)} %get-tuple-element.52.v.pooled, f32[2,8,768]{2,1,0:T(8,128)} %get-tuple-element.53.left.v_left, ...), custom_call_target="tpu_custom_call" | custom-call | flops 7247757312 | bytes 25165824 | tf_op jit(solution)/shard_map/conv_two_forward/pallas_call | solution.py:724
  97.1 23.9 %conv_three_both.1 = (f32[2,2048,768]{2,1,0:T(8,128)}, f32[2,2048,384]{2,1,0:T(8,128)}, f32[2,8,384]{2,1,0:T(8,128)}, bf16[6,384,128]{2,1,0:T(8,128)(2,1)}) custom-call(f32[2,2048,384]{2,1,0:T(8,128)} %get-tuple-element.56.narrow.v, f32[2,2048,768]{2,1,0:T(8,128)} %ct.1, f32[2,2048,768]{2,1,0:T(8,128)} %get-tuple-element.52.v.pooled, ...), custom_call_target="tpu_custom_call" | custom-call | flops 7247757312 | bytes 37748736 | tf_op jit(solution)/shard_map/conv_three_both/pallas_call | solution.py:802
  121.0 10.1 %exchange_2.1 = (f32[8,384]{1,0:T(8,128)}, f32[2,8,384]{2,1,0:T(8,128)}, f32[2,8,384]{2,1,0:T(8,128)}) custom-call(f32[2,8,384]{2,1,0:T(8,128)} %get-tuple-element.60.refs_0_, f32[2,2048,384]{2,1,0:T(8,128)} %get-tuple-element.59.refs_1_.da), custom_call_target="tpu_custom_call" | custom-call | tf_op jit(solution)/shard_map/exchange_2/pallas_call | solution.py:303
  131.1 37.1 %conv_two_back.1 = (f32[2,2048,768]{2,1,0:T(8,128)}, bf16[9,768,128]{2,1,0:T(8,128)(2,1)}, f32[8,768]{1,0:T(8,128)}, f32[2,8,768]{2,1,0:T(8,128)}, f32[2,8,768]{2,1,0:T(8,128)}) custom-call(f32[2,2048,384]{2,1,0:T(8,128)} %get-tuple-element.59.refs_1_.da, f32[2,8,384]{2,1,0:T(8,128)} %get-tuple-element.61.da_left, f32[2,8,384]{2,1,0:T(8,128)} %get-tuple-element.62.da_right, ...), custom_call_target="tpu_custom_call" | custom-call | flops 14495514624 | bytes 50331648 | tf_op jit(solution)/shard_map/conv_two_back/pallas_call | solution.py:1018
  168.2 49.9 %conv_one_weigh.1 = (bf16[2,2048,2304]{2,1,0:T(8,128)(2,1)}, bf16[3,6,768,128]{3,2,1,0:T(8,128)(2,1)}, bf16[6,1536,128]{2,1,0:T(8,128)(2,1)}) custom-call(f32[2,2048,768]{2,1,0:T(8,128)} %get-tuple-element.67.da, f32[2,8,768]{2,1,0:T(8,128)} %get-tuple-element.68.da_left, f32[2,8,768]{2,1,0:T(8,128)} %get-tuple-element.69.da_right, ...), custom_call_target="tpu_custom_call" | custom-call | flops 28991029248 | bytes 75497472 | tf_op jit(solution)/shard_map/conv_one_weigh/pallas_call | solution.py:1349
  218.1 78.7 %conv_one_spread.1 = (bf16[2,4096,768]{2,1,0:T(8,128)(2,1)}, bf16[15,1536,128]{2,1,0:T(8,128)(2,1)}, f32[8,768]{1,0:T(8,128)}) custom-call(bf16[2,2048,2304]{2,1,0:T(8,128)(2,1)} %get-tuple-element.77.low, f32[2,4096,768]{2,1,0:T(8,128)} %x.5, f32[8,768]{1,0:T(8,128)} %get-tuple-element.78.sums1.sums, f32[768]{0:T(1024)} %gain.7, f32[768]{0:T(1024)} %shift1.1, ...), custom_call_target="tpu_custom_call" | custom-call | flops 24159191040 | bytes 75497472 | tf_op jit(solution)/shard_map/conv_one_spread/pallas_call | solution.py:1612
  296.8 10.2 %widen.1 = (f32[5,768,768]{2,1,0:T(8,128)}, f32[3,768,384]{2,1,0:T(8,128)}, f32[384,768]{1,0:T(8,128)}, f32[768]{0:T(1024)}, f32[768]{0:T(1024)}, /*index=5*/f32...) custom-call(bf16[5,6,768,128]{3,2,1,0:T(8,128)(2,1)} %bitcast.5, bf16[9216,128]{1,0:T(8,128)(2,1)} %bitcast.6, ...), custom_call_target="tpu_custom_call" | custom-call | bytes 17694720 | tf_op jit(solution)/shard_map/widen/pallas_call | solution.py:1678
  307.0 22.2 %input_back.1 = f32[2,4096,768]{2,1,0:T(8,128)} custom-call(f32[2,4096,768]{2,1,0:T(8,128)} %x.5, bf16[2,4096,768]{2,1,0:T(8,128)(2,1)} %get-tuple-element.80.da, f32[8,768]{1,0:T(8,128)} %get-tuple-element.78.sums1.sums, f32[8,768]{1,0:T(8,128)} %get-tuple-element.81.grads.grads1, f32[768]{0:T(1024)} %gain.7), custom_call_target="tpu_custom_call" | custom-call | bytes 62914560 | tf_op jit(solution)/shard_map/input_back/pallas_call | solution.py:1720

commit v4 on v3

--- a/solution.py
+++ b/solution.py
@@ -20,6 +20,7 @@
 VMEM_LIMIT = 60 << 20
 EARLY = 3
 AHEAD = 3
+SLOTS = 3
 NN = (((1,), (0,)), ((), ()))
 NT = (((1,), (1,)), ((), ()))
 TN = (((0,), (0,)), ((), ()))
@@ -282,34 +283,6 @@
 
 def lanes_of(c):
     return slice(c * LANES, (c + 1) * LANES)
-
-
-def exchange_kernel(arrays, *refs):
-    stats, sources, sums = refs[0], refs[1 : 1 + arrays], refs[1 + arrays]
-    outs, scratch = refs[2 + arrays : 2 + 3 * arrays], refs[2 + 3 * arrays :]
-    talk = Exchange(scratch[: Exchange.SUMS], scratch[Exchange.SUMS :])
-    greet(talk.seqs, talk.dps)
-    talk.start_edges(sources)
-    talk.start_sums(stats)
-    talk.finish_edges(sources)
-    for out, land in zip(outs, talk.lands):
-        out[...] = land[...]
-    talk.finish_sums(sums)
-
-
-def exchange(stats, arrays, number):
-    channels = stats.shape[2]
-    edges = Exchange.edges(arrays)
-    got = pl.pallas_call(
-        functools.partial(exchange_kernel, len(arrays)),
-        out_shape=[jax.ShapeDtypeStruct((8, channels), f32)] + edges,
-        in_specs=[VM] + [ANY] * len(arrays),
-        out_specs=[VM] * (1 + len(edges)),
-        scratch_shapes=Exchange.scratch(channels) + Exchange.edge_scratch(arrays),
-        compiler_params=pltpu.CompilerParams(collective_id=number, has_side_effects=True),
-        name=f"exchange_{number}",
-    )(stats, *arrays)
-    return got[0], got[1:]
 
 
 def joining(estimate, number):
@@ -600,8 +573,11 @@
     scale, offset = ROOT * scale, ROOT * offset
     stats[...] = jnp.zeros_like(stats)
 
-    def load(i, slot):
-        walk.fetch(i, v, left, right, vs.at[slot], v_sem.at[slot])
+    def load(i):
+        walk.fetch(i, v, left, right, vs.at[i % SLOTS], v_sem.at[i % SLOTS])
+
+    def wait_load(i):
+        wait_for(vs.at[i % SLOTS], v_sem.at[i % SLOTS])
 
     def h_copy(i, slot):
         w, _ = walk.where(i)
@@ -615,7 +591,7 @@
 
     def activate(i, slot, c):
         a, b = scale[:, lanes_of(c)], offset[:, lanes_of(c)]
-        src, dst, cols = vs.at[slot], lhs[slot], lanes(c)
+        src, dst, cols = vs.at[i % SLOTS], lhs[slot], lanes(c)
 
         def ends():
             head = gelu_scaled(src[0:EDGE, cols] * a + b)
@@ -643,13 +619,13 @@
             units += [rows(r), taps(r - UNIT)]
         return units + [taps(tile - UNIT)]
 
-    load(0, 0)
+    for i in range(min(SLOTS, tiles)):
+        load(i)
     talk = Exchange(talks[: Exchange.SUMS], talks[Exchange.SUMS :])
     greet(talk.seqs, talk.dps)
-    wait_for(vs.at[0], v_sem.at[0])
+    wait_load(0)
     w_copy = pltpu.make_async_copy(w_hbm, w_ref, w_sem)
     w_copy.start()
-    load(1, 1)
     for c in range(slabs):
         for unit in activate(0, 0, c):
             unit()
@@ -663,11 +639,11 @@
 
             @pl.when(i + 1 < tiles)
             def _():
-                wait_for(vs.at[other], v_sem.at[other])
-
-            @pl.when(i + 2 < tiles)
-            def _():
-                load(i + 2, slot)
+                wait_load(i + 1)
+
+            @pl.when(jnp.logical_and(i >= 1, i + SLOTS - 1 < tiles))
+            def _():
+                load(i + SLOTS - 1)
 
             @pl.when(i >= 1)
             def _():
@@ -732,14 +708,14 @@
         in_specs=[ANY, ANY, ANY, VM, VM, VM, ANY],
         out_specs=[ANY, ANY, VM, VM, VM],
         scratch_shapes=[
-            pltpu.VMEM((2, tile + 2 * EDGE, channels), f32),
+            pltpu.VMEM((SLOTS, tile + 2 * EDGE, channels), f32),
             pltpu.VMEM((slabs, tile + 2 * EDGE, LANES), f32),
             pltpu.VMEM((tile, 3 * channels), bf16),
             pltpu.VMEM((tile, 3 * channels), bf16),
             pltpu.VMEM((2, tile, width), f32),
             pltpu.VMEM((3 * channels, width), bf16),
             pltpu.VMEM((2, 8, width), f32),
-            DMA((2,)),
+            DMA((SLOTS,)),
             DMA((2,)),
             DMA((2,)),
             DMA,
@@ -834,234 +810,14 @@
     )(narrow, cotangent, pooled, sums, gain, shift, weight)
 
 
-def conv_two_back_kernel(
-    tile, entries, da, da_left, da_right, v, v_left, v_right, sums3, grads3, gain3, pooled, sums2, gain2, shift2,
-    h, w_hbm, da_out, w_grad, grads2, b_left, b_right,
-    das, vs, ps, hs, low_buf, low_a, low_b, g_buf, outs, total, w_ref, w_flip, stats,
-    a_sem, v_sem, p_sem, h_sem, o_sem, w_sem, *talks,
-):
-    windows, length, width = da.shape
-    channels = pooled.shape[2]
-    thin, slabs = width // LANES, channels // LANES
-    walk = Walk(windows, length, tile)
-    tiles = walk.count
-    low = (low_a, low_b)
-    center3, inverse3 = center_inverse(sums3[...], entries)
-    grads = grads3[...]
-    scale3 = inverse3 * flat_row(gain3)
-    lean = scale3 * inverse3 * (grads[0:1] / entries)
-    flat = scale3 * (grads[1:2] / entries)
-    center, inverse = center_inverse(sums2[...], entries)
-    scale = inverse * flat_row(gain2)
-    offset = ROOT * (flat_row(shift2) - center * scale)
-    scale = ROOT * scale
-    stats[...] = jnp.zeros_like(stats)
-    total[...] = jnp.zeros_like(total)
-
-    def load(i, slot):
-        walk.fetch(i, da, da_left, da_right, das.at[slot], a_sem.at[slot])
-        walk.fetch(i, v, v_left, v_right, vs.at[slot], v_sem.at[slot])
-
-    def wait_load(slot):
-        wait_for(das.at[slot], a_sem.at[slot])
-        wait_for(vs.at[slot], v_sem.at[slot])
-
-    def late_copies(i, slot):
-        w, _ = walk.where(i)
-        return (
-            pltpu.make_async_copy(pooled.at[w, walk.rows(i)], ps.at[slot], p_sem.at[slot]),
-            pltpu.make_async_copy(h.at[w, walk.rows(i)], hs.at[slot], h_sem.at[slot]),
-        )
-
-    def o_copy(i, slot):
-        w, _ = walk.where(i)
-        return pltpu.make_async_copy(outs.at[slot], da_out.at[w, walk.rows(i)], o_sem.at[slot])
-
-    def lower(i, slot, c):
-        at, cols = lanes_of(c), lanes(c)
-        m, s, l, f = center3[:, at], scale3[:, at], lean[:, at], flat[:, at]
-        dst = low[slot]
-
-        def value(q, size):
-            return das[slot, q : q + size, cols] * s - (vs[slot, q : q + size, cols] - m) * l - f
-
-        def ends():
-            low_buf[c, 0:EDGE] = jnp.where(walk.hide_left(i), 0.0, value(0, EDGE))
-            low_buf[c, EDGE + tile : 2 * EDGE + tile] = jnp.where(walk.hide_right(i), 0.0, value(EDGE + tile, EDGE))
-
-        def rows(r):
-            def run():
-                low_buf[c, EDGE + r : EDGE + r + UNIT] = value(EDGE + r, UNIT)
-
-            return run
-
-        def taps(r):
-            def run():
-                for tap in range(3):
-                    q = EDGE + r - 5 * (tap - 1)
-                    dst[r : r + UNIT, lanes(tap * thin + c)] = low_buf[c, q : q + UNIT].astype(bf16)
-
-            return run
-
-        units = [ends, rows(0)]
-        for r in range(UNIT, tile, UNIT):
-            units += [rows(r), taps(r - UNIT)]
-        return units + [taps(tile - UNIT)]
-
-    def finish(slot, c):
-        at, cols = lanes_of(c), lanes(c)
-        a, b = scale[:, at], offset[:, at]
-        sums = [jnp.zeros((8, LANES), f32), jnp.zeros((8, LANES), f32)]
-
-        def rows(r):
-            def run():
-                q = ps[slot, r : r + UNIT, cols] * a + b
-                back = slope_scaled(q) * g_buf[r : r + UNIT, cols]
-                outs[slot, r : r + UNIT, cols] = back
-                sums[0] = sums[0] + folded(back * q)
-                sums[1] = sums[1] + folded(back)
-
-            return run
-
-        def close():
-            stats[0, :, cols] += sums[0]
-            stats[1, :, cols] += sums[1]
-
-        return [rows(r) for r in range(0, tile, UNIT)] + [close]
-
-    load(0, 0)
-    w_copy = pltpu.make_async_copy(w_hbm, w_ref, w_sem)
-    w_copy.start()
-    for copy in late_copies(0, 0):
-        copy.start()
-    talk = Exchange(talks[: Exchange.SUMS], talks[Exchange.SUMS :])
-    greet(talk.seqs, talk.dps)
-    wait_load(0)
-    load(1, 1)
-    for c in range(thin):
-        for unit in lower(0, 0, c):
-            unit()
-    w_copy.wait()
-    for k in range(3):
-        w_flip[k * width : (k + 1) * width] = w_ref[k].T
-
-    def pair(j, _):
-        for slot in range(2):
-            i = 2 * j + slot
-            other = 1 - slot
-
-            @pl.when(i + 1 < tiles)
-            def _():
-                wait_load(other)
-                for copy in late_copies(i + 1, other):
-                    copy.start()
-
-            @pl.when(i + 2 < tiles)
-            def _():
-                load(i + 2, slot)
-
-            for copy in late_copies(i, slot):
-                copy.wait()
-
-            @pl.when(i >= 2)
-            def _():
-                o_copy(i - 2, slot).wait()
-
-            def back(n):
-                def run():
-                    cols = lanes(n, 256)
-                    g_buf[:, cols] = dot(low[slot][...], w_flip[:, cols])
-
-                return run
-
-            def weigh(n):
-                def run():
-                    at = slice(n * 256, (n + 1) * 256)
-                    total[at] += dot(hs[slot, :, at], low[slot][...], TN)
-
-                return run
-
-            units = []
-            for c in range(thin):
-                units += lower(i + 1, other, c)
-            interleave([back(n) for n in range(channels // 256)], units)
-            units = []
-            for c in range(slabs):
-                units += finish(slot, c)
-            interleave([weigh(n) for n in range(channels // 256)], units)
-            o_copy(i, slot).start()
-
-        return 0
-
-    lax.fori_loop(0, tiles // 2, pair, 0)
-    shifts = 0.5 * stats[1]
-    stats[0] = (0.5 / ROOT * stats[0] - shifts * flat_row(shift2)) / flat_row(gain2)
-    stats[1] = shifts
-    o_copy(tiles - 2, 0).wait()
-    o_copy(tiles - 1, 1).wait()
-    talk.start_edges((da_out,))
-    talk.start_sums(stats)
-    for c in range(3 * thin):
-        w_grad[c] = ((0.5 / ROOT) * total[:, lanes_of(c)]).astype(bf16)
-    talk.finish_edges((da_out,))
-    b_left[...] = talk.lands[0][...]
-    b_right[...] = talk.lands[1][...]
-    talk.finish_sums(grads2)
-
-
-def conv_two_back(da, da_sides, v, v_sides, sums3, grads3, gain3, pooled, sums2, gain2, shift2, h, weight, entries, number):
-    windows, length, width = da.shape
-    channels = pooled.shape[2]
-    tile = min(512, length)
-    thin, slabs = width // LANES, channels // LANES
-    back = jax.ShapeDtypeStruct((windows, length, channels), f32)
-    got = pl.pallas_call(
-        functools.partial(conv_two_back_kernel, tile, entries),
-        out_shape=[
-            back,
-            jax.ShapeDtypeStruct((3 * thin, channels, LANES), bf16),
-            jax.ShapeDtypeStruct((8, channels), f32),
-        ]
-        + Exchange.edges([back]),
-        in_specs=[ANY] * 6 + [VM] * 3 + [ANY] + [VM] * 3 + [ANY] * 2,
-        out_specs=[ANY] + [VM] * 4,
-        scratch_shapes=[
-            pltpu.VMEM((2, tile + 2 * EDGE, width), f32),
-            pltpu.VMEM((2, tile + 2 * EDGE, width), f32),
-            pltpu.VMEM((2, tile, channels), f32),
-            pltpu.VMEM((2, tile, channels), bf16),
-            pltpu.VMEM((thin, tile + 2 * EDGE, LANES), f32),
-            pltpu.VMEM((tile, 3 * width), bf16),
-            pltpu.VMEM((tile, 3 * width), bf16),
-            pltpu.VMEM((tile, channels), f32),
-            pltpu.VMEM((2, tile, channels), f32),
-            pltpu.VMEM((channels, 3 * width), f32),
-            pltpu.VMEM(weight.shape, bf16),
-            pltpu.VMEM((3 * width, channels), bf16),
-            pltpu.VMEM((2, 8, channels), f32),
-            DMA((2,)),
-            DMA((2,)),
-            DMA((2,)),
-            DMA((2,)),
-            DMA((2,)),
-            DMA,
-        ]
-        + Exchange.scratch(channels)
-        + Exchange.edge_scratch([back]),
-        name="conv_two_back",
-        **joining(params(12 * pooled.size * width, 16 * pooled.size, pooled.size), number),
-    )(da, *da_sides, v, *v_sides, sums3, grads3, gain3, pooled, sums2, gain2, shift2, h, weight)
-    return got[:3], got[3:]
-
-
 class Reduction:
     STAGES = 8
-    LAG = 3
-
-    def __init__(self, data, done, lands, send, recv):
+
+    def __init__(self, data, done, lands, send, recv, lag):
         self.data, self.done, self.lands, self.send, self.recv = data, done, lands, send, recv
         self.chunks, self.rows = data.shape[0], data.shape[1]
-        self.steps = self.chunks + self.LAG * self.STAGES
+        self.lag = lag
+        self.steps = self.chunks + lag * self.STAGES
         self.planes = lax.axis_size("dp") // 4
         seq, dp = lax.axis_index("seq"), lax.axis_index("dp")
         self.seq, self.dp = seq, dp
@@ -1137,7 +893,7 @@
 
     def step(self, t):
         for stage in range(self.STAGES, -1, -1):
-            c = t - self.LAG * stage
+            c = t - self.lag * stage
 
             @pl.when(jnp.logical_and(c >= 0, c < self.chunks))
             def _():
@@ -1160,39 +916,275 @@
         return [pltpu.VMEM(shape, bf16) for shape in shapes] + [DMA((chunks, copies)), DMA((chunks, copies))]
 
     @staticmethod
-    def of(data, refs):
-        return Reduction(data, refs[0], refs[1:5], refs[5], refs[6])
-
-
-def conv_one_weigh_kernel(
-    tile, entries, joined, seqs, dps, da, da_left, da_right, v, v_left, v_right, ct, ct_left, ct_right, sums2, grads2,
-    gain2, s, first, two, three, low_out, w_grad, small, das, vs, cts, ss, firsts, low_buf, low_a, low_b, coef, total,
-    packed, data, a_sem, v_sem, c_sem, s_sem, f_sem, l_sem, g_sem, d_sem, *reduction,
+    def of(data, refs, lag):
+        return Reduction(data, refs[0], refs[1:5], refs[5], refs[6], lag)
+
+
+def conv_two_back_kernel(
+    tile, entries, joined, da, stats3, v, v_left, v_right, sums3, gain3, pooled, p_left, p_right, sums2, gain2, shift2,
+    h, w_hbm, ct, ct_left, ct_right, s, first, three, da_out, low_out, w_grad, small, grads3, grads2,
+    das, vs, hs, low_buf, low_a, low_b, total, w_ref, w_flip, stats, wide, wide_buf, wide_a, wide_b, ss, firsts, coef,
+    taps, packed, data, a_sem, v_sem, p_sem, h_sem, o_sem, w_sem, r_sem, s_sem, f_sem, l_sem, g_sem, d_sem, t_sem, *refs,
 ):
-    windows, length, channels = da.shape
-    slabs = channels // LANES
+    windows, length, width = da.shape
+    channels = pooled.shape[2]
+    thin, slabs = width // LANES, channels // LANES
     walk = Walk(windows, length, tile)
     tiles = walk.count
     low = (low_a, low_b)
-    half_entries = entries / 2
-    center2, inverse2 = center_inverse(sums2[...], half_entries)
-    grads = grads2[...]
-    scale2 = 0.5 * inverse2 * flat_row(gain2)
-    lean = scale2 * inverse2 * (grads[0:1] / half_entries)
-    flat = scale2 * (grads[1:2] / half_entries)
-    for c in range(slabs):
-        for row, values in enumerate((0.5 * scale2, lean, center2 * lean - flat)):
-            coef[c, row : row + 1] = values[:, lanes_of(c)]
-
-    def load(i, slot):
-        walk.fetch(i, da, da_left, da_right, das.at[slot], a_sem.at[slot])
+    center, inverse = center_inverse(sums2[...], entries)
+    scale = inverse * flat_row(gain2)
+    offset = ROOT * (flat_row(shift2) - center * scale)
+    scale = ROOT * scale
+    stats[...] = jnp.zeros_like(stats)
+    total[...] = jnp.zeros_like(total)
+
+    def load(i):
+        slot = i % SLOTS
+        walk.fetch(i, da, talk3.lands[0], talk3.lands[1], das.at[slot], a_sem.at[slot])
         walk.fetch(i, v, v_left, v_right, vs.at[slot], v_sem.at[slot])
-        walk.fetch(i, ct, ct_left, ct_right, cts.at[slot], c_sem.at[slot])
-
-    def wait_load(slot):
+
+    def wait_load(i):
+        slot = i % SLOTS
         wait_for(das.at[slot], a_sem.at[slot])
         wait_for(vs.at[slot], v_sem.at[slot])
-        wait_for(cts.at[slot], c_sem.at[slot])
+
+    def h_copy(i):
+        w, _ = walk.where(i)
+        return pltpu.make_async_copy(h.at[w, walk.rows(i)], hs.at[i % SLOTS], h_sem.at[i % SLOTS])
+
+    def p_copy(i):
+        w, _ = walk.where(i)
+        return pltpu.make_async_copy(
+            pooled.at[w, walk.rows(i)], wide.at[i % SLOTS, 0, pl.ds(0, tile)], p_sem.at[i % SLOTS]
+        )
+
+    def o_copy(i, slot):
+        w, _ = walk.where(i)
+        return pltpu.make_async_copy(wide.at[slot, 1, pl.ds(0, tile)], da_out.at[w, walk.rows(i)], o_sem.at[slot])
+
+    def lower(i, slot, c):
+        at, cols = lanes_of(c), lanes(c)
+        m, s, l, f = center3[:, at], scale3[:, at], lean[:, at], flat[:, at]
+        dst = low[slot]
+
+        def value(q, size):
+            at = i % SLOTS
+            return das[at, q : q + size, cols] * s - (vs[at, q : q + size, cols] - m) * l - f
+
+        def ends():
+            low_buf[c, 0:EDGE] = jnp.where(walk.hide_left(i), 0.0, value(0, EDGE))
+            low_buf[c, EDGE + tile : 2 * EDGE + tile] = jnp.where(walk.hide_right(i), 0.0, value(EDGE + tile, EDGE))
+
+        def rows(r):
+            def run():
+                low_buf[c, EDGE + r : EDGE + r + UNIT] = value(EDGE + r, UNIT)
+
+            return run
+
+        def taps(r):
+            def run():
+                for tap in range(3):
+                    q = EDGE + r - 5 * (tap - 1)
+                    dst[r : r + UNIT, lanes(tap * thin + c)] = low_buf[c, q : q + UNIT].astype(bf16)
+
+            return run
+
+        units = [ends, rows(0)]
+        for r in range(UNIT, tile, UNIT):
+            units += [rows(r), taps(r - UNIT)]
+        return units + [taps(tile - UNIT)]
+
+    def finish(i, slot, c):
+        at, cols = lanes_of(c), lanes(c)
+        a, b = scale[:, at], offset[:, at]
+        sums = [jnp.zeros((8, LANES), f32), jnp.zeros((8, LANES), f32)]
+
+        def rows(r):
+            def run():
+                q = wide[i % SLOTS, 0, r : r + UNIT, cols] * a + b
+                back = slope_scaled(q) * wide[slot, 2, r : r + UNIT, cols]
+                wide[slot, 1, r : r + UNIT, cols] = back
+                sums[0] = sums[0] + folded(back * q)
+                sums[1] = sums[1] + folded(back)
+
+            return run
+
+        def close():
+            stats[0, :, cols] += sums[0]
+            stats[1, :, cols] += sums[1]
+
+        return [rows(r) for r in range(0, tile, UNIT)] + [close]
+
+    n = Exchange.SUMS
+    talk3 = Exchange(refs[:n], refs[2 * n : 2 * n + 4])
+    talk2 = Exchange(refs[n : 2 * n], refs[2 * n + 4 : 2 * n + 8])
+    w_copy = pltpu.make_async_copy(w_hbm, w_ref, w_sem)
+    w_copy.start()
+    f_copy = pltpu.make_async_copy(first, firsts, f_sem)
+    f_copy.start()
+    size = three.shape[1]
+
+    def three_copy(c):
+        chunk, start = divmod(3 * thin * channels + c * size, data.shape[1])
+        return pltpu.make_async_copy(three.at[c], data.at[chunk, pl.ds(start, size)], t_sem.at[c])
+
+    for c in range(slabs):
+        three_copy(c).start()
+    for i in range(min(SLOTS, tiles)):
+        h_copy(i).start()
+    greet(talk3.seqs, talk3.dps)
+    talk3.start_edges((da,))
+    talk3.start_sums(stats3)
+    w_copy.wait()
+    for k in range(3):
+        w_flip[k * width : (k + 1) * width] = w_ref[k].T
+    talk3.finish_edges((da,))
+    for i in range(min(SLOTS, tiles)):
+        load(i)
+    talk3.finish_sums(grads3)
+    center3, inverse3 = center_inverse(sums3[...], entries)
+    sums = grads3[...]
+    scale3 = inverse3 * flat_row(gain3)
+    lean = scale3 * inverse3 * (sums[0:1] / entries)
+    flat = scale3 * (sums[1:2] / entries)
+
+    def low_tile(i, slot):
+        for c in range(thin):
+            for unit in lower(i, slot, c):
+                unit()
+
+    def weigh_pair(j, _):
+        for slot in range(2):
+            i = 2 * j + slot
+            other = 1 - slot
+
+            @pl.when(i + 1 < tiles)
+            def _():
+                wait_load(i + 1)
+
+            @pl.when(jnp.logical_and(i >= 1, i + SLOTS - 1 < tiles))
+            def _():
+                load(i + SLOTS - 1)
+                h_copy(i + SLOTS - 1).start()
+
+            h_copy(i).wait()
+
+            def weigh(n):
+                def run():
+                    at = slice(n * 256, (n + 1) * 256)
+                    total[at] += dot(hs[i % SLOTS, :, at], low[slot][...], TN)
+
+                return run
+
+            units = []
+            for c in range(thin):
+                units += lower(i + 1, other, c)
+            interleave([weigh(n) for n in range(channels // 256)], units)
+        return 0
+
+    wait_load(0)
+    low_tile(0, 0)
+    lax.fori_loop(0, tiles // 2, weigh_pair, 0)
+    for i in range(min(SLOTS, tiles)):
+        load(i)
+    for c in range(3 * thin):
+        chunk, start = divmod(c * channels, data.shape[1])
+        data[chunk, start : start + channels] = ((0.5 / ROOT) * total[:, lanes_of(c)]).astype(bf16)
+    for c in range(slabs):
+        three_copy(c).wait()
+    if joined:
+        sharing = Reduction.of(data, refs[2 * n + 8 :], 4)
+
+    def back_turn(i, slot, last):
+        other = 1 - slot
+        if not last:
+            @pl.when(i + 1 < tiles)
+            def _():
+                wait_load(i + 1)
+
+            @pl.when(jnp.logical_and(i >= 1, i + SLOTS - 1 < tiles))
+            def _():
+                load(i + SLOTS - 1)
+
+            @pl.when(jnp.logical_and(i >= 1, i + 1 < tiles))
+            def _():
+                p_copy(i + 1).start()
+
+        @pl.when(i >= 1)
+        def _():
+            p_copy(i - 1).wait()
+
+        @pl.when(i >= 3)
+        def _():
+            o_copy(i - 3, other).wait()
+
+        def back(n):
+            def run():
+                cols = lanes(n, 256)
+                wide[slot, 2, 0:tile, cols] = dot(low[slot][...], w_flip[:, cols])
+
+            return run
+
+        units = []
+        for c in range(slabs):
+            units += finish(i + SLOTS - 1, other, c)
+        if last:
+            for unit in units:
+                unit()
+        else:
+            for c in range(thin):
+                units += lower(i + 1, other, c)
+            interleave([back(n) for n in range(channels // 256)], units)
+
+        @pl.when(i >= 1)
+        def _():
+            o_copy(i - 1, other).start()
+
+    def back_pair(j, _):
+        for slot in range(2):
+            back_turn(2 * j + slot, slot, False)
+            if joined:
+                sharing.step(2 * (2 * j + slot))
+                sharing.step(2 * (2 * j + slot) + 1)
+        return 0
+
+    wide[SLOTS - 1, 0, 0:tile] = jnp.zeros((tile, channels), f32)
+    wide[1, 2, 0:tile] = jnp.zeros((tile, channels), f32)
+    for i in range(2):
+        p_copy(i).start()
+    wait_load(0)
+    low_tile(0, 0)
+    lax.fori_loop(0, tiles // 2, back_pair, 0)
+    back_turn(tiles, 0, True)
+    shifts = 0.5 * stats[1]
+    stats[0] = (0.5 / ROOT * stats[0] - shifts * flat_row(shift2)) / flat_row(gain2)
+    stats[1] = shifts
+    o_copy(tiles - 2, 0).wait()
+    o_copy(tiles - 1, 1).wait()
+    talk2.start_edges((da_out,))
+    talk2.start_sums(stats)
+    taps[...] = jnp.zeros_like(taps)
+    talk2.finish_edges((da_out,))
+    lefts, rights = (talk2.lands[0], p_left, ct_left), (talk2.lands[1], p_right, ct_right)
+
+    def wide_load(i):
+        slot = i % SLOTS
+        for n, src in enumerate((da_out, pooled, ct)):
+            walk.fetch(i, src, lefts[n], rights[n], wide.at[slot, n], r_sem.at[slot])
+
+    for i in range(min(SLOTS - 1, tiles)):
+        wide_load(i)
+    f_copy.wait()
+    talk2.finish_sums(grads2)
+    sums = grads2[...]
+    scale2 = 0.5 * inverse * flat_row(gain2)
+    lean2 = scale2 * inverse * (sums[0:1] / entries)
+    flat2 = scale2 * (sums[1:2] / entries)
+    for c in range(slabs):
+        for row, values in enumerate((0.5 * scale2, lean2, center * lean2 - flat2)):
+            coef[c, row : row + 1] = values[:, lanes_of(c)]
+    wides = (wide_a, wide_b)
 
     def s_copy(i, slot):
         w, _ = walk.where(i)
@@ -1200,70 +1192,53 @@
 
     def l_copy(i, slot):
         w, _ = walk.where(i)
-        return pltpu.make_async_copy(low[slot], low_out.at[w, walk.rows(i)], l_sem.at[slot])
-
-    def lower(i, slot, c):
+        return pltpu.make_async_copy(wides[slot], low_out.at[w, walk.rows(i)], l_sem.at[slot])
+
+    def shift_slab(i, slot, c):
         cols = lanes(c)
         sc, l, f = coef[c, 0:1], coef[c, 1:2], coef[c, 2:3]
-        dst = low[slot]
+        dst = wides[slot]
 
         def value(q, size):
-            rows = slice(q, q + size)
-            return 0.5 * cts[slot, rows, cols] + das[slot, rows, cols] * sc - vs[slot, rows, cols] * l + f
+            a, p, g = (wide[i % SLOTS, n, q : q + size, cols] for n in range(3))
+            return 0.5 * g + a * sc - p * l + f
 
         def ends():
-            low_buf[c, 0:EDGE] = jnp.where(walk.hide_left(i), 0.0, value(0, EDGE))
-            low_buf[c, EDGE + tile : 2 * EDGE + tile] = jnp.where(walk.hide_right(i), 0.0, value(EDGE + tile, EDGE))
+            wide_buf[c, 0:EDGE] = jnp.where(walk.hide_left(i), 0.0, value(0, EDGE))
+            wide_buf[c, EDGE + tile : 2 * EDGE + tile] = jnp.where(walk.hide_right(i), 0.0, value(EDGE + tile, EDGE))
 
         def rows(r):
             def run():
-                low_buf[c, EDGE + r : EDGE + r + UNIT] = value(EDGE + r, UNIT)
+                wide_buf[c, EDGE + r : EDGE + r + UNIT] = value(EDGE + r, UNIT)
 
             return run
 
-        def taps(r):
+        def shifts(r):
             def run():
                 for tap in range(3):
                     q = EDGE + r + 1 - tap
                     at = pl.ds(pl.multiple_of(tap * channels + c * LANES, LANES), LANES)
-                    dst[r : r + UNIT, at] = low_buf[c, q : q + UNIT].astype(bf16)
+                    dst[r : r + UNIT, at] = wide_buf[c, q : q + UNIT].astype(bf16)
 
             return run
 
         units = [ends, rows(0)]
         for r in range(UNIT, tile, UNIT):
-            units += [rows(r), taps(r - UNIT)]
-        return units + [taps(tile - UNIT)]
-
-    load(0, 0)
-    wait_load(0)
+            units += [rows(r), shifts(r - UNIT)]
+        return units + [shifts(tile - UNIT)]
+
     s_copy(0, 0).start()
-    f_copy = pltpu.make_async_copy(first, firsts, f_sem)
-    f_copy.start()
-    load(1, 1)
-    at = 0
-    for src in (two, three):
-        size = src.shape[1]
-        for c in range(src.shape[0]):
-            chunk, start = divmod(at, data.shape[1])
-            pltpu.make_async_copy(src.at[c], data.at[chunk, pl.ds(start, size)], d_sem).start()
-            at += size
-    if joined:
-        greet(seqs, dps)
-        sharing = Reduction.of(data, reduction)
-    total[...] = jnp.zeros_like(total)
+    wait_for(wide.at[0], r_sem.at[0])
 
     def first_slab(c, _):
-        for unit in lower(0, 0, c):
+        for unit in shift_slab(0, 0, c):
             unit()
         return 0
 
     lax.fori_loop(0, slabs, first_slab, 0)
     l_copy(0, 0).start()
-    f_copy.wait()
-    wait_for(data, d_sem)
-
-    def pair(j, _):
+
+    def wide_pair(j, _):
         for slot in range(2):
             i = 2 * j + slot
             other = 1 - slot
@@ -1273,16 +1248,16 @@
             def _():
                 row = lax.broadcasted_iota(jnp.int32, (16, channels), 0)
                 here = jnp.where(row == 0, firsts[w].astype(f32), 0.0).astype(bf16)
-                total[1] += dot(here, low[slot][0:16, channels : 2 * channels], TN)
+                taps[1] += dot(here, wides[slot][0:16, channels : 2 * channels], TN)
 
             @pl.when(i + 1 < tiles)
             def _():
-                wait_load(other)
+                wait_for(wide.at[(i + 1) % SLOTS], r_sem.at[(i + 1) % SLOTS])
                 s_copy(i + 1, other).start()
 
-            @pl.when(i + 2 < tiles)
-            def _():
-                load(i + 2, slot)
+            @pl.when(i + SLOTS - 1 < tiles)
+            def _():
+                wide_load(i + SLOTS - 1)
 
             @pl.when(i >= 1)
             def _():
@@ -1296,14 +1271,14 @@
                 def weigh(k):
                     def run():
                         at = pl.ds(pl.multiple_of((k // 2) * channels + n * 256, 256), 256)
-                        total[k, :, cols] += dot(ss[slot, k % 2], low[slot][:, at], TN)
+                        taps[k, :, cols] += dot(ss[slot, k % 2], wides[slot][:, at], TN)
 
                     return run
 
-                units = lower(i + 1, other, 2 * n) + lower(i + 1, other, 2 * n + 1)
+                units = shift_slab(i + 1, other, 2 * n) + shift_slab(i + 1, other, 2 * n + 1)
                 interleave([weigh(k) for k in range(EARLY)], units)
                 if joined:
-                    sharing.step(i * (channels // 256) + n)
+                    sharing.step(2 * tiles + i * (channels // 256) + n)
                 return 0
 
             lax.fori_loop(0, channels // 256, part, 0)
@@ -1314,11 +1289,11 @@
 
         return 0
 
-    lax.fori_loop(0, tiles // 2, pair, 0)
+    lax.fori_loop(0, tiles // 2, wide_pair, 0)
     l_copy(tiles - 1, 1).wait()
     for k in range(EARLY):
         for c in range(slabs):
-            packed[k, c] = ((0.5 / ROOT) * total[k, :, lanes_of(c)]).astype(bf16)
+            packed[k, c] = ((0.5 / ROOT) * taps[k, :, lanes_of(c)]).astype(bf16)
     g_copy = pltpu.make_async_copy(packed, w_grad, g_sem)
     g_copy.start()
     if joined:
@@ -1326,63 +1301,83 @@
             sharing.step(t)
             return 0
 
-        lax.fori_loop(tiles * (channels // 256), sharing.steps, more, 0)
-        d_copy = pltpu.make_async_copy(sharing.done, small, d_sem)
-    else:
-        d_copy = pltpu.make_async_copy(data, small, d_sem)
+        lax.fori_loop(2 * tiles + tiles * (channels // 256), sharing.steps, more, 0)
+    d_copy = pltpu.make_async_copy(sharing.done if joined else data, small, d_sem)
     d_copy.start()
     d_copy.wait()
     g_copy.wait()
 
 
-def conv_one_weigh(da, da_sides, v, v_sides, ct, ct_sides, sums2, grads2, gain2, s, first, two, three, entries, number):
-    windows, length, channels = da.shape
+def conv_two_back(
+    da, stats3, v, v_sides, sums3, gain3, pooled, p_sides, sums2, gain2, shift2, h, weight, ct, ct_sides, s, first, three,
+    entries, number,
+):
+    windows, length, width = da.shape
+    channels = pooled.shape[2]
     tile = min(512, length)
-    slabs = channels // LANES
+    thin, slabs = width // LANES, channels // LANES
+    back = jax.ShapeDtypeStruct((windows, length, channels), f32)
     packed = (EARLY, slabs, channels, LANES)
     rows = 2 * channels
-    chunks = (two.shape[0] * two.shape[1] + three.shape[0] * three.shape[1]) // rows
+    chunks = (3 * channels * width + width * channels) // (rows * LANES)
     joined = Reduction.fits(rows)
-    estimate = params(4 * EARLY * da.size * channels, 24 * da.size, 0)
-    if joined:
-        estimate = joining(estimate, number)
-    low, parts, small = pl.pallas_call(
-        functools.partial(conv_one_weigh_kernel, tile, entries, joined, lax.axis_size("seq"), lax.axis_size("dp")),
-        out_shape=(
+    got = pl.pallas_call(
+        functools.partial(conv_two_back_kernel, tile, entries, joined),
+        out_shape=[
+            back,
             jax.ShapeDtypeStruct((windows, length, 3 * channels), bf16),
             jax.ShapeDtypeStruct(packed, bf16),
             jax.ShapeDtypeStruct((chunks, rows, LANES), bf16),
-        ),
-        in_specs=[ANY] * 9 + [VM] * 3 + [ANY] * 4,
-        out_specs=(ANY, ANY, ANY),
+            jax.ShapeDtypeStruct((8, width), f32),
+            jax.ShapeDtypeStruct((8, channels), f32),
+        ],
+        in_specs=[ANY, VM] + [ANY] * 3 + [VM] * 2 + [ANY] * 3 + [VM] * 3 + [ANY] * 8,
+        out_specs=[ANY] * 4 + [VM] * 2,
         scratch_shapes=[
-            pltpu.VMEM((2, tile + 2 * EDGE, channels), f32),
-            pltpu.VMEM((2, tile + 2 * EDGE, channels), f32),
-            pltpu.VMEM((2, tile + 2 * EDGE, channels), f32),
-            pltpu.VMEM((2, 2, tile, channels), bf16),
-            pltpu.VMEM(first.shape, bf16),
+            pltpu.VMEM((SLOTS, tile + 2 * EDGE, width), f32),
+            pltpu.VMEM((SLOTS, tile + 2 * EDGE, width), f32),
+            pltpu.VMEM((SLOTS, tile, channels), bf16),
+            pltpu.VMEM((thin, tile + 2 * EDGE, LANES), f32),
+            pltpu.VMEM((tile, 3 * width), bf16),
+            pltpu.VMEM((tile, 3 * width), bf16),
+            pltpu.VMEM((channels, 3 * width), f32),
+            pltpu.VMEM(weight.shape, bf16),
+            pltpu.VMEM((3 * width, channels), bf16),
+            pltpu.VMEM((2, 8, channels), f32),
+            pltpu.VMEM((SLOTS, 3, tile + 2 * EDGE, channels), f32),
             pltpu.VMEM((slabs, tile + 2 * EDGE, LANES), f32),
             pltpu.VMEM((tile, 3 * channels), bf16),
             pltpu.VMEM((tile, 3 * channels), bf16),
+            pltpu.VMEM((2, 2, tile, channels), bf16),
+            pltpu.VMEM(first.shape, bf16),
             pltpu.VMEM((slabs, 8, LANES), f32),
             pltpu.VMEM((EARLY, channels, channels), f32),
             pltpu.VMEM(packed, bf16),
             pltpu.VMEM((chunks, rows, LANES), bf16),
         ]
-        + [DMA((2,))] * 4
-        + [DMA, DMA((2,)), DMA, DMA]
+        + [DMA((SLOTS,))] * 4
+        + [DMA((2,))]
+        + [DMA, DMA((SLOTS,)), DMA((2,)), DMA, DMA((2,)), DMA, DMA, DMA((slabs,))]
+        + Exchange.scratch(width)
+        + Exchange.scratch(channels)
+        + Exchange.edge_scratch([da])
+        + Exchange.edge_scratch([back])
         + (Reduction.scratch(chunks, rows) if joined else []),
-        name="conv_one_weigh",
-        **estimate,
-    )(da, *da_sides, v, *v_sides, ct, *ct_sides, sums2, grads2, gain2, s, first, two, three)
+        name="conv_two_back",
+        **joining(params(20 * pooled.size * channels, 40 * pooled.size, pooled.size), number),
+    )(
+        da, stats3, v, *v_sides, sums3, gain3, pooled, *p_sides, sums2, gain2, shift2, h, weight, ct, *ct_sides, s, first,
+        three,
+    )
+    low, parts, small = got[1:4]
     if not joined:
         small = lax.psum(small, ("dp", "seq"))
-    return low, parts, small
+    return low, parts, small, got[4], got[5]
 
 
 def conv_one_spread_kernel(
-    tile, entries, joined, low, x, sums1, gain1, shift1, w_hbm, s, parts, da_out, w_grad, grads1,
-    lows, xs, g_buf, outs, coef, w_ref, total, ss, ls, data, stats, l_sem, x_sem, o_sem, w_sem, d_sem, t_sem, *refs,
+    tile, entries, joined, low, x, sums1, gain1, shift1, w_hbm, s, parts, da_out, q_out, w_grad, grads1,
+    lows, xs, g_buf, outs, q_buf, coef, w_ref, total, ss, ls, data, stats, l_sem, x_sem, o_sem, q_sem, w_sem, d_sem, t_sem, *refs,
 ):
     windows, length, _ = low.shape
     channels = x.shape[2]
@@ -1406,9 +1401,12 @@
         w, _ = walk.where(i)
         return pltpu.make_async_copy(x.at[w, walk.rows(i, 2)], xs.at[slot], x_sem.at[slot])
 
-    def o_copy(i, slot):
+    def o_copies(i, slot):
         w, _ = walk.where(i)
-        return pltpu.make_async_copy(outs.at[slot], da_out.at[w, walk.rows(i, 2)], o_sem.at[slot])
+        return (
+            pltpu.make_async_copy(outs.at[slot], da_out.at[w, walk.rows(i, 2)], o_sem.at[slot]),
+            pltpu.make_async_copy(q_buf.at[slot], q_out.at[w, walk.rows(i, 2)], q_sem.at[slot]),
+        )
 
     def t_copies(g, slot):
         k = EARLY + g // tiles
@@ -1432,7 +1430,7 @@
     w_copy = pltpu.make_async_copy(w_hbm, w_ref, w_sem)
     w_copy.start()
     if joined:
-        sharing = Reduction.of(data, reduction)
+        sharing = Reduction.of(data, reduction, 3)
         sharing.step(0)
 
     late = (5 - EARLY) * tiles
@@ -1491,6 +1489,7 @@
                 incoming = g_buf[slot, c, EDGE + r : EDGE + r + UNIT] + g_buf[slot, c, EDGE + r - 1 : EDGE + r - 1 + UNIT]
                 back = slope_scaled(q) * incoming
                 outs[slot, r : r + UNIT, cols] = back.astype(bf16)
+                q_buf[slot, r : r + UNIT, cols] = q.astype(bf16)
                 held[0] = held[0] + folded(back * q)
                 held[1] = held[1] + folded(back)
 
@@ -1553,7 +1552,8 @@
 
         @pl.when(i >= 3)
         def _():
-            o_copy(i - 3, other).wait()
+            for copy in o_copies(i - 3, other):
+                copy.wait()
 
         if not last:
             x_copy(i, slot).start()
@@ -1572,7 +1572,8 @@
 
         @pl.when(i >= 1)
         def _():
-            o_copy(i - 1, other).start()
+            for copy in o_copies(i - 1, other):
+                copy.start()
 
     xs[1] = jnp.zeros(xs.shape[1:], f32)
     g_buf[1] = jnp.zeros(g_buf.shape[1:], f32)
@@ -1586,8 +1587,8 @@
     turn(tiles, 0, True)
     settle()
     talk.start_sums(stats)
-    o_copy(tiles - 2, 0).wait()
-    o_copy(tiles - 1, 1).wait()
+    for copy in o_copies(tiles - 2, 0) + o_copies(tiles - 1, 1):
+        copy.wait()
     if joined:
         def more(t, _):
             sharing.step(t)
@@ -1609,19 +1610,21 @@
     parts = parts.reshape(EARLY * slabs // 2, rows, LANES)
     joined = Reduction.fits(rows)
     estimate = params(10 * low.size * channels // 3, 12 * x.size, x.size)
-    da, grad, grads1 = pl.pallas_call(
+    da, q, grad, grads1 = pl.pallas_call(
         functools.partial(conv_one_spread_kernel, tile, entries, joined),
         out_shape=(
+            jax.ShapeDtypeStruct((windows, 2 * length, channels), bf16),
             jax.ShapeDtypeStruct((windows, 2 * length, channels), bf16),
             jax.ShapeDtypeStruct((chunks, rows, LANES), bf16),
             jax.ShapeDtypeStruct((8, channels), f32),
         ),
         in_specs=[ANY] * 2 + [VM] * 3 + [ANY] * 3,
-        out_specs=(ANY, ANY, VM),
+        out_specs=(ANY, ANY, ANY, VM),
         scratch_shapes=[
             pltpu.VMEM((2, tile, 3 * channels), bf16),
             pltpu.VMEM((2, 2 * tile, channels), f32),
             pltpu.VMEM((2, slabs, 2 * tile + 2 * EDGE, LANES), f32),
+            pltpu.VMEM((2, 2 * tile, channels), bf16),
             pltpu.VMEM((2, 2 * tile, channels), bf16),
             pltpu.VMEM((slabs, 8, LANES), f32),
             pltpu.VMEM(weight.shape, bf16),
@@ -1630,6 +1633,7 @@
             pltpu.VMEM((AHEAD + 1, tile, channels), bf16),
             pltpu.VMEM((chunks, rows, LANES), bf16),
             pltpu.VMEM((2, 8, channels), f32),
+            DMA((2,)),
             DMA((2,)),
             DMA((2,)),
             DMA((2,)),
@@ -1644,18 +1648,34 @@
     )(low, x, sums1, gain1, shift1, weight, s, parts)
     if not joined:
         grad = lax.psum(grad, ("dp", "seq"))
-    return da, grad, grads1
-
-
-def widen_kernel(one, small, grads1, grads2, grads3, one_out, two_out, three_out, *vectors):
-    for c in range(one.shape[1]):
-        one_out[0, :, lanes_of(c)] = one[0, c].astype(f32)
+    return da, q, grad, grads1
+
+
+def last_kernel(
+    entries, taps, da, q, sums, grads1, gain, shift, one, small, grads2, grads3, out, one_out, two_out, three_out, *vectors
+):
+    center, inverse = center_inverse(sums[...], entries)
+    both = grads1[...]
+    scale = inverse * flat_row(gain)
+    lean = inverse * (both[0:1] / entries)
+    flat = flat_row(shift) * lean - scale * (both[1:2] / entries)
+    for c in range(da.shape[2] // LANES):
+        cols, at = lanes(c), lanes_of(c)
+        s, l, f = 0.5 * scale[:, at], (1.0 / ROOT) * lean[:, at], flat[:, at]
+        for r in range(0, da.shape[1], 128):
+            rows = slice(r, r + 128)
+            out[0, rows, cols] = da[0, rows, cols].astype(f32) * s - q[0, rows, cols].astype(f32) * l + f
+
+    @pl.when(pl.program_id(0) < taps)
+    def _():
+        for c in range(one.shape[1]):
+            one_out[0, :, lanes_of(c)] = one[0, c].astype(f32)
 
     @pl.when(pl.program_id(0) == 0)
     def _():
-        taps, rows, width = two_out.shape
+        kinds, rows, width = two_out.shape
         at = 0
-        for k in range(taps):
+        for k in range(kinds):
             for c in range(width // LANES):
                 two_out[k, :, lanes_of(c)] = small[at : at + rows].astype(f32)
                 at += rows
@@ -1668,70 +1688,43 @@
             vectors[2 * n + 1][...] = grads[1]
 
 
-def widen(one, small, two_shape, three_shape, grads):
-    channels = two_shape[1]
+def last(da, q, sums, gain, shift, one, small, two_shape, three_shape, grads, entries):
+    windows, length, channels = da.shape
     slabs = channels // LANES
-    one = one.reshape(5, slabs, channels, LANES)
+    tile = min(1024, windows * length // 8)
+    per = length // tile
+    taps = 5
+    one = one.reshape(taps, slabs, channels, LANES)
     small = small.reshape(-1, LANES)
-    flat = lambda k: (0, 0)
+    rows = pl.BlockSpec((1, tile, channels), lambda i: (i // per, i % per, 0))
+    flat = lambda i: (0, 0)
+    vector = lambda v: pl.BlockSpec((v.shape[0],), lambda i: (0,))
     lengths = [g.shape[1] for g in grads for _ in range(2)]
+    tap = lambda i: jnp.minimum(i, taps - 1)
+    grads1, grads2, grads3 = grads
     return pl.pallas_call(
-        widen_kernel,
-        grid=(5,),
+        functools.partial(last_kernel, entries, taps),
+        grid=(windows * per,),
         out_shape=[
-            jax.ShapeDtypeStruct((5, channels, channels), f32),
+            jax.ShapeDtypeStruct(da.shape, f32),
+            jax.ShapeDtypeStruct((taps, channels, channels), f32),
             jax.ShapeDtypeStruct(two_shape, f32),
             jax.ShapeDtypeStruct(three_shape, f32),
         ]
         + [jax.ShapeDtypeStruct((n,), f32) for n in lengths],
-        in_specs=[pl.BlockSpec((1, slabs, channels, LANES), lambda k: (k, 0, 0, 0)), pl.BlockSpec(small.shape, flat)]
-        + [pl.BlockSpec(g.shape, flat) for g in grads],
+        in_specs=[rows, rows, pl.BlockSpec(sums.shape, flat), pl.BlockSpec(grads1.shape, flat), vector(gain), vector(shift)]
+        + [pl.BlockSpec((1, slabs, channels, LANES), lambda i: (tap(i), 0, 0, 0)), pl.BlockSpec(small.shape, flat)]
+        + [pl.BlockSpec(g.shape, flat) for g in grads[1:]],
         out_specs=[
-            pl.BlockSpec((1, channels, channels), lambda k: (k, 0, 0)),
-            pl.BlockSpec(two_shape, lambda k: (0, 0, 0)),
+            rows,
+            pl.BlockSpec((1, channels, channels), lambda i: (tap(i), 0, 0)),
+            pl.BlockSpec(two_shape, lambda i: (0, 0, 0)),
             pl.BlockSpec(three_shape, flat),
         ]
-        + [pl.BlockSpec((n,), lambda k: (0,)) for n in lengths],
-        name="widen",
-        **params(moved=6 * one.size),
-    )(one, small, *grads)
-
-
-def last_kernel(entries, x, da, sums, grads, gain, out):
-    center, inverse = center_inverse(sums[...], entries)
-    both = grads[...]
-    scale = inverse * flat_row(gain)
-    lean = scale * inverse * (both[0:1] / entries)
-    flat = scale * (both[1:2] / entries)
-    for c in range(x.shape[2] // LANES):
-        cols, at = lanes(c), lanes_of(c)
-        m, s, l, f = center[:, at], scale[:, at], lean[:, at], flat[:, at]
-        for r in range(0, x.shape[1], 128):
-            rows = slice(r, r + 128)
-            out[0, rows, cols] = da[0, rows, cols].astype(f32) * (0.5 * s) - (x[0, rows, cols] - m) * l - f
-
-
-def input_back(x, da, sums, grads, gain, entries):
-    windows, length, channels = x.shape
-    tile = min(1024, length)
-    per = length // tile
-    rows = pl.BlockSpec((1, tile, channels), lambda i: (i // per, i % per, 0))
-    whole = lambda i: (0, 0)
-    return pl.pallas_call(
-        functools.partial(last_kernel, entries),
-        grid=(windows * per,),
-        out_shape=jax.ShapeDtypeStruct(x.shape, f32),
-        in_specs=[
-            rows,
-            rows,
-            pl.BlockSpec((8, channels), whole),
-            pl.BlockSpec((8, channels), whole),
-            pl.BlockSpec((channels,), lambda i: (0,)),
-        ],
-        out_specs=rows,
-        name="input_back",
-        **params(moved=10 * x.size),
-    )(x, da, sums, grads, gain)
+        + [pl.BlockSpec((n,), lambda i: (0,)) for n in lengths],
+        name="last",
+        **params(moved=8 * da.size + 6 * one.size),
+    )(da, q, sums, grads1, gain, shift, one, small, grads2, grads3)
 
 
 def on_device(
@@ -1759,20 +1752,17 @@
     outputs, da3, stats, three_grad = conv_three_both(
         narrow, cotangent, pooled, sums3, gain_three, shift_three, conv_three, half
     )
-    grads3, a_sides = exchange(stats, [da3], 2)
-    (da2, two_grad, grads2), b_sides = conv_two_back(
-        da3, a_sides, narrow, n_sides, sums3, grads3, gain_three, pooled, sums2, gain_two, shift_two,
-        hidden_two, conv_two, half, 3,
+    low, parts, small, grads3, grads2 = conv_two_back(
+        da3, stats, narrow, n_sides, sums3, gain_three, pooled, p_sides, sums2, gain_two, shift_two, hidden_two, conv_two,
+        cotangent, c_sides, s, first, three_grad, half, 2,
     )
-    low, parts, small = conv_one_weigh(
-        da2, b_sides, pooled, p_sides, cotangent, c_sides, sums2, grads2, gain_two, s, first,
-        two_grad, three_grad, entries, 4,
+    da1, q1, one_grad, grads1 = conv_one_spread(
+        low, inputs, sums1, gain_one, shift_one, conv_one, s, parts, entries, 3
     )
-    da1, one_grad, grads1 = conv_one_spread(
-        low, inputs, sums1, gain_one, shift_one, conv_one, s, parts, entries, 5
+    input_grad, *small_grads = last(
+        da1, q1, sums1, gain_one, shift_one, one_grad, small, conv_two.shape, conv_three.shape,
+        (grads1, grads2, grads3), entries,
     )
-    input_grad = input_back(inputs, da1, sums1, grads1, gain_one, entries)
-    small_grads = widen(one_grad, small, conv_two.shape, conv_three.shape, (grads1, grads2, grads3))
     return (outputs, input_grad, *small_grads)
 
 

time: 330 us -> 318 us (0.964)
  Pallas kernels: 329 us -> 317 us
    pallas_call x5 -> x2, Pallas kernels: 129 us -> 119 us  [the longest x1 91.2 us: conv_two_back(): pl.pallas_call(functools.partial(conv_two_back_kernel, tile, entries, joi...]
where the time goes in v4:
time: 318 us
  Pallas kernels  317 us (100%)
    pallas_call x1, Pallas kernels, conv_two_back(): pl.pallas_call(functools.partial(conv_two_back_kernel, tile, entries, joi...  91.2 us
    pallas_call x1, Pallas kernels, conv_one_spread(): pl.pallas_call(functools.partial(conv_one_spread_kernel, tile, entries, j...  78.7 us
    pallas_call x1, Pallas kernels, conv_one_forward(): pl.pallas_call(functools.partial(conv_one_kernel, tile, entries), out_sha...  67.1 us
    pallas_call x1, Pallas kernels, conv_two_forward(): pl.pallas_call(functools.partial(conv_two_kernel, tile, entries), out_sha...  28.6 us
    pallas_call x1, Pallas kernels, last(): pl.pallas_call(functools.partial(last_kernel, entries, taps), grid=(windo...  27.4 us
    pallas_call x1, Pallas kernels, conv_three_both(): pl.pallas_call(functools.partial(conv_three_kernel, entries), grid=(windo...  23.9 us

profile of v4, /device:TPU:0, one launch (start us, length us, event | category | flops | bytes accessed | tf_op | source)
XLA Modules:
  0.0 317.8 jit_solution(10506670498191765745)
XLA Ops:
  0.6 67.1 %conv_one_forward.1 = (f32[2,2048,768]{2,1,0:T(8,128)}, bf16[2,2,2048,768]{3,2,1,0:T(8,128)(2,1)}, bf16[2,16,768]{2,1,0:T(8,128)(2,1)}, f32[8,768]{1,0:T(8,128)}...) custom-call(f32[2,4096,768]{2,1,0:T(8,128)} %x.3, ...), custom_call_target="tpu_custom_call" | custom-call | flops 24159191040 | bytes 75497472 | tf_op jit(solution)/shard_map/conv_one_forward/pallas_call | solution.py:525
  67.7 28.6 %conv_two_forward.1 = (f32[2,2048,384]{2,1,0:T(8,128)}, bf16[2,2048,768]{2,1,0:T(8,128)(2,1)}, f32[8,384]{1,0:T(8,128)}, f32[2,8,384]{2,1,0:T(8,128)}, f32[2,8,384]{2,1,0:T(8,128)}) custom-call(f32[2,2048,768]{2,1,0:T(8,128)} %get-tuple-element.48.v.pooled, f32[2,8,768]{2,1,0:T(8,128)} %get-tuple-element.49.left.p_left, ...), custom_call_target="tpu_custom_call" | custom-call | flops 7247757312 | bytes 25165824 | tf_op jit(solution)/shard_map/conv_two_forward/pallas_call | solution.py:700
  96.3 23.9 %conv_three_both.1 = (f32[2,2048,768]{2,1,0:T(8,128)}, f32[2,2048,384]{2,1,0:T(8,128)}, f32[2,8,384]{2,1,0:T(8,128)}, bf16[6,384,128]{2,1,0:T(8,128)(2,1)}) custom-call(f32[2,2048,384]{2,1,0:T(8,128)} %get-tuple-element.52.narrow.v, f32[2,2048,768]{2,1,0:T(8,128)} %ct.1, f32[2,2048,768]{2,1,0:T(8,128)} %get-tuple-element.48.v.pooled, ...), custom_call_target="tpu_custom_call" | custom-call | flops 7247757312 | bytes 37748736 | tf_op jit(solution)/shard_map/conv_three_both/pallas_call | solution.py:778
  120.2 91.2 %conv_two_back.1 = (f32[2,2048,768]{2,1,0:T(8,128)}, bf16[2,2048,2304]{2,1,0:T(8,128)(2,1)}, bf16[3,6,768,128]{3,2,1,0:T(8,128)(2,1)}, bf16[6,1536,128]{2,1,0:T(...) custom-call(f32[2,2048,384]{2,1,0:T(8,128)} %get-tuple-element.55.da, f32[2,8,384]{2,1,0:T(8,128)} %get-tuple-element.56.stats3, ...), custom_call_target="tpu_custom_call" | custom-call | flops 48318382080 | bytes 125829120 | tf_op jit(solution)/shard_map/conv_two_back/pallas_call | solution.py:1324
  211.5 78.7 %conv_one_spread.1 = (bf16[2,4096,768]{2,1,0:T(8,128)(2,1)}, bf16[2,4096,768]{2,1,0:T(8,128)(2,1)}, bf16[15,1536,128]{2,1,0:T(8,128)(2,1)}, f32[8,768]{1,0:T(8,128)}) custom-call(bf16[2,2048,2304]{2,1,0:T(8,128)(2,1)} %get-tuple-element.65.low, f32[2,4096,768]{2,1,0:T(8,128)} %x.3, f32[8,768]{1,0:T(8,128)} %get-tuple-element.66.sums1.sums, f32[768]{0:T(1024)} %gain.7, ...), custom_call_target="tpu_custom_call" | custom-call | flops 24159191040 | bytes 75497472 | tf_op jit(solution)/shard_map/conv_one_spread/pallas_call | solution.py:1613
  290.2 27.4 %last.1 = (f32[2,4096,768]{2,1,0:T(8,128)}, f32[5,768,768]{2,1,0:T(8,128)}, f32[3,768,384]{2,1,0:T(8,128)}, f32[384,768]{1,0:T(8,128)}, f32[768]{0:T(1024)}, /*i...) custom-call(bf16[2,4096,768]{2,1,0:T(8,128)(2,1)} %get-tuple-element.68.da, ...), custom_call_target="tpu_custom_call" | custom-call | bytes 68026368 | tf_op jit(solution)/shard_map/last/pallas_call | solution.py:1705

commit v5 on v4

--- a/solution.py
+++ b/solution.py
@@ -19,7 +19,8 @@
 CUBIC = 0.7978845608028654 * 0.044715
 VMEM_LIMIT = 60 << 20
 EARLY = 3
-AHEAD = 3
+AHEAD = 2
+TALL = 1024
 SLOTS = 3
 NN = (((1,), (0,)), ((), ()))
 NT = (((1,), (1,)), ((), ()))
@@ -30,11 +31,6 @@
     return lax.dot_general(a, b, dims, preferred_element_type=f32)
 
 
-def gelu(v):
-    half = 0.5 * v
-    return half + half * jnp.tanh(v * (LINEAR + CUBIC * (v * v)))
-
-
 ROOT = CUBIC ** (1.0 / 3.0)
 BEND = LINEAR / ROOT
 
@@ -47,20 +43,6 @@
     square = q * q
     th = jnp.tanh(q * (BEND + square))
     return (1.0 + th) * (1.0 + (1.0 - th) * (q * (BEND + 3.0 * square)))
-
-
-def gelu_both(v):
-    square = v * v
-    up = 0.5 + 0.5 * jnp.tanh(v * (LINEAR + CUBIC * square))
-    value = v * up
-    slope = up + value * (1.0 - up) * (2.0 * LINEAR + (6.0 * CUBIC) * square)
-    return value, slope
-
-
-def gelu_slope(v):
-    square = v * v
-    up = 0.5 + 0.5 * jnp.tanh(v * (LINEAR + CUBIC * square))
-    return up + (v * up) * (1.0 - up) * (2.0 * LINEAR + (6.0 * CUBIC) * square)
 
 
 def center_inverse(sums, entries):
@@ -294,10 +276,140 @@
     )
 
 
+def conv_two_phase(
+    tile, entries, v, left, right, sums, gain, shift, w_copy, w_ref, talk, narrow, h_out, sums3, n_left, n_right,
+    vs, h_buf, lhs_a, lhs_b, outs, stats, v_sem, h_sem, o_sem,
+):
+    windows, length, channels = v.shape
+    slabs = channels // LANES
+    walk = Walk(windows, length, tile)
+    tiles = walk.count
+    lhs = (lhs_a, lhs_b)
+    stats[...] = jnp.zeros_like(stats)
+
+    def load(i):
+        walk.fetch(i, v, left, right, vs.at[i % SLOTS], v_sem.at[i % SLOTS])
+
+    def wait_load(i):
+        wait_for(vs.at[i % SLOTS], v_sem.at[i % SLOTS])
+
+    def h_copy(i, slot):
+        w, _ = walk.where(i)
+        return pltpu.make_async_copy(
+            lhs[slot].at[:, pl.ds(channels, channels)], h_out.at[w, walk.rows(i)], h_sem.at[slot]
+        )
+
+    def o_copy(i, slot):
+        w, _ = walk.where(i)
+        return pltpu.make_async_copy(outs.at[slot], narrow.at[w, walk.rows(i)], o_sem.at[slot])
+
+    def activate(i, slot, c):
+        a, b = scale[:, lanes_of(c)], offset[:, lanes_of(c)]
+        src, dst, cols = vs.at[i % SLOTS], lhs[slot], lanes(c)
+
+        def ends():
+            head = gelu_scaled(src[0:EDGE, cols] * a + b)
+            h_buf[c, 0:EDGE] = jnp.where(walk.hide_left(i), 0.0, head)
+            tail = gelu_scaled(src[EDGE + tile : 2 * EDGE + tile, cols] * a + b)
+            h_buf[c, EDGE + tile : 2 * EDGE + tile] = jnp.where(walk.hide_right(i), 0.0, tail)
+
+        def rows(r):
+            def run():
+                q = EDGE + r
+                h_buf[c, q : q + UNIT] = gelu_scaled(src[q : q + UNIT, cols] * a + b)
+
+            return run
+
+        def taps(r):
+            def run():
+                for tap in range(3):
+                    at = EDGE + r + 5 * (tap - 1)
+                    dst[r : r + UNIT, lanes(tap * slabs + c)] = h_buf[c, at : at + UNIT].astype(bf16)
+
+            return run
+
+        units = [ends, rows(0)]
+        for r in range(UNIT, tile, UNIT):
+            units += [rows(r), taps(r - UNIT)]
+        return units + [taps(tile - UNIT)]
+
+    for i in range(min(SLOTS, tiles)):
+        load(i)
+    center, inverse = center_inverse(sums(), entries)
+    scale = inverse * flat_row(gain)
+    offset = ROOT * (flat_row(shift) - center * scale)
+    scale = ROOT * scale
+    wait_load(0)
+    for c in range(slabs):
+        for unit in activate(0, 0, c):
+            unit()
+    h_copy(0, 0).start()
+    w_copy.wait()
+
+    def pair(j, _):
+        for slot in range(2):
+            i = 2 * j + slot
+            other = 1 - slot
+
+            @pl.when(i + 1 < tiles)
+            def _():
+                wait_load(i + 1)
+
+            @pl.when(jnp.logical_and(i >= 1, i + SLOTS - 1 < tiles))
+            def _():
+                load(i + SLOTS - 1)
+
+            @pl.when(i >= 1)
+            def _():
+                h_copy(i - 1, other).wait()
+
+            @pl.when(i >= 2)
+            def _():
+                o_copy(i - 2, slot).wait()
+
+            held = []
+
+            def piece(k):
+                def run():
+                    at = slice(k * channels, (k + 1) * channels)
+                    part = dot(lhs[slot][:, at], w_ref[at])
+                    held[:] = [held[0] + part] if held else [part]
+
+                return run
+
+            units = []
+            for c in range(slabs):
+                units += activate(i + 1, other, c)
+            interleave([piece(k) for k in range(3)], units)
+            total = (0.5 / ROOT) * held[0]
+            outs[slot] = total
+            stats[0] += folded(total)
+            stats[1] += folded(total * total)
+            o_copy(i, slot).start()
+
+            @pl.when(i + 1 < tiles)
+            def _():
+                h_copy(i + 1, other).start()
+
+        return 0
+
+    lax.fori_loop(0, tiles // 2, pair, 0)
+    h_copy(tiles - 1, 1).wait()
+    o_copy(tiles - 2, 0).wait()
+    o_copy(tiles - 1, 1).wait()
+    talk.start_edges((narrow,))
+    talk.start_sums(stats)
+    talk.finish_edges((narrow,))
+    n_left[...] = talk.lands[0][...]
+    n_right[...] = talk.lands[1][...]
+    talk.finish_sums(sums3)
+
+
 def conv_one_kernel(
-    tile, entries, x, cotangent, gain, shift, w_hbm,
-    pooled, s_out, first_out, sums1, sums2, c_left, c_right, p_left, p_right,
-    xs, h_buf, lhs_a, lhs_b, outs, coef, w_ref, stats, x_sem, s_sem, f_sem, o_sem, w_sem, *talks,
+    tile, entries, x, cotangent, gain, shift, w_hbm, gain2, shift2, w2_hbm,
+    pooled, pooled_low, s_out, first_out, narrow, h_out, sums1, sums2, sums3, c_left, c_right, p_left, p_right, n_left, n_right,
+    xs, h_buf, lhs_a, lhs_b, outs, low_outs, coef, w_ref, stats, vs, v_buf, v_lhs_a, v_lhs_b, v_outs, w2_ref, stats3,
+    x_sem, scan_sem, s_sem, f_sem, o_sem, q_sem, w_sem, v_sem, h_sem, n_sem, w2_sem, *talks,
 ):
     windows, length, channels = x.shape
     slabs = channels // LANES
@@ -306,30 +418,41 @@
     tiles = walk.count
     lhs = (lhs_a, lhs_b)
     n = Exchange.SUMS
-    talk1 = Exchange(talks[:n], talks[2 * n : 2 * n + 6])
-    talk2 = Exchange(talks[n : 2 * n], talks[2 * n + 6 :])
+    talk1 = Exchange(talks[:n], talks[3 * n : 3 * n + 6])
+    talk2 = Exchange(talks[n : 2 * n], talks[3 * n + 6 : 3 * n + 10])
+    talk3 = Exchange(talks[2 * n : 3 * n], talks[3 * n + 10 :])
     left, right = talk1.lands[:2]
 
-    def scan_copy(i, slot):
-        w, _ = walk.where(i)
-        return pltpu.make_async_copy(x.at[w, walk.rows(i, 2)], xs.at[slot, pl.ds(EDGE, span)], x_sem.at[slot])
-
-    scan_copy(0, 0).start()
-    scan_copy(1, 1).start()
+    pieces = 4
+    part = 2 * span // pieces
+
+    def scan_copy(i):
+        slot, w = i % pieces, i // (length // part)
+        at = pl.ds(pl.multiple_of(i % (length // part) * part, 8), part)
+        room = xs.at[slot // 2, pl.ds(pl.multiple_of(EDGE + slot % 2 * part, 8), part)]
+        return pltpu.make_async_copy(x.at[w, at], room, scan_sem.at[slot])
+
+    for i in range(pieces - 1):
+        scan_copy(i).start()
     greet(talk1.seqs, talk1.dps)
     talk1.start_edges((x, cotangent))
     stats[...] = jnp.zeros_like(stats)
 
     def scan(i, _):
-        slot = i % 2
-        scan_copy(i, slot).wait()
+        slot = i % pieces
+        scan_copy(i).wait()
+
+        @pl.when(i + pieces - 1 < windows * length // part)
+        def _():
+            scan_copy(i + pieces - 1).start()
 
         def slab(c, _):
             cols = lanes(c)
             total = jnp.zeros((8, LANES), f32)
             squares = jnp.zeros((8, LANES), f32)
-            for r in range(EDGE, EDGE + span, 128):
-                v = xs[slot, r : r + 128, cols]
+            for r in range(0, part, 128):
+                at = pl.ds(pl.multiple_of(EDGE + slot % 2 * part + r, 8), 128)
+                v = xs[slot // 2, at, cols]
                 total += folded(v)
                 squares += folded(v * v)
             stats[0, :, cols] += total
@@ -337,16 +460,12 @@
             return 0
 
         lax.fori_loop(0, slabs, slab, 0)
-
-        @pl.when(i + 2 < tiles)
-        def _():
-            scan_copy(i + 2, slot).start()
-
         return 0
 
-    lax.fori_loop(0, tiles, scan, 0)
+    lax.fori_loop(0, windows * length // part, scan, 0)
     talk1.start_sums(stats)
     w_copy = pltpu.make_async_copy(w_hbm, w_ref, w_sem)
+    w2_copy = pltpu.make_async_copy(w2_hbm, w2_ref, w2_sem)
 
     def load(i, slot):
         walk.fetch(i, x, left, right, xs.at[slot], x_sem.at[slot], 2)
@@ -364,9 +483,12 @@
             lhs[slot].at[pl.ds(0, 16), pl.ds(channels, channels)], first_out.at[w], f_sem
         )
 
-    def o_copy(i, slot):
+    def o_copies(i, slot):
         w, _ = walk.where(i)
-        return pltpu.make_async_copy(outs.at[slot], pooled.at[w, walk.rows(i)], o_sem.at[slot])
+        return (
+            pltpu.make_async_copy(outs.at[slot], pooled.at[w, walk.rows(i)], o_sem.at[slot]),
+            pltpu.make_async_copy(low_outs.at[slot], pooled_low.at[w, walk.rows(i)], q_sem.at[slot]),
+        )
 
     def activate(i, slot, c):
         scale = coef[c, 0:1]
@@ -419,6 +541,7 @@
         def finish():
             total = (0.25 / ROOT) * held[0]
             outs[slot, :, cols] = total
+            low_outs[slot, :, cols] = total.astype(bf16)
             stats[0, :, cols] += folded(total)
             stats[1, :, cols] += folded(total * total)
 
@@ -475,7 +598,8 @@
 
             @pl.when(i >= 2)
             def _():
-                o_copy(i - 2, slot).wait()
+                for copy in o_copies(i - 2, slot):
+                    copy.wait()
 
             def part(n, _):
                 pieces, finish = matmul(slot, n)
@@ -487,7 +611,8 @@
                 return 0
 
             lax.fori_loop(0, channels // 256, part, 0)
-            o_copy(i, slot).start()
+            for copy in o_copies(i, slot):
+                copy.start()
 
             @pl.when(i + 1 < tiles)
             def _():
@@ -505,209 +630,60 @@
         s_copy(tiles - 1, 1, which).wait()
     if walk.per == 1:
         first_copy(tiles - 1, 1).wait()
-    o_copy(tiles - 2, 0).wait()
-    o_copy(tiles - 1, 1).wait()
+    for copy in o_copies(tiles - 2, 0) + o_copies(tiles - 1, 1):
+        copy.wait()
     talk2.start_edges((pooled,))
     talk2.start_sums(stats)
+    w2_copy.start()
     talk2.finish_edges((pooled,))
     p_left[...] = talk2.lands[0][...]
     p_right[...] = talk2.lands[1][...]
-    talk2.finish_sums(sums2)
-
-
-def conv_one_forward(x, cotangent, gain, shift, weight, entries, number):
+
+    def all_sums():
+        talk2.finish_sums(sums2)
+        return sums2[...]
+
+    conv_two_phase(
+        tile, entries / 2, pooled, talk2.lands[0], talk2.lands[1], all_sums, gain2, shift2, w2_copy, w2_ref, talk3,
+        narrow, h_out, sums3, n_left, n_right, vs, v_buf, v_lhs_a, v_lhs_b, v_outs, stats3, v_sem, h_sem, n_sem,
+    )
+
+
+def conv_forward(x, cotangent, gain, shift, weight, gain2, shift2, weight2, entries, number):
     windows, length, channels = x.shape
     half = length // 2
     tile = min(512, half)
     slabs = channels // LANES
+    width = weight2.shape[2]
     pooled = jax.ShapeDtypeStruct((windows, half, channels), f32)
-    edges = Exchange.edges([cotangent, pooled])
+    narrow = jax.ShapeDtypeStruct((windows, half, width), f32)
+    edges = Exchange.edges([cotangent, pooled, narrow])
     got = pl.pallas_call(
         functools.partial(conv_one_kernel, tile, entries),
         out_shape=[
             pooled,
+            jax.ShapeDtypeStruct(pooled.shape, bf16),
             jax.ShapeDtypeStruct((2, windows, half, channels), bf16),
             jax.ShapeDtypeStruct((windows, 16, channels), bf16),
+            narrow,
+            jax.ShapeDtypeStruct((windows, half, channels), bf16),
             jax.ShapeDtypeStruct((8, channels), f32),
             jax.ShapeDtypeStruct((8, channels), f32),
+            jax.ShapeDtypeStruct((8, width), f32),
         ]
         + edges,
-        in_specs=[ANY, ANY, VM, VM, ANY],
-        out_specs=[ANY] * 3 + [VM] * 6,
+        in_specs=[ANY, ANY, VM, VM, ANY, VM, VM, ANY],
+        out_specs=[ANY] * 6 + [VM] * 9,
         scratch_shapes=[
             pltpu.VMEM((2, 2 * tile + 2 * EDGE, channels), f32),
             pltpu.VMEM((slabs, 2 * tile + 2 * EDGE, LANES), f32),
             pltpu.VMEM((tile, 5 * channels), bf16),
             pltpu.VMEM((tile, 5 * channels), bf16),
             pltpu.VMEM((2, tile, channels), f32),
+            pltpu.VMEM((2, tile, channels), bf16),
             pltpu.VMEM((slabs, 8, LANES), f32),
             pltpu.VMEM((5 * channels, channels), bf16),
             pltpu.VMEM((2, 8, channels), f32),
-            DMA((2,)),
-            DMA((2, 2)),
-            DMA,
-            DMA((2,)),
-            DMA,
-        ]
-        + Exchange.scratch(channels) * 2
-        + Exchange.edge_scratch([x, cotangent])
-        + Exchange.edge_scratch([pooled]),
-        name="conv_one_forward",
-        **joining(params(10 * windows * half * channels * channels, 12 * x.size, x.size), number),
-    )(x, cotangent, gain, shift, weight.reshape(5 * channels, channels))
-    return got[:5], got[5:7], got[7:9]
-
-
-def conv_two_kernel(
-    tile, entries, v, left, right, sums, gain, shift, w_hbm, narrow, h_out, sums3, n_left, n_right,
-    vs, h_buf, lhs_a, lhs_b, outs, w_ref, stats, v_sem, h_sem, o_sem, w_sem, *talks,
-):
-    windows, length, channels = v.shape
-    slabs = channels // LANES
-    walk = Walk(windows, length, tile)
-    tiles = walk.count
-    lhs = (lhs_a, lhs_b)
-    center, inverse = center_inverse(sums[...], entries)
-    scale = inverse * flat_row(gain)
-    offset = flat_row(shift) - center * scale
-    scale, offset = ROOT * scale, ROOT * offset
-    stats[...] = jnp.zeros_like(stats)
-
-    def load(i):
-        walk.fetch(i, v, left, right, vs.at[i % SLOTS], v_sem.at[i % SLOTS])
-
-    def wait_load(i):
-        wait_for(vs.at[i % SLOTS], v_sem.at[i % SLOTS])
-
-    def h_copy(i, slot):
-        w, _ = walk.where(i)
-        return pltpu.make_async_copy(
-            lhs[slot].at[:, pl.ds(channels, channels)], h_out.at[w, walk.rows(i)], h_sem.at[slot]
-        )
-
-    def o_copy(i, slot):
-        w, _ = walk.where(i)
-        return pltpu.make_async_copy(outs.at[slot], narrow.at[w, walk.rows(i)], o_sem.at[slot])
-
-    def activate(i, slot, c):
-        a, b = scale[:, lanes_of(c)], offset[:, lanes_of(c)]
-        src, dst, cols = vs.at[i % SLOTS], lhs[slot], lanes(c)
-
-        def ends():
-            head = gelu_scaled(src[0:EDGE, cols] * a + b)
-            h_buf[c, 0:EDGE] = jnp.where(walk.hide_left(i), 0.0, head)
-            tail = gelu_scaled(src[EDGE + tile : 2 * EDGE + tile, cols] * a + b)
-            h_buf[c, EDGE + tile : 2 * EDGE + tile] = jnp.where(walk.hide_right(i), 0.0, tail)
-
-        def rows(r):
-            def run():
-                q = EDGE + r
-                h_buf[c, q : q + UNIT] = gelu_scaled(src[q : q + UNIT, cols] * a + b)
-
-            return run
-
-        def taps(r):
-            def run():
-                for tap in range(3):
-                    at = EDGE + r + 5 * (tap - 1)
-                    dst[r : r + UNIT, lanes(tap * slabs + c)] = h_buf[c, at : at + UNIT].astype(bf16)
-
-            return run
-
-        units = [ends, rows(0)]
-        for r in range(UNIT, tile, UNIT):
-            units += [rows(r), taps(r - UNIT)]
-        return units + [taps(tile - UNIT)]
-
-    for i in range(min(SLOTS, tiles)):
-        load(i)
-    talk = Exchange(talks[: Exchange.SUMS], talks[Exchange.SUMS :])
-    greet(talk.seqs, talk.dps)
-    wait_load(0)
-    w_copy = pltpu.make_async_copy(w_hbm, w_ref, w_sem)
-    w_copy.start()
-    for c in range(slabs):
-        for unit in activate(0, 0, c):
-            unit()
-    h_copy(0, 0).start()
-    w_copy.wait()
-
-    def pair(j, _):
-        for slot in range(2):
-            i = 2 * j + slot
-            other = 1 - slot
-
-            @pl.when(i + 1 < tiles)
-            def _():
-                wait_load(i + 1)
-
-            @pl.when(jnp.logical_and(i >= 1, i + SLOTS - 1 < tiles))
-            def _():
-                load(i + SLOTS - 1)
-
-            @pl.when(i >= 1)
-            def _():
-                h_copy(i - 1, other).wait()
-
-            @pl.when(i >= 2)
-            def _():
-                o_copy(i - 2, slot).wait()
-
-            held = []
-
-            def piece(k):
-                def run():
-                    at = slice(k * channels, (k + 1) * channels)
-                    part = dot(lhs[slot][:, at], w_ref[at])
-                    held[:] = [held[0] + part] if held else [part]
-
-                return run
-
-            units = []
-            for c in range(slabs):
-                units += activate(i + 1, other, c)
-            interleave([piece(k) for k in range(3)], units)
-            total = (0.5 / ROOT) * held[0]
-            outs[slot] = total
-            stats[0] += folded(total)
-            stats[1] += folded(total * total)
-            o_copy(i, slot).start()
-
-            @pl.when(i + 1 < tiles)
-            def _():
-                h_copy(i + 1, other).start()
-
-        return 0
-
-    lax.fori_loop(0, tiles // 2, pair, 0)
-    h_copy(tiles - 1, 1).wait()
-    o_copy(tiles - 2, 0).wait()
-    o_copy(tiles - 1, 1).wait()
-    talk.start_edges((narrow,))
-    talk.start_sums(stats)
-    talk.finish_edges((narrow,))
-    n_left[...] = talk.lands[0][...]
-    n_right[...] = talk.lands[1][...]
-    talk.finish_sums(sums3)
-
-
-def conv_two_forward(v, left, right, sums, gain, shift, weight, entries, number):
-    windows, length, channels = v.shape
-    tile = min(512, length)
-    slabs = channels // LANES
-    width = weight.shape[2]
-    narrow = jax.ShapeDtypeStruct((windows, length, width), f32)
-    got = pl.pallas_call(
-        functools.partial(conv_two_kernel, tile, entries),
-        out_shape=[
-            narrow,
-            jax.ShapeDtypeStruct((windows, length, channels), bf16),
-            jax.ShapeDtypeStruct((8, width), f32),
-        ]
-        + Exchange.edges([narrow]),
-        in_specs=[ANY, ANY, ANY, VM, VM, VM, ANY],
-        out_specs=[ANY, ANY, VM, VM, VM],
-        scratch_shapes=[
             pltpu.VMEM((SLOTS, tile + 2 * EDGE, channels), f32),
             pltpu.VMEM((slabs, tile + 2 * EDGE, LANES), f32),
             pltpu.VMEM((tile, 3 * channels), bf16),
@@ -715,57 +691,121 @@
             pltpu.VMEM((2, tile, width), f32),
             pltpu.VMEM((3 * channels, width), bf16),
             pltpu.VMEM((2, 8, width), f32),
+            DMA((2,)),
+            DMA((4,)),
+            DMA((2, 2)),
+            DMA,
+            DMA((2,)),
+            DMA((2,)),
+            DMA,
             DMA((SLOTS,)),
             DMA((2,)),
             DMA((2,)),
             DMA,
         ]
+        + Exchange.scratch(channels) * 2
         + Exchange.scratch(width)
+        + Exchange.edge_scratch([x, cotangent])
+        + Exchange.edge_scratch([pooled])
         + Exchange.edge_scratch([narrow]),
-        name="conv_two_forward",
-        **joining(params(6 * v.size * width, 8 * v.size, v.size), number),
-    )(v, left, right, sums, gain, shift, weight.reshape(3 * channels, width))
-    return got[:3], got[3:]
+        name="conv_forward",
+        **joining(params(13 * windows * half * channels * channels, 20 * x.size, 2 * x.size), number),
+    )(
+        x, cotangent, gain, shift, weight.reshape(5 * channels, channels), gain2, shift2,
+        weight2.reshape(3 * channels, width),
+    )
+    return got[:6], got[6:9], got[9:11], got[11:13], got[13:15]
 
 
 def conv_three_kernel(
     entries, narrow, cotangent, pooled, sums, gain, shift, w_ref, outputs, da, stats, w_grad,
-    branch, grad, hidden, total,
+    branch_a, branch_b, grad_a, grad_b, hidden, total, coef,
 ):
-    tile = narrow.shape[1]
+    tile, width = narrow.shape[1:]
+    channels = cotangent.shape[2]
     step = pl.program_id(0)
-    center, inverse = center_inverse(sums[...], entries)
+
+    @pl.when(step == 0)
+    def _():
+        center, inverse = center_inverse(sums[...], entries)
+        scale = inverse * flat_row(gain)
+        offset = flat_row(shift) - center * scale
+        coef[0:1] = ROOT * scale
+        coef[1:2] = ROOT * offset
+        stats[...] = jnp.zeros_like(stats)
+
+    def turn(branch, grad, branch_old, grad_old):
+        held = [[jnp.zeros((8, LANES), f32), jnp.zeros((8, LANES), f32)] for _ in range(width // LANES)]
+
+        def back(n):
+            def run():
+                rows = slice(n * tile // 4, (n + 1) * tile // 4)
+                branch[rows] = cotangent[0, rows].astype(bf16)
+                if n % 2 == 1:
+                    both = slice((n - 1) * tile // 4, (n + 1) * tile // 4)
+                    grad[both] = dot(branch[both], w_ref[...], NT)
+
+            return run
+
+        def rows(r, c):
+            def run():
+                cols = lanes_of(c)
+                q = narrow[0, r : r + UNIT, cols] * coef[0:1, cols] + coef[1:2, cols]
+                square = q * q
+                th = jnp.tanh(q * (BEND + square))
+                up = 1.0 + th
+                hidden[r : r + UNIT, cols] = (q * up).astype(bf16)
+                back = up * (1.0 + (1.0 - th) * (q * (BEND + 3.0 * square))) * grad_old[r : r + UNIT, cols]
+                da[0, r : r + UNIT, cols] = back
+                held[c][0] = held[c][0] + folded(back * q)
+                held[c][1] = held[c][1] + folded(back)
+
+            return run
+
+        def forward(n):
+            def run():
+                at = slice(n * tile // 2, (n + 1) * tile // 2)
+                outputs[0, at] = pooled[0, at].astype(f32) + (0.5 / ROOT) * dot(hidden[at], w_ref[...])
+
+            return run
+
+        def weigh(n):
+            def run():
+                at = slice(n * tile // 2, (n + 1) * tile // 2)
+                got = dot(hidden[at], branch_old[at], TN)
+                total[...] = jnp.where(step <= 1, got, total[...] + got) if n == 0 else total[...] + got
+
+            return run
+
+        units = [rows(r, c) for r in range(0, tile, UNIT) for c in range(width // LANES)]
+        half = len(units) // 2
+        interleave([back(n) for n in range(4)], units[:half])
+        interleave([forward(0), weigh(0)], units[half:])
+        forward(1)()
+        weigh(1)()
+        for c in range(width // LANES):
+            for n in range(2):
+                stats[n, :, lanes_of(c)] += held[c][n]
+
+    @pl.when(step % 2 == 0)
+    def _():
+        turn(branch_a, grad_a, branch_b, grad_b)
+
+    @pl.when(step % 2 == 1)
+    def _():
+        turn(branch_b, grad_b, branch_a, grad_a)
 
     @pl.when(step == 0)
     def _():
         stats[...] = jnp.zeros_like(stats)
-        total[...] = jnp.zeros_like(total)
-
-    branch[...] = cotangent[0].astype(bf16)
-    grad[...] = dot(branch[...], w_ref[...], NT)
-    for c in range(narrow.shape[2] // LANES):
-        cols = lanes(c)
-        at = lanes_of(c)
-        m, inv, g, s = center[:, at], inverse[:, at], gain[at][None], shift[at][None]
-        gains = jnp.zeros((8, LANES), f32)
-        shifts = jnp.zeros((8, LANES), f32)
-        for r in range(0, tile, UNIT):
-            normed = (narrow[0, r : r + UNIT, cols] - m) * inv
-            value, slope = gelu_both(normed * g + s)
-            hidden[r : r + UNIT, cols] = value.astype(bf16)
-            back = slope * grad[r : r + UNIT, cols]
-            da[0, r : r + UNIT, cols] = back
-            gains += folded(back * normed)
-            shifts += folded(back)
-        stats[0, :, cols] += gains
-        stats[1, :, cols] += shifts
-    outputs[0] = pooled[0] + dot(hidden[...], w_ref[...])
-    total[...] += dot(hidden[...], branch[...], TN)
 
     @pl.when(step == pl.num_programs(0) - 1)
     def _():
-        for c in range(total.shape[1] // LANES):
-            w_grad[c] = total[:, lanes_of(c)].astype(bf16)
+        shifts = 0.5 * stats[1]
+        stats[0] = (0.5 / ROOT * stats[0] - shifts * flat_row(shift)) / flat_row(gain)
+        stats[1] = shifts
+        for c in range(channels // LANES):
+            w_grad[c] = ((0.5 / ROOT) * total[:, lanes_of(c)]).astype(bf16)
 
 
 def conv_three_both(narrow, cotangent, pooled, sums, gain, shift, weight, entries):
@@ -773,11 +813,13 @@
     channels = weight.shape[1]
     tile = min(512, length)
     per = length // tile
-    rows = lambda i: (i // per, i % per, 0)
+    tiles = windows * per
+    ahead = lambda i: (jnp.minimum(i, tiles - 1) // per, jnp.minimum(i, tiles - 1) % per, 0)
+    rows = lambda i: (jnp.maximum(i - 1, 0) // per, jnp.maximum(i - 1, 0) % per, 0)
     whole = lambda i: (0, 0)
     return pl.pallas_call(
         functools.partial(conv_three_kernel, entries),
-        grid=(windows * per,),
+        grid=(tiles + 1,),
         out_shape=(
             jax.ShapeDtypeStruct((windows, length, channels), f32),
             jax.ShapeDtypeStruct((windows, length, width), f32),
@@ -786,7 +828,7 @@
         ),
         in_specs=[
             pl.BlockSpec((1, tile, width), rows),
-            pl.BlockSpec((1, tile, channels), rows),
+            pl.BlockSpec((1, tile, channels), ahead),
             pl.BlockSpec((1, tile, channels), rows),
             pl.BlockSpec((8, width), whole),
             pl.BlockSpec((width,), lambda i: (0,)),
@@ -799,12 +841,9 @@
             pl.BlockSpec((2, 8, width), lambda i: (0, 0, 0)),
             pl.BlockSpec((channels // LANES, width, LANES), lambda i: (0, 0, 0)),
         ),
-        scratch_shapes=[
-            pltpu.VMEM((tile, channels), bf16),
-            pltpu.VMEM((tile, width), f32),
-            pltpu.VMEM((tile, width), bf16),
-            pltpu.VMEM((width, channels), f32),
-        ],
+        scratch_shapes=[pltpu.VMEM((tile, channels), bf16)] * 2
+        + [pltpu.VMEM((tile, width), f32)] * 2
+        + [pltpu.VMEM((tile, width), bf16), pltpu.VMEM((width, channels), f32), pltpu.VMEM((8, width), f32)],
         name="conv_three_both",
         **params(6 * narrow.size * channels, 12 * cotangent.size, narrow.size),
     )(narrow, cotangent, pooled, sums, gain, shift, weight)
@@ -970,7 +1009,7 @@
 
         def value(q, size):
             at = i % SLOTS
-            return das[at, q : q + size, cols] * s - (vs[at, q : q + size, cols] - m) * l - f
+            return das[at, q : q + size, cols] * (0.5 * s) - (vs[at, q : q + size, cols] - m) * l - f
 
         def ends():
             low_buf[c, 0:EDGE] = jnp.where(walk.hide_left(i), 0.0, value(0, EDGE))
@@ -1141,6 +1180,10 @@
         def _():
             o_copy(i - 1, other).start()
 
+        @pl.when(i == 0)
+        def _():
+            stats[...] = jnp.zeros_like(stats)
+
     def back_pair(j, _):
         for slot in range(2):
             back_turn(2 * j + slot, slot, False)
@@ -1149,8 +1192,6 @@
                 sharing.step(2 * (2 * j + slot) + 1)
         return 0
 
-    wide[SLOTS - 1, 0, 0:tile] = jnp.zeros((tile, channels), f32)
-    wide[1, 2, 0:tile] = jnp.zeros((tile, channels), f32)
     for i in range(2):
         p_copy(i).start()
     wait_load(0)
@@ -1385,6 +1426,7 @@
     span = 2 * tile
     walk = Walk(windows, length, tile)
     tiles = walk.count
+    tall = Walk(windows, length, min(TALL, length))
     center, inverse = center_inverse(sums1[...], entries)
     scale = inverse * flat_row(gain1)
     offset = flat_row(shift1) - center * scale
@@ -1409,9 +1451,9 @@
         )
 
     def t_copies(g, slot):
-        k = EARLY + g // tiles
-        w, _ = walk.where(g % tiles)
-        rows = walk.rows(g % tiles)
+        k = EARLY + g // tall.count
+        w, _ = tall.where(g % tall.count)
+        rows = tall.rows(g % tall.count)
         at = pl.ds(pl.multiple_of((k // 2) * channels, channels), channels)
         return (
             pltpu.make_async_copy(s.at[k % 2, w, rows], ss.at[slot], t_sem.at[slot, 0]),
@@ -1433,14 +1475,14 @@
         sharing = Reduction.of(data, reduction, 3)
         sharing.step(0)
 
-    late = (5 - EARLY) * tiles
+    late = (5 - EARLY) * tall.count
     triple = slabs // 2
 
     def due(g):
-        whole, part = g // tiles, g % tiles
+        whole, part = g // tall.count, g % tall.count
         first = jnp.where(whole == 0, 1, (EARLY + whole - 1) * triple)
         count = jnp.where(whole == 0, EARLY * triple - 1, triple)
-        return first + count * part // tiles, first + count * (part + 1) // tiles
+        return first + count * part // tall.count, first + count * (part + 1) // tall.count
 
     def weigh(g, _):
         slot = g % (AHEAD + 1)
@@ -1452,19 +1494,19 @@
             for copy in t_copies(g + AHEAD, (g + AHEAD) % (AHEAD + 1)):
                 copy.start()
 
-        @pl.when(g % tiles == 0)
+        @pl.when(g % tall.count == 0)
         def _():
             total[...] = dot(ss[slot], ls[slot], TN)
 
-        @pl.when(g % tiles > 0)
+        @pl.when(g % tall.count > 0)
         def _():
             total[...] += dot(ss[slot], ls[slot], TN)
 
-        @pl.when(g % tiles == tiles - 1)
+        @pl.when(g % tall.count == tall.count - 1)
         def _():
             for c in range(slabs):
                 at = slice((c % 2) * channels, (c % 2 + 1) * channels)
-                data[(EARLY + g // tiles) * triple + c // 2, at] = ((0.5 / ROOT) * total[:, lanes_of(c)]).astype(bf16)
+                data[(EARLY + g // tall.count) * triple + c // 2, at] = ((0.5 / ROOT) * total[:, lanes_of(c)]).astype(bf16)
 
         if joined:
             def take(t, _):
@@ -1575,8 +1617,10 @@
             for copy in o_copies(i - 1, other):
                 copy.start()
 
-    xs[1] = jnp.zeros(xs.shape[1:], f32)
-    g_buf[1] = jnp.zeros(g_buf.shape[1:], f32)
+        @pl.when(i == 0)
+        def _():
+            stats[...] = jnp.zeros_like(stats)
+
 
     def pair(j, _):
         for slot in range(2):
@@ -1629,8 +1673,8 @@
             pltpu.VMEM((slabs, 8, LANES), f32),
             pltpu.VMEM(weight.shape, bf16),
             pltpu.VMEM((channels, channels), f32),
-            pltpu.VMEM((AHEAD + 1, tile, channels), bf16),
-            pltpu.VMEM((AHEAD + 1, tile, channels), bf16),
+            pltpu.VMEM((AHEAD + 1, min(TALL, length), channels), bf16),
+            pltpu.VMEM((AHEAD + 1, min(TALL, length), channels), bf16),
             pltpu.VMEM((chunks, rows, LANES), bf16),
             pltpu.VMEM((2, 8, channels), f32),
             DMA((2,)),
@@ -1743,14 +1787,11 @@
     windows, length, channels = inputs.shape
     entries = float(windows * length * lax.axis_size("dp") * lax.axis_size("seq"))
     half = entries / 2
-    (pooled, s, first, sums1, sums2), c_sides, p_sides = conv_one_forward(
-        inputs, cotangent, gain_one, shift_one, conv_one, entries, 0
-    )
-    (narrow, hidden_two, sums3), n_sides = conv_two_forward(
-        pooled, *p_sides, sums2, gain_two, shift_two, conv_two, half, 1
+    (pooled, pooled_low, s, first, narrow, hidden_two), (sums1, sums2, sums3), c_sides, p_sides, n_sides = conv_forward(
+        inputs, cotangent, gain_one, shift_one, conv_one, gain_two, shift_two, conv_two, entries, 0
     )
     outputs, da3, stats, three_grad = conv_three_both(
-        narrow, cotangent, pooled, sums3, gain_three, shift_three, conv_three, half
+        narrow, cotangent, pooled_low, sums3, gain_three, shift_three, conv_three, half
     )
     low, parts, small, grads3, grads2 = conv_two_back(
         da3, stats, narrow, n_sides, sums3, gain_three, pooled, p_sides, sums2, gain_two, shift_two, hidden_two, conv_two,

time: 318 us -> 311 us (0.978)
  Pallas kernels: 317 us -> 310 us
    pallas_call x3 -> x2, Pallas kernels: 120 us -> 113 us  [the longest x1 90.6 us: conv_forward(): pl.pallas_call(functools.partial(conv_one_kernel, tile, entries), out_sha...]
where the time goes in v5:
time: 311 us
  Pallas kernels  310 us (100%)
    pallas_call x1, Pallas kernels, conv_two_back(): pl.pallas_call(functools.partial(conv_two_back_kernel, tile, entries, joi...  91.5 us
    pallas_call x1, Pallas kernels, conv_forward(): pl.pallas_call(functools.partial(conv_one_kernel, tile, entries), out_sha...  90.6 us
    pallas_call x1, Pallas kernels, conv_one_spread(): pl.pallas_call(functools.partial(conv_one_spread_kernel, tile, entries, j...  78 us
    pallas_call x1, Pallas kernels, last(): pl.pallas_call(functools.partial(last_kernel, entries, taps), grid=(windo...  27.4 us
    pallas_call x1, Pallas kernels, conv_three_both(): pl.pallas_call(functools.partial(conv_three_kernel, entries), grid=(tiles...  22.4 us

profile of v5, /device:TPU:0, one launch (start us, length us, event | category | flops | bytes accessed | tf_op | source)
XLA Modules:
  0.0 310.7 jit_solution(16326275496605587318)
XLA Ops:
  0.6 90.6 %conv_forward.1 = (f32[2,2048,768]{2,1,0:T(8,128)}, bf16[2,2048,768]{2,1,0:T(8,128)(2,1)}, bf16[2,2,2048,768]{3,2,1,0:T(8,128)(2,1)}, bf16[2,16,768]{2,1,0:T(8,1...) custom-call(f32[2,4096,768]{2,1,0:T(8,128)} %x.3, ...), custom_call_target="tpu_custom_call" | custom-call | flops 31406948352 | bytes 125829120 | tf_op jit(solution)/shard_map/conv_forward/pallas_call | solution.py:661
  91.2 22.4 %conv_three_both.1 = (f32[2,2048,768]{2,1,0:T(8,128)}, f32[2,2048,384]{2,1,0:T(8,128)}, f32[2,8,384]{2,1,0:T(8,128)}, bf16[6,384,128]{2,1,0:T(8,128)(2,1)}) custom-call(f32[2,2048,384]{2,1,0:T(8,128)} %get-tuple-element.49.narrow.v, f32[2,2048,768]{2,1,0:T(8,128)} %ct.1, bf16[2,2048,768]{2,1,0:T(8,128)(2,1)} %get-tuple-element.50.pooled, ...), custom_call_target="tpu_custom_call" | custom-call | flops 7247757312 | bytes 37748736 | tf_op jit(solution)/shard_map/conv_three_both/pallas_call | solution.py:820
  113.6 91.5 %conv_two_back.1 = (f32[2,2048,768]{2,1,0:T(8,128)}, bf16[2,2048,2304]{2,1,0:T(8,128)(2,1)}, bf16[3,6,768,128]{3,2,1,0:T(8,128)(2,1)}, bf16[6,1536,128]{2,1,0:T(...) custom-call(f32[2,2048,384]{2,1,0:T(8,128)} %get-tuple-element.53.da, f32[2,8,384]{2,1,0:T(8,128)} %get-tuple-element.54.stats3, ...), custom_call_target="tpu_custom_call" | custom-call | flops 48318382080 | bytes 125829120 | tf_op jit(solution)/shard_map/conv_two_back/pallas_call | solution.py:1365
  205.1 78.0 %conv_one_spread.1 = (bf16[2,4096,768]{2,1,0:T(8,128)(2,1)}, bf16[2,4096,768]{2,1,0:T(8,128)(2,1)}, bf16[15,1536,128]{2,1,0:T(8,128)(2,1)}, f32[8,768]{1,0:T(8,128)}) custom-call(bf16[2,2048,2304]{2,1,0:T(8,128)(2,1)} %get-tuple-element.67.low, f32[2,4096,768]{2,1,0:T(8,128)} %x.3, f32[8,768]{1,0:T(8,128)} %get-tuple-element.68.sums1.sums, f32[768]{0:T(1024)} %gain.5, ...), custom_call_target="tpu_custom_call" | custom-call | flops 24159191040 | bytes 75497472 | tf_op jit(solution)/shard_map/conv_one_spread/pallas_call | solution.py:1657
  283.1 27.4 %last.1 = (f32[2,4096,768]{2,1,0:T(8,128)}, f32[5,768,768]{2,1,0:T(8,128)}, f32[3,768,384]{2,1,0:T(8,128)}, f32[384,768]{1,0:T(8,128)}, f32[768]{0:T(1024)}, /*i...) custom-call(bf16[2,4096,768]{2,1,0:T(8,128)(2,1)} %get-tuple-element.70.da, ...), custom_call_target="tpu_custom_call" | custom-call | bytes 68026368 | tf_op jit(solution)/shard_map/last/pallas_call | solution.py:1749

commit v6 on v5

--- a/solution.py
+++ b/solution.py
@@ -17,7 +17,7 @@
 MESH = pl.DeviceIdType.MESH
 LINEAR = 0.7978845608028654
 CUBIC = 0.7978845608028654 * 0.044715
-VMEM_LIMIT = 60 << 20
+VMEM_LIMIT = 62 << 20
 EARLY = 3
 AHEAD = 2
 TALL = 1024
@@ -153,7 +153,10 @@
 
     lax.fori_loop(1, seqs, near, 0)
     lax.fori_loop(1, dps, far, 0)
-    pl.semaphore_wait(barrier, seqs - 1 + dps - 1)
+
+
+def meet(seqs, dps):
+    pl.semaphore_wait(pltpu.get_barrier_semaphore(), seqs - 1 + dps - 1)
 
 
 class Exchange:
@@ -435,7 +438,6 @@
     for i in range(pieces - 1):
         scan_copy(i).start()
     greet(talk1.seqs, talk1.dps)
-    talk1.start_edges((x, cotangent))
     stats[...] = jnp.zeros_like(stats)
 
     def scan(i, _):
@@ -463,6 +465,8 @@
         return 0
 
     lax.fori_loop(0, windows * length // part, scan, 0)
+    meet(talk1.seqs, talk1.dps)
+    talk1.start_edges((x, cotangent))
     talk1.start_sums(stats)
     w_copy = pltpu.make_async_copy(w_hbm, w_ref, w_sem)
     w2_copy = pltpu.make_async_copy(w2_hbm, w2_ref, w2_sem)
@@ -852,10 +856,10 @@
 class Reduction:
     STAGES = 8
 
-    def __init__(self, data, done, lands, send, recv, lag):
+    def __init__(self, data, done, lands, send, recv, leave, lag, out):
         self.data, self.done, self.lands, self.send, self.recv = data, done, lands, send, recv
         self.chunks, self.rows = data.shape[0], data.shape[1]
-        self.lag = lag
+        self.lag, self.leave, self.out = lag, leave, out
         self.steps = self.chunks + lag * self.STAGES
         self.planes = lax.axis_size("dp") // 4
         seq, dp = lax.axis_index("seq"), lax.axis_index("dp")
@@ -940,6 +944,18 @@
                     self.arrive(c, stage - 1)
                 if stage < self.STAGES:
                     self.launch(c, stage)
+                else:
+                    self.out_copy(c).start()
+
+    def out_copy(self, c):
+        return pltpu.make_async_copy(self.done.at[c], self.out.at[c], self.leave.at[c])
+
+    def drain(self):
+        def one(c, _):
+            self.out_copy(c).wait()
+            return 0
+
+        lax.fori_loop(0, self.chunks, one, 0)
 
     @staticmethod
     def fits(rows):
@@ -952,11 +968,15 @@
         copies = 2 * (planes - 1) + 6
         shapes = [(chunks, rows, LANES)] + [(chunks, rows >> (n + 1), LANES) for n in range(3)]
         shapes += [(chunks, planes - 1, rows // 8 // planes, LANES)]
-        return [pltpu.VMEM(shape, bf16) for shape in shapes] + [DMA((chunks, copies)), DMA((chunks, copies))]
+        return [pltpu.VMEM(shape, bf16) for shape in shapes] + [
+            DMA((chunks, copies)),
+            DMA((chunks, copies)),
+            DMA((chunks,)),
+        ]
 
     @staticmethod
-    def of(data, refs, lag):
-        return Reduction(data, refs[0], refs[1:5], refs[5], refs[6], lag)
+    def of(data, refs, lag, out):
+        return Reduction(data, refs[0], refs[1:5], refs[5], refs[6], refs[7], lag, out)
 
 
 def conv_two_back_kernel(
@@ -1058,6 +1078,7 @@
     n = Exchange.SUMS
     talk3 = Exchange(refs[:n], refs[2 * n : 2 * n + 4])
     talk2 = Exchange(refs[n : 2 * n], refs[2 * n + 4 : 2 * n + 8])
+    greet(talk3.seqs, talk3.dps)
     w_copy = pltpu.make_async_copy(w_hbm, w_ref, w_sem)
     w_copy.start()
     f_copy = pltpu.make_async_copy(first, firsts, f_sem)
@@ -1072,7 +1093,7 @@
         three_copy(c).start()
     for i in range(min(SLOTS, tiles)):
         h_copy(i).start()
-    greet(talk3.seqs, talk3.dps)
+    meet(talk3.seqs, talk3.dps)
     talk3.start_edges((da,))
     talk3.start_sums(stats3)
     w_copy.wait()
@@ -1133,7 +1154,7 @@
     for c in range(slabs):
         three_copy(c).wait()
     if joined:
-        sharing = Reduction.of(data, refs[2 * n + 8 :], 4)
+        sharing = Reduction.of(data, refs[2 * n + 8 :], 4, small)
 
     def back_turn(i, slot, last):
         other = 1 - slot
@@ -1332,21 +1353,24 @@
 
     lax.fori_loop(0, tiles // 2, wide_pair, 0)
     l_copy(tiles - 1, 1).wait()
+    g_copies = [pltpu.make_async_copy(packed.at[k], w_grad.at[k], g_sem.at[k]) for k in range(EARLY)]
     for k in range(EARLY):
         for c in range(slabs):
             packed[k, c] = ((0.5 / ROOT) * taps[k, :, lanes_of(c)]).astype(bf16)
-    g_copy = pltpu.make_async_copy(packed, w_grad, g_sem)
-    g_copy.start()
+        g_copies[k].start()
     if joined:
         def more(t, _):
             sharing.step(t)
             return 0
 
         lax.fori_loop(2 * tiles + tiles * (channels // 256), sharing.steps, more, 0)
-    d_copy = pltpu.make_async_copy(sharing.done if joined else data, small, d_sem)
-    d_copy.start()
-    d_copy.wait()
-    g_copy.wait()
+        sharing.drain()
+    else:
+        d_copy = pltpu.make_async_copy(data, small, d_sem)
+        d_copy.start()
+        d_copy.wait()
+    for copy in g_copies:
+        copy.wait()
 
 
 def conv_two_back(
@@ -1398,7 +1422,7 @@
         ]
         + [DMA((SLOTS,))] * 4
         + [DMA((2,))]
-        + [DMA, DMA((SLOTS,)), DMA((2,)), DMA, DMA((2,)), DMA, DMA, DMA((slabs,))]
+        + [DMA, DMA((SLOTS,)), DMA((2,)), DMA, DMA((2,)), DMA((EARLY,)), DMA, DMA((slabs,))]
         + Exchange.scratch(width)
         + Exchange.scratch(channels)
         + Exchange.edge_scratch([da])
@@ -1467,21 +1491,19 @@
             copy.start()
     talk, reduction = Exchange(refs[: Exchange.SUMS]), refs[Exchange.SUMS :]
     greet(talk.seqs, talk.dps)
-    d_copy.wait()
     l_copy(0, 0).start()
     w_copy = pltpu.make_async_copy(w_hbm, w_ref, w_sem)
     w_copy.start()
     if joined:
-        sharing = Reduction.of(data, reduction, 3)
-        sharing.step(0)
+        sharing = Reduction.of(data, reduction, 3, w_grad)
 
     late = (5 - EARLY) * tall.count
     triple = slabs // 2
 
     def due(g):
         whole, part = g // tall.count, g % tall.count
-        first = jnp.where(whole == 0, 1, (EARLY + whole - 1) * triple)
-        count = jnp.where(whole == 0, EARLY * triple - 1, triple)
+        first = jnp.where(whole == 0, 0, (EARLY + whole - 1) * triple)
+        count = jnp.where(whole == 0, EARLY * triple, triple)
         return first + count * part // tall.count, first + count * (part + 1) // tall.count
 
     def weigh(g, _):
@@ -1507,6 +1529,11 @@
             for c in range(slabs):
                 at = slice((c % 2) * channels, (c % 2 + 1) * channels)
                 data[(EARLY + g // tall.count) * triple + c // 2, at] = ((0.5 / ROOT) * total[:, lanes_of(c)]).astype(bf16)
+
+        @pl.when(g == 0)
+        def _():
+            d_copy.wait()
+            meet(talk.seqs, talk.dps)
 
         if joined:
             def take(t, _):
@@ -1639,10 +1666,13 @@
             return 0
 
         lax.fori_loop(4 * triple + tiles * (channels // 256), sharing.steps, more, 0)
-    d_copy = pltpu.make_async_copy(sharing.done if joined else data, w_grad, d_sem)
-    d_copy.start()
     talk.finish_sums(grads1)
-    d_copy.wait()
+    if joined:
+        sharing.drain()
+    else:
+        d_copy = pltpu.make_async_copy(data, w_grad, d_sem)
+        d_copy.start()
+        d_copy.wait()
 
 
 def conv_one_spread(low, x, sums1, gain1, shift1, weight, s, parts, entries, number):

time: 311 us -> 309 us (level)
  no operation moved by 1% of the time
where the time goes in v6:
time: 309 us
  Pallas kernels  308 us (100%)
    pallas_call x1, Pallas kernels, conv_forward(): pl.pallas_call(functools.partial(conv_one_kernel, tile, entries), out_sha...  90.2 us
    pallas_call x1, Pallas kernels, conv_two_back(): pl.pallas_call(functools.partial(conv_two_back_kernel, tile, entries, joi...  90.2 us
    pallas_call x1, Pallas kernels, conv_one_spread(): pl.pallas_call(functools.partial(conv_one_spread_kernel, tile, entries, j...  77.6 us
    pallas_call x1, Pallas kernels, last(): pl.pallas_call(functools.partial(last_kernel, entries, taps), grid=(windo...  27.4 us
    pallas_call x1, Pallas kernels, conv_three_both(): pl.pallas_call(functools.partial(conv_three_kernel, entries), grid=(tiles...  22.4 us

profile of v6, /device:TPU:0, one launch (start us, length us, event | category | flops | bytes accessed | tf_op | source)
XLA Modules:
  0.0 308.6 jit_solution(16899841529839209091)
XLA Ops:
  0.6 90.2 %conv_forward.1 = (f32[2,2048,768]{2,1,0:T(8,128)}, bf16[2,2048,768]{2,1,0:T(8,128)(2,1)}, bf16[2,2,2048,768]{3,2,1,0:T(8,128)(2,1)}, bf16[2,16,768]{2,1,0:T(8,1...) custom-call(f32[2,4096,768]{2,1,0:T(8,128)} %x.3, ...), custom_call_target="tpu_custom_call" | custom-call | flops 31406948352 | bytes 125829120 | tf_op jit(solution)/shard_map/conv_forward/pallas_call | solution.py:665
  90.8 22.4 %conv_three_both.1 = (f32[2,2048,768]{2,1,0:T(8,128)}, f32[2,2048,384]{2,1,0:T(8,128)}, f32[2,8,384]{2,1,0:T(8,128)}, bf16[6,384,128]{2,1,0:T(8,128)(2,1)}) custom-call(f32[2,2048,384]{2,1,0:T(8,128)} %get-tuple-element.49.narrow.v, f32[2,2048,768]{2,1,0:T(8,128)} %ct.1, bf16[2,2048,768]{2,1,0:T(8,128)(2,1)} %get-tuple-element.50.pooled, ...), custom_call_target="tpu_custom_call" | custom-call | flops 7247757312 | bytes 37748736 | tf_op jit(solution)/shard_map/conv_three_both/pallas_call | solution.py:824
  113.2 90.2 %conv_two_back.1 = (f32[2,2048,768]{2,1,0:T(8,128)}, bf16[2,2048,2304]{2,1,0:T(8,128)(2,1)}, bf16[3,6,768,128]{3,2,1,0:T(8,128)(2,1)}, bf16[6,1536,128]{2,1,0:T(...) custom-call(f32[2,2048,384]{2,1,0:T(8,128)} %get-tuple-element.53.da, f32[2,8,384]{2,1,0:T(8,128)} %get-tuple-element.54.stats3, ...), custom_call_target="tpu_custom_call" | custom-call | flops 48318382080 | bytes 125829120 | tf_op jit(solution)/shard_map/conv_two_back/pallas_call | solution.py:1389
  203.3 77.6 %conv_one_spread.1 = (bf16[2,4096,768]{2,1,0:T(8,128)(2,1)}, bf16[2,4096,768]{2,1,0:T(8,128)(2,1)}, bf16[15,1536,128]{2,1,0:T(8,128)(2,1)}, f32[8,768]{1,0:T(8,128)}) custom-call(bf16[2,2048,2304]{2,1,0:T(8,128)(2,1)} %get-tuple-element.67.low, f32[2,4096,768]{2,1,0:T(8,128)} %x.3, f32[8,768]{1,0:T(8,128)} %get-tuple-element.68.sums1.sums, f32[768]{0:T(1024)} %gain.5, ...), custom_call_target="tpu_custom_call" | custom-call | flops 24159191040 | bytes 75497472 | tf_op jit(solution)/shard_map/conv_one_spread/pallas_call | solution.py:1687
  281.0 27.4 %last.1 = (f32[2,4096,768]{2,1,0:T(8,128)}, f32[5,768,768]{2,1,0:T(8,128)}, f32[3,768,384]{2,1,0:T(8,128)}, f32[384,768]{1,0:T(8,128)}, f32[768]{0:T(1024)}, /*i...) custom-call(bf16[2,4096,768]{2,1,0:T(8,128)(2,1)} %get-tuple-element.70.da, ...), custom_call_target="tpu_custom_call" | custom-call | bytes 68026368 | tf_op jit(solution)/shard_map/last/pallas_call | solution.py:1779
